TPU v7x, 32 devices: a whole 2x2x4 slice. The times are simulated.
32 devices in a mesh: seq: 4 (over x, core), dp: 8 (over z, y).
Axes of the slice: x: 2, y: 2, z: 4, core: 2. Of those that a mesh axis runs over, the one named last changes fastest.
Arguments:
- long_tokens: bfloat16 [16, 512, 1024], P('dp', 'seq'), may hold values from -6 to 6
- short_tokens: bfloat16 [64, 128, 1024], P(('seq', 'dp')), may hold values from -6 to 6
- long_grad_out: bfloat16 [16, 512, 1024], P('dp', 'seq'), may hold values from -6 to 6
- short_grad_out: bfloat16 [64, 128, 1024], P(('seq', 'dp')), may hold values from -6 to 6
- query_weight: bfloat16 [1024, 1024], P(('seq', 'dp')), may hold values from -0.25 to 0.25
- key_weight: bfloat16 [1024, 1024], P(('seq', 'dp')), may hold values from -0.25 to 0.25
- value_weight: bfloat16 [1024, 1024], P(('seq', 'dp')), may hold values from -0.1875 to 0.1875
- output_weight: bfloat16 [1024, 1024], P(('seq', 'dp')), may hold values from -1 to 1
- attn_gain: bfloat16 [1024], P(('seq', 'dp')), may hold values from 0.25 to 1.75
- ffn_gain: bfloat16 [1024], P(('seq', 'dp')), may hold values from 0.25 to 1.75
- rel_table: bfloat16 [512], P(('seq', 'dp')), may hold values from -4 to 4
- router_weight: bfloat16 [1024, 8], P(('seq', 'dp')), may hold values from -0.375 to 0.375
- gate_weight: bfloat16 [8, 1024, 2816], P('dp', 'seq'), may hold values from -0.1875 to 0.1875
- up_weight: bfloat16 [8, 1024, 2816], P('dp', 'seq'), may hold values from -0.1875 to 0.1875
- down_weight: bfloat16 [8, 1024, 2816], P('dp', 'seq'), may hold values from -0.21875 to 0.21875
- long_positions: int32 [16, 512], P('dp'), may hold values from 0 to 1022, as said below
- short_positions: int32 [64, 128], P(('seq', 'dp')), may hold values from 0 to 254, as said below
- long_lengths: int32 [16], P('dp'), may hold values from 64 to 512, as said below
- short_lengths: int32 [64], P(('seq', 'dp')), may hold values from 16 to 128, as said below
- long_routes: int32 [16, 512, 2], P('dp', 'seq'), may hold values from 0 to 7, all different within a row
- short_routes: int32 [64, 128, 2], P(('seq', 'dp')), may hold values from 0 to 7, all different within a row
Outputs:
- long_out: bfloat16 [16, 512, 1024], P('dp', 'seq')
- short_out: bfloat16 [64, 128, 1024], P(('seq', 'dp'))
- long_grad_in: float32 [16, 512, 1024], P('dp', 'seq')
- short_grad_in: float32 [64, 128, 1024], P(('seq', 'dp'))
- query_grad: float32 [1024, 1024], P(('seq', 'dp'))
- key_grad: float32 [1024, 1024], P(('seq', 'dp'))
- value_grad: float32 [1024, 1024], P(('seq', 'dp'))
- output_grad: float32 [1024, 1024], P(('seq', 'dp'))
- attn_gain_grad: float32 [1024], P(('seq', 'dp'))
- ffn_gain_grad: float32 [1024], P(('seq', 'dp'))
- table_grad: float32 [512], P(('seq', 'dp'))
- router_grad: float32 [1024, 8], P(('seq', 'dp'))
- gate_grad: float32 [8, 1024, 2816], P('dp', 'seq')
- up_grad: float32 [8, 1024, 2816], P('dp', 'seq')
- down_grad: float32 [8, 1024, 2816], P('dp', 'seq')
Inputs may be any that keep to these rules, and one draw needn't show every extreme that they name: `long_positions`: in each item the positions start at 0 and rise by 1 or 2 from one token to the next. `short_positions`: in each item the positions start at 0 and rise by 1 or 2 from one token to the next. `long_lengths`: of the 2 long items of each index of dp, one has length 512. `short_lengths`: of the 16 short items of each index of seq, one has length 128.
All inputs are finite; a program needn't handle non-finite values.
Results may differ from a plain program's by a relative error of at most 0.017.
The roundings to bfloat16 on the way count: a program that leaves them out, or rounds other values in their place, can miss the bound.
Values may be sent and summed in bfloat16 or wider, within the bound.
A program may use at most 256 MiB of HBM per device.

v0:
```python
import jax
import jax.numpy as jnp
from jax import lax
from jax.sharding import PartitionSpec as P

HEADS = 16
HEAD = 64
BUCKETS = 32


far_edges = (12, 16, 23, 32, 46, 64, 91)
epsilon = 1e-06
masked = -1e30


def bucket_of(query_pos, key_pos):
    offset = key_pos[..., None, :] - query_pos[..., :, None]
    distance = jnp.abs(offset)
    beyond = jnp.zeros_like(distance)
    for border in far_edges:
        beyond = beyond + (distance >= border).astype(jnp.int32)
    inner = jnp.where(distance < 8, distance, 8 + beyond)
    return inner + jnp.where(offset > 0, BUCKETS // 2, 0)


def rms_norm(hidden, gain):
    scale = lax.rsqrt(jnp.mean(hidden * hidden, axis=-1, keepdims=True) + epsilon)
    return hidden * scale * gain


def gelu_mul(gate_pre, up_pre):
    return jax.nn.gelu(gate_pre, approximate=True) * up_pre


def gate_values(logits, choose):
    probs = jax.nn.softmax(logits, axis=-1)
    chosen = jnp.sum(choose * probs[:, None, :], axis=-1)
    return chosen / jnp.sum(chosen, axis=-1, keepdims=True)


def score_block(queries, key_rows, query_pos, key_pos, key_ok, bias_table):
    batch_size, rows, model_width = queries.shape
    columns = key_rows.shape[1]
    scores = jnp.einsum(
        "bqhd,bkhd->bhqk",
        queries.reshape(batch_size, rows, HEADS, HEAD),
        key_rows.reshape(batch_size, columns, HEADS, HEAD),
        preferred_element_type=jnp.float32,
    )
    onehot = (
        bucket_of(query_pos, key_pos)[..., None] == jnp.arange(BUCKETS, dtype=jnp.int32)
    ).astype(jnp.bfloat16)
    rel_bias = jnp.einsum("bqkn,hn->bhqk", onehot, bias_table, preferred_element_type=jnp.float32)
    return (jnp.where(key_ok[:, None, None, :], scores + rel_bias, masked), onehot)


def attention_forward(queries, key_rows, value_rows, query_pos, key_pos, key_ok, bias_table):
    scores, onehot = score_block(queries, key_rows, query_pos, key_pos, key_ok, bias_table)
    batch_size, rows, model_width = queries.shape
    columns = key_rows.shape[1]
    row_peak = jnp.max(scores, axis=-1, keepdims=True)
    lifted = jnp.exp(scores - row_peak)
    row_total = jnp.sum(lifted, axis=-1, keepdims=True)
    probs = lifted / row_total
    mixed = jnp.einsum(
        "bhqk,bkhd->bqhd",
        probs.astype(jnp.bfloat16),
        value_rows.reshape(batch_size, columns, HEADS, HEAD),
        preferred_element_type=jnp.float32,
    )
    return (
        mixed.astype(jnp.bfloat16).reshape(batch_size, rows, model_width),
        (row_peak + jnp.log(row_total))[..., 0],
    )


def attention_backward(
    queries, key_rows, value_rows, mixed_grad, log_total, query_pos, key_pos, key_ok, bias_table
):
    scores, onehot = score_block(queries, key_rows, query_pos, key_pos, key_ok, bias_table)
    batch_size, rows, model_width = queries.shape
    columns = key_rows.shape[1]
    probs = jnp.exp(scores - log_total[..., None])
    grad_four = mixed_grad.reshape(batch_size, rows, HEADS, HEAD)
    value_four = value_rows.reshape(batch_size, columns, HEADS, HEAD)
    query_four = queries.reshape(batch_size, rows, HEADS, HEAD)
    key_four = key_rows.reshape(batch_size, columns, HEADS, HEAD)
    prob_grad = jnp.einsum(
        "bqhd,bkhd->bhqk", grad_four, value_four, preferred_element_type=jnp.float32
    )
    score_grad = (probs * (prob_grad - jnp.sum(probs * prob_grad, axis=-1, keepdims=True))).astype(
        jnp.bfloat16
    )
    query_part = jnp.einsum(
        "bhqk,bkhd->bqhd", score_grad, key_four, preferred_element_type=jnp.float32
    ).reshape(batch_size, rows, model_width)
    key_part = jnp.einsum(
        "bhqk,bqhd->bkhd", score_grad, query_four, preferred_element_type=jnp.float32
    ).reshape(batch_size, columns, model_width)
    value_part = jnp.einsum(
        "bhqk,bqhd->bkhd", probs.astype(jnp.bfloat16), grad_four, preferred_element_type=jnp.float32
    ).reshape(batch_size, columns, model_width)
    table_part = jnp.einsum("bhqk,bqkn->hn", score_grad, onehot, preferred_element_type=jnp.float32)
    return (query_part, key_part, value_part, table_part)


def on_device(
    long_tokens,
    short_tokens,
    long_grad_out,
    short_grad_out,
    query_weight,
    key_weight,
    value_weight,
    output_weight,
    attn_gain,
    ffn_gain,
    rel_table,
    router_weight,
    gate_weight,
    up_weight,
    down_weight,
    long_positions,
    short_positions,
    long_lengths,
    short_lengths,
    long_routes,
    short_routes,
):
    long_items, quarter, model_width = long_tokens.shape
    short_items, short_len = (short_tokens.shape[0], short_tokens.shape[1])
    long_rows = long_items * quarter
    tokens = long_rows + short_items * short_len
    local_experts = gate_weight.shape[0]
    dp_size = lax.axis_size("dp")
    experts = local_experts * dp_size
    capacity = (5 * tokens + 2 * experts - 1) // (2 * experts)
    seq_index = lax.axis_index("seq")
    attn_set = (
        lax.all_gather(query_weight, ("seq", "dp"), axis=0, tiled=True),
        lax.all_gather(key_weight, ("seq", "dp"), axis=0, tiled=True),
        lax.all_gather(value_weight, ("seq", "dp"), axis=0, tiled=True),
        lax.all_gather(output_weight, ("seq", "dp"), axis=0, tiled=True),
        lax.all_gather(attn_gain, ("seq", "dp"), axis=0, tiled=True),
        lax.all_gather(ffn_gain, ("seq", "dp"), axis=0, tiled=True),
        lax.all_gather(rel_table, ("seq", "dp"), axis=0, tiled=True),
        lax.all_gather(router_weight, ("seq", "dp"), axis=0, tiled=True),
    )
    expert_set = (
        lax.all_gather(gate_weight, "seq", axis=1, tiled=True),
        lax.all_gather(up_weight, "seq", axis=1, tiled=True),
        lax.all_gather(down_weight, "seq", axis=1, tiled=True),
    )
    resid_in = jnp.concatenate(
        [long_tokens.reshape(long_rows, model_width), short_tokens.reshape(-1, model_width)], 0
    ).astype(jnp.float32)
    gain_first = attn_set[4].astype(jnp.float32)
    normed = rms_norm(resid_in, gain_first).astype(jnp.bfloat16)
    projected = [
        jnp.dot(normed, matrix, preferred_element_type=jnp.float32).astype(jnp.bfloat16)
        for matrix in attn_set[:3]
    ]
    long_q, long_k, long_v = [
        block[:long_rows].reshape(long_items, quarter, model_width) for block in projected
    ]
    short_q, short_k, short_v = [
        block[long_rows:].reshape(short_items, short_len, model_width) for block in projected
    ]
    bias_table = attn_set[6].reshape(HEADS, BUCKETS)
    long_keys, long_values = (
        lax.all_gather(long_k, "seq", axis=1, tiled=True),
        lax.all_gather(long_v, "seq", axis=1, tiled=True),
    )
    key_span = long_keys.shape[1]
    query_pos = lax.dynamic_slice_in_dim(long_positions, seq_index * quarter, quarter, 1)
    long_ok = jnp.arange(key_span, dtype=jnp.int32)[None, :] < long_lengths[:, None]
    short_ok = jnp.arange(short_len, dtype=jnp.int32)[None, :] < short_lengths[:, None]
    long_mix, long_lse = attention_forward(
        long_q, long_keys, long_values, query_pos, long_positions, long_ok, bias_table
    )
    short_mix, short_lse = attention_forward(
        short_q, short_k, short_v, short_positions, short_positions, short_ok, bias_table
    )
    mixed_all = jnp.concatenate(
        [long_mix.reshape(long_rows, model_width), short_mix.reshape(-1, model_width)], 0
    )
    resid_mid = resid_in + jnp.dot(mixed_all, attn_set[3], preferred_element_type=jnp.float32)
    gain_second = attn_set[5].astype(jnp.float32)
    normed_two = rms_norm(resid_mid, gain_second).astype(jnp.bfloat16)
    logits = jnp.dot(normed_two, attn_set[7], preferred_element_type=jnp.float32)
    routes = jnp.concatenate([long_routes.reshape(-1, 2), short_routes.reshape(-1, 2)], 0)
    choose = (routes[..., None] == jnp.arange(experts, dtype=jnp.int32)).astype(jnp.float32)
    gate_share, gate_pull = jax.vjp(lambda logit_in: gate_values(logit_in, choose), logits)
    flat_routes = routes.reshape(-1)
    member = (flat_routes[:, None] == jnp.arange(experts, dtype=jnp.int32)).astype(jnp.int32)
    queue_pos = jnp.sum(jnp.cumsum(member, axis=0) * member, axis=1) - 1
    route_kept = queue_pos < capacity
    slot_index = jnp.where(route_kept, flat_routes * capacity + queue_pos, experts * capacity)
    slot_pair = (
        jnp.zeros(experts * capacity + 1, jnp.int32)
        .at[slot_index]
        .set(jnp.arange(2 * tokens, dtype=jnp.int32))[:-1]
    )
    slot_used = jnp.zeros(experts * capacity + 1, jnp.bool_).at[slot_index].set(True)[:-1]
    pair_slot = jnp.where(route_kept, slot_index, 0)
    outgoing = jnp.where(
        slot_used[:, None], jnp.take(normed_two, slot_pair // 2, axis=0), 0
    ).reshape(experts, capacity, model_width)
    gate_full, up_full, down_full = expert_set
    arrived = lax.all_to_all(outgoing, "dp", split_axis=0, concat_axis=0, tiled=True)
    slot_count = arrived.shape[1]
    inputs = arrived.reshape(dp_size, local_experts, slot_count, model_width)
    gate_pre = jnp.einsum("slcd,ldf->slcf", inputs, gate_full, preferred_element_type=jnp.float32)
    up_pre = jnp.einsum("slcd,ldf->slcf", inputs, up_full, preferred_element_type=jnp.float32)
    hidden = gelu_mul(gate_pre, up_pre).astype(jnp.bfloat16)
    result = jnp.einsum(
        "slcf,ldf->slcd", hidden, down_full, preferred_element_type=jnp.float32
    ).astype(jnp.bfloat16)
    returned = lax.all_to_all(
        result.reshape(experts, slot_count, model_width),
        "dp",
        split_axis=0,
        concat_axis=0,
        tiled=True,
    )
    ffn_width = hidden.shape[-1]
    back_rows, expert_in, gate_pre, up_pre, hidden = (
        returned,
        arrived,
        gate_pre.reshape(experts, slot_count, ffn_width),
        up_pre.reshape(experts, slot_count, ffn_width),
        hidden.reshape(experts, slot_count, ffn_width),
    )
    pair_out = (
        jnp.where(
            route_kept[:, None],
            jnp.take(back_rows.reshape(experts * capacity, model_width), pair_slot, axis=0),
            0,
        )
        .reshape(tokens, 2, model_width)
        .astype(jnp.float32)
    )
    kept_two = route_kept.reshape(tokens, 2).astype(jnp.float32)
    weighting = gate_share * kept_two
    final = resid_mid + weighting[:, 0:1] * pair_out[:, 0] + weighting[:, 1:2] * pair_out[:, 1]
    final_low = final.astype(jnp.bfloat16)
    long_out = final_low[:long_rows].reshape(long_items, quarter, model_width)
    short_out = final_low[long_rows:].reshape(short_items, short_len, model_width)
    grad_out = jnp.concatenate(
        [long_grad_out.reshape(long_rows, model_width), short_grad_out.reshape(-1, model_width)], 0
    ).astype(jnp.float32)
    pair_grad = (
        (weighting[:, :, None] * grad_out[:, None, :])
        .astype(jnp.bfloat16)
        .reshape(2 * tokens, model_width)
    )
    share_grad = kept_two * jnp.sum(grad_out[:, None, :] * pair_out, axis=-1)
    logit_grad = gate_pull(share_grad)[0].astype(jnp.bfloat16)
    out_slots = jnp.where(slot_used[:, None], jnp.take(pair_grad, slot_pair, axis=0), 0).reshape(
        experts, capacity, model_width
    )
    attn_back = (
        lax.all_gather(query_weight, ("seq", "dp"), axis=0, tiled=True),
        lax.all_gather(key_weight, ("seq", "dp"), axis=0, tiled=True),
        lax.all_gather(value_weight, ("seq", "dp"), axis=0, tiled=True),
        lax.all_gather(output_weight, ("seq", "dp"), axis=0, tiled=True),
        lax.all_gather(attn_gain, ("seq", "dp"), axis=0, tiled=True),
        lax.all_gather(ffn_gain, ("seq", "dp"), axis=0, tiled=True),
        lax.all_gather(rel_table, ("seq", "dp"), axis=0, tiled=True),
        lax.all_gather(router_weight, ("seq", "dp"), axis=0, tiled=True),
    )
    expert_back = (
        lax.all_gather(gate_weight, "seq", axis=1, tiled=True),
        lax.all_gather(up_weight, "seq", axis=1, tiled=True),
        lax.all_gather(down_weight, "seq", axis=1, tiled=True),
    )
    gate_back, up_back, down_back = expert_back
    arrived_grad = lax.all_to_all(out_slots, "dp", split_axis=0, concat_axis=0, tiled=True)
    shape_four = (dp_size, local_experts, capacity, -1)
    grad_four = arrived_grad.reshape(dp_size, local_experts, capacity, model_width)
    hidden_grad = jnp.einsum(
        "slcd,ldf->slcf", grad_four, down_back, preferred_element_type=jnp.float32
    )
    unused_geglu, geglu_pull = jax.vjp(
        gelu_mul, gate_pre.reshape(shape_four), up_pre.reshape(shape_four)
    )
    gate_pre_grad, up_pre_grad = geglu_pull(hidden_grad)
    gate_pre_grad = gate_pre_grad.astype(jnp.bfloat16)
    up_pre_grad = up_pre_grad.astype(jnp.bfloat16)
    input_grad = (
        jnp.einsum("slcf,ldf->slcd", gate_pre_grad, gate_back, preferred_element_type=jnp.float32)
        + jnp.einsum("slcf,ldf->slcd", up_pre_grad, up_back, preferred_element_type=jnp.float32)
    ).astype(jnp.bfloat16)
    returned_grad = lax.all_to_all(
        input_grad.reshape(experts, capacity, model_width),
        "dp",
        split_axis=0,
        concat_axis=0,
        tiled=True,
    )
    inputs_four = expert_in.reshape(dp_size, local_experts, capacity, model_width)
    hidden_four = hidden.reshape(shape_four)
    gate_local = jnp.einsum(
        "slcd,slcf->ldf", inputs_four, gate_pre_grad, preferred_element_type=jnp.float32
    )
    up_local = jnp.einsum(
        "slcd,slcf->ldf", inputs_four, up_pre_grad, preferred_element_type=jnp.float32
    )
    down_local = jnp.einsum(
        "slcd,slcf->ldf", grad_four, hidden_four, preferred_element_type=jnp.float32
    )
    gate_grad, up_grad, down_grad = (
        lax.psum_scatter(
            gate_local.astype(jnp.bfloat16), "seq", scatter_dimension=1, tiled=True
        ).astype(jnp.float32),
        lax.psum_scatter(
            up_local.astype(jnp.bfloat16), "seq", scatter_dimension=1, tiled=True
        ).astype(jnp.float32),
        lax.psum_scatter(
            down_local.astype(jnp.bfloat16), "seq", scatter_dimension=1, tiled=True
        ).astype(jnp.float32),
    )
    route_grad = (
        jnp.where(
            route_kept[:, None],
            jnp.take(returned_grad.reshape(experts * capacity, model_width), pair_slot, axis=0),
            0,
        )
        .reshape(tokens, 2, model_width)
        .astype(jnp.float32)
    )
    normed_two_grad = (
        route_grad[:, 0]
        + route_grad[:, 1]
        + jnp.einsum("te,de->td", logit_grad, attn_back[7], preferred_element_type=jnp.float32)
    )
    router_local = jnp.einsum(
        "td,te->de", normed_two, logit_grad, preferred_element_type=jnp.float32
    )
    unused_mid, norm_two_pull = jax.vjp(rms_norm, resid_mid, attn_back[5].astype(jnp.float32))
    mid_norm_grad, ffn_gain_local = norm_two_pull(normed_two_grad)
    middle_grad = grad_out + mid_norm_grad
    branch_grad = middle_grad.astype(jnp.bfloat16)
    output_local = jnp.einsum(
        "td,te->de", mixed_all, branch_grad, preferred_element_type=jnp.float32
    )
    mix_grad = jnp.einsum(
        "te,de->td", branch_grad, attn_back[3], preferred_element_type=jnp.float32
    ).astype(jnp.bfloat16)
    long_mix_grad = mix_grad[:long_rows].reshape(long_items, quarter, model_width)
    short_mix_grad = mix_grad[long_rows:].reshape(short_items, short_len, model_width)
    table_back = attn_back[6].reshape(HEADS, BUCKETS)

    def long_item(pack):
        single = [member_item[None] for member_item in pack]
        parts = attention_backward(
            single[0],
            single[1],
            single[2],
            single[3],
            single[4],
            single[5],
            single[6],
            single[7],
            table_back,
        )
        return (parts[0][0], parts[1][0], parts[2][0], parts[3])

    long_parts = lax.map(
        long_item,
        (
            long_q,
            long_keys,
            long_values,
            long_mix_grad,
            long_lse,
            query_pos,
            long_positions,
            long_ok,
        ),
    )
    long_key_grad, long_value_grad = (
        lax.psum_scatter(
            long_parts[1].astype(jnp.bfloat16), "seq", scatter_dimension=1, tiled=True
        ).astype(jnp.float32),
        lax.psum_scatter(
            long_parts[2].astype(jnp.bfloat16), "seq", scatter_dimension=1, tiled=True
        ).astype(jnp.float32),
    )
    short_parts = attention_backward(
        short_q,
        short_k,
        short_v,
        short_mix_grad,
        short_lse,
        short_positions,
        short_positions,
        short_ok,
        table_back,
    )
    query_act = jnp.concatenate(
        [long_parts[0].reshape(long_rows, model_width), short_parts[0].reshape(-1, model_width)], 0
    ).astype(jnp.bfloat16)
    key_act = jnp.concatenate(
        [long_key_grad.reshape(long_rows, model_width), short_parts[1].reshape(-1, model_width)], 0
    ).astype(jnp.bfloat16)
    value_act = jnp.concatenate(
        [long_value_grad.reshape(long_rows, model_width), short_parts[2].reshape(-1, model_width)],
        0,
    ).astype(jnp.bfloat16)
    table_local = (jnp.sum(long_parts[3], axis=0) + short_parts[3]).reshape(-1)
    normed_grad = (
        jnp.einsum("te,de->td", query_act, attn_back[0], preferred_element_type=jnp.float32)
        + jnp.einsum("te,de->td", key_act, attn_back[1], preferred_element_type=jnp.float32)
        + jnp.einsum("te,de->td", value_act, attn_back[2], preferred_element_type=jnp.float32)
    )
    query_local = jnp.einsum("td,te->de", normed, query_act, preferred_element_type=jnp.float32)
    key_local = jnp.einsum("td,te->de", normed, key_act, preferred_element_type=jnp.float32)
    value_local = jnp.einsum("td,te->de", normed, value_act, preferred_element_type=jnp.float32)
    unused_in, norm_one_pull = jax.vjp(rms_norm, resid_in, attn_back[4].astype(jnp.float32))
    in_norm_grad, attn_gain_local = norm_one_pull(normed_grad)
    input_grad_all = middle_grad + in_norm_grad
    long_grad_in = input_grad_all[:long_rows].reshape(long_items, quarter, model_width)
    short_grad_in = input_grad_all[long_rows:].reshape(short_items, short_len, model_width)
    summed = (
        lax.psum_scatter(query_local, ("seq", "dp"), scatter_dimension=0, tiled=True),
        lax.psum_scatter(key_local, ("seq", "dp"), scatter_dimension=0, tiled=True),
        lax.psum_scatter(value_local, ("seq", "dp"), scatter_dimension=0, tiled=True),
        lax.psum_scatter(output_local, ("seq", "dp"), scatter_dimension=0, tiled=True),
        lax.psum_scatter(attn_gain_local, ("seq", "dp"), scatter_dimension=0, tiled=True),
        lax.psum_scatter(ffn_gain_local, ("seq", "dp"), scatter_dimension=0, tiled=True),
        lax.psum_scatter(table_local, ("seq", "dp"), scatter_dimension=0, tiled=True),
        lax.psum_scatter(router_local, ("seq", "dp"), scatter_dimension=0, tiled=True),
    )
    return (
        long_out,
        short_out,
        long_grad_in,
        short_grad_in,
        summed[0],
        summed[1],
        summed[2],
        summed[3],
        summed[4],
        summed[5],
        summed[6],
        summed[7],
        gate_grad,
        up_grad,
        down_grad,
    )


def solution(mesh):
    placed = (
        P("dp", "seq", None),
        P(("seq", "dp"), None, None),
        P("dp", "seq", None),
        P(("seq", "dp"), None, None),
        P(("seq", "dp"), None),
        P(("seq", "dp"), None),
        P(("seq", "dp"), None),
        P(("seq", "dp"), None),
        P(("seq", "dp")),
        P(("seq", "dp")),
        P(("seq", "dp")),
        P(("seq", "dp"), None),
        P("dp", "seq", None),
        P("dp", "seq", None),
        P("dp", "seq", None),
        P("dp", None),
        P(("seq", "dp"), None),
        P("dp"),
        P(("seq", "dp")),
        P("dp", "seq", None),
        P(("seq", "dp"), None, None),
    )
    return jax.shard_map(
        on_device,
        mesh=mesh,
        in_specs=placed,
        out_specs=(
            P("dp", "seq", None),
            P(("seq", "dp"), None, None),
            P("dp", "seq", None),
            P(("seq", "dp"), None, None),
            P(("seq", "dp"), None),
            P(("seq", "dp"), None),
            P(("seq", "dp"), None),
            P(("seq", "dp"), None),
            P(("seq", "dp")),
            P(("seq", "dp")),
            P(("seq", "dp")),
            P(("seq", "dp"), None),
            P("dp", "seq", None),
            P("dp", "seq", None),
            P("dp", "seq", None),
        ),
        check_vma=False,
    )
```

profile of v0, /device:TPU:0, one launch (start us, length us, event | category | flops | bytes accessed | tf_op | source)
XLA Modules:
  0.0 1739.7 jit_solution(6333741280781654339)
XLA Ops:
  12.0 42.1 %all-reduce.7 = (bf16[1024]{0:T(1024)(128)(2,1)S(1)}, bf16[512]{0:T(512)(128)(2,1)S(1)}, bf16[1024]{0:T(1024)(128)(2,1)S(1)}) all-reduce(bf16[1024]{0:T(1024)(128)(2,1)S(1)} %dynamic-update-slice, bf16[512]{0:T(512)(128)(2,1)S(1)} %dynamic-update-slice.1, ...), channel_id=1, replica_groups=mesh['seq'=4,'dp'=8] {'seq','dp'}, use_global_device_ids=true, to_apply=%add | all-reduce | flops 2560 | bytes 10240
  56.2 14.1 all-gather.17.cloned.1.call-done
  75.5 53.2 %all-gather.11.cloned.1.call-done = bf16[1024,1024]{1,0:T(8,128)(2,1)} async-done(((bf16[32,1024]{1,0:T(8,128)(2,1)}), bf16[1024,1024]{1,0:T(8,128)(2,1)}) %all-gather.11.cloned.1.call-update) | async-done | bytes 2097168 | tf_op jit(solution)/shard_map/all_gather | solution.py:142
  137.8 5.9 fusion.21
  143.8 67.0 %all-gather = bf16[32,32,8]{1,2,0:T(8,128)(2,1)S(1)} all-gather(bf16[1,32,8]{1,2,0:T(8,128)(2,1)S(1)} %bitcast.402), channel_id=1, replica_groups=mesh['seq'=4,'dp'=8] {'seq','dp'}, dimensions={0}, use_global_device_ids=true | all-gather | bytes 16896 | tf_op jit(solution)/shard_map/all_gather | solution.py:147
  219.2 6.2 mul.343
  252.4 10.1 fusion.162
  267.9 6.2 fusion.89
  274.9 20.2 %all-gather.21.cloned.1.call-done = bf16[1024,1024]{1,0:T(8,128)(2,1)} async-done(((bf16[32,1024]{1,0:T(8,128)(2,1)}), bf16[1024,1024]{1,0:T(8,128)(2,1)}) %all-gather.21.cloned.1.call-update) | async-done | bytes 2097168 | tf_op jit(solution)/shard_map/all_gather | solution.py:143
  300.4 4.5 scatter_custom_fusion.1
  304.9 5.1 gather_fusion
  317.1 5.1 gather_fusion.1
  322.2 4.6 select_select_fusion
  331.7 59.2 %all-to-all-done.2 = bf16[8,160,1024]{2,1,0:T(8,128)(2,1)S(1)} async-done(((bf16[8,160,1024]{2,1,0:T(8,128)(2,1)}), bf16[8,160,1024]{2,1,0:T(8,128)(2,1)S(1)}, u32[]{:S(2)}, u32[]{:S(2)}) %all-to-all-start.2) | async-done | bytes 2621472 | tf_op jit(solution)/shard_map/all_to_all | solution.py:278
  391.0 4.7 all-to-all-start
  395.7 13.5 fusion.43
  409.2 45.5 %all-to-all-done = bf16[8,160,1024]{2,1,0:T(8,128)(2,1)} async-done(((bf16[8,160,1024]{2,1,0:T(8,128)(2,1)}), bf16[8,160,1024]{2,1,0:T(8,128)(2,1)}, u32[]{:S(2)}, u32[]{:S(2)}) %all-to-all-start) | async-done | bytes 2621472 | tf_op jit(solution)/shard_map/all_to_all | solution.py:210
  454.7 13.8 fusion.49
  468.5 24.6 %fusion.37 = (bf16[8,160,2816]{2,1,0:T(8,128)(2,1)S(1)}, bf16[8,1,160,2816]{3,2,0,1:T(8,128)(2,1)}, bf16[8,160,2816]{2,1,0:T(8,128)(2,1)}) fusion(f32[8,160,2816]{2,1,0:T(8,128)} %fusion.43, f32[8,160,2816]{2,1,0:T(8,128)} %fusion.49, bf16[8,160,1024]{2,1,0:T(8,128)(2,1)} %all-to-all-done, bf16[1,1024,2816]{2,1,0:T(8,128)(2,1)} %all-gather.23.cloned.1.call-done), kind=kOutput, calls=%fused_computation.75 | convolution fusion | flops 7475691520 | bytes 58851328 | tf_op jit(solution)/shard_map/slcd,ldf->slcf/dot_general | solution.py:213
  493.1 14.4 fusion.40
  507.5 10.9 add_convert_fusion
  522.1 12.7 fusion.83
  534.7 47.0 %all-to-all-done.3 = bf16[8,160,1024]{2,1,0:T(8,128)(2,1)S(1)} async-done(((bf16[8,160,1024]{2,1,0:T(8,128)(2,1)}), bf16[8,160,1024]{2,1,0:T(8,128)(2,1)S(1)}, u32[]{:S(2)}, u32[]{:S(2)}) %all-to-all-start.3) | async-done | bytes 2621472 | tf_op jit(solution)/shard_map/all_to_all | solution.py:294
  586.7 5.8 gather_fusion.3
  592.5 52.6 %all-to-all-done.1 = bf16[8,160,1024]{2,1,0:T(8,128)(2,1)} async-done(((bf16[8,160,1024]{2,1,0:T(8,128)(2,1)}), bf16[8,160,1024]{2,1,0:T(8,128)(2,1)}, u32[]{:S(2)}, u32[]{:S(2)}) %all-to-all-start.1) | async-done | bytes 2621472 | tf_op jit(solution)/shard_map/all_to_all | solution.py:219
  645.1 7.1 gather_fusion.2
  659.4 5.8 reshape.699
  665.2 9.2 fusion.153
  675.0 5.2 multiply_reduce_fusion.2
  680.2 6.0 reshape.698
  686.3 7.2 fusion.154
  698.4 85.9 %while.16 = (s32[]{:T(128)}, bf16[2,128,1024]{2,1,0:T(8,128)(2,1)}, bf16[2,512,1024]{2,1,0:T(8,128)(2,1)}, bf16[2,512,1024]{2,1,0:T(8,128)(2,1)}, f32[2,16,32]{2...) while((s32[]{:T(128)}, bf16[2,128,1024]{2,1,0:T(8,128)(2,1)}, ...), condition=%wide.region_22.24_spmd, body=%wide.region_20.23_spmd.sunk | while | flops 820770816 | bytes 123792768 | solution.py:369
  703.0 5.3 copy.304
  745.9 5.3 copy.304
  786.9 13.9 fusion.42
  800.9 13.0 fusion.56
  815.6 12.6 fusion.57
  846.5 5.0 fusion.110
  857.7 4.6 fusion.107
  868.3 4.5 fusion.108
  880.6 104.1 %reduce-scatter.31.cloned.1.call-done = f32[32,8]{1,0:T(8,128)} async-done(((f32[1024,8]{1,0:T(8,128)}), f32[32,8]{1,0:T(8,128)}) %reduce-scatter.31.cloned.1.call-update) | async-done | bytes 1040
  993.0 37.3 %all-reduce.6 = (f32[1024]{0:T(1024)S(1)}, f32[1024]{0:T(1024)S(1)}, f32[512]{0:T(512)S(1)}) all-reduce(f32[1024]{0:T(1024)S(1)} %get-tuple-element.153, f32[1024]{0:T(1024)S(1)} %copy-done.72, f32[512]{0:T(512)S(1)} %reshape.697), channel_id=8, replica_groups=mesh['seq'=4,'dp'=8] {'seq','dp'}, use_global_device_ids=true, to_apply=%region_32.34.clone | all-reduce | flops 2560 | bytes 20480
  1042.8 54.2 %reduce-scatter.27.cloned.1.call-done = bf16[1,256,2816]{2,1,0:T(8,128)(2,1)} async-done(((bf16[1,1024,2816]{2,1,0:T(8,128)(2,1)}), bf16[1,256,2816]{2,1,0:T(8,128)(2,1)}) %reduce-scatter.27.cloned.1.call-update) | async-done | bytes 1441808 | tf_op jit(solution)/shard_map/reduce_scatter | solution.py:316
  1100.1 54.3 %reduce-scatter.29.cloned.1.call-done = bf16[1,256,2816]{2,1,0:T(8,128)(2,1)} async-done(((bf16[1,1024,2816]{2,1,0:T(8,128)(2,1)}), bf16[1,256,2816]{2,1,0:T(8,128)(2,1)}) %reduce-scatter.29.cloned.1.call-update) | async-done | bytes 1441808 | tf_op jit(solution)/shard_map/reduce_scatter | solution.py:319
  1157.5 143.8 %reduce-scatter.23.cloned.1.call-done = f32[32,1024]{1,0:T(8,128)} async-done(((f32[1024,1024]{1,0:T(8,128)}), f32[32,1024]{1,0:T(8,128)}) %reduce-scatter.23.cloned.1.call-update) | async-done | bytes 131088 | tf_op jit(solution)/shard_map/reduce_scatter | solution.py:429
  1301.3 143.4 %reduce-scatter.17.cloned.1.call-done = f32[32,1024]{1,0:T(8,128)} async-done(((f32[1024,1024]{1,0:T(8,128)}), f32[32,1024]{1,0:T(8,128)}) %reduce-scatter.17.cloned.1.call-update) | async-done | bytes 131088 | tf_op jit(solution)/shard_map/reduce_scatter | solution.py:426
  1444.7 144.1 %reduce-scatter.21.cloned.1.call-done = f32[32,1024]{1,0:T(8,128)} async-done(((f32[1024,1024]{1,0:T(8,128)}), f32[32,1024]{1,0:T(8,128)}) %reduce-scatter.21.cloned.1.call-update) | async-done | bytes 131088 | tf_op jit(solution)/shard_map/reduce_scatter | solution.py:428
  1588.8 144.2 %reduce-scatter.19.cloned.1.call-done = f32[32,1024]{1,0:T(8,128)} async-done(((f32[1024,1024]{1,0:T(8,128)}), f32[32,1024]{1,0:T(8,128)}) %reduce-scatter.19.cloned.1.call-update) | async-done | bytes 131088 | tf_op jit(solution)/shard_map/reduce_scatter | solution.py:427
  (438 shorter events, 245.0 us)
Async XLA Ops:
  7.2 63.1 %all-gather.17.cloned.1.call-start = ((), (), s32[]{:S(2)}) async-start(), calls=%async_computation.17 | async-start | bytes 2162688 | tf_op jit(solution)/shard_map/all_gather | solution.py:141
  7.9 120.8 %all-gather.11.cloned.1.call-start = ((), (), s32[]{:S(2)}) async-start(), calls=%async_computation.14 | async-start | bytes 2162688 | tf_op jit(solution)/shard_map/all_gather | solution.py:142
  8.7 216.7 %all-gather.15.cloned.1.call-start = ((), (), s32[]{:S(2)}) async-start(), calls=%async_computation.16 | async-start | bytes 2162688 | tf_op jit(solution)/shard_map/all_gather | solution.py:140
  9.4 243.0 %all-gather.19.cloned.1.call-start = ((), (), s32[]{:S(2)}) async-start(), calls=%async_computation.18 | async-start | bytes 2621440 | tf_op jit(solution)/shard_map/all_gather | solution.py:171
  54.1 82.0 %copy-start.78 = (bf16[512]{0:T(512)(128)(2,1)}, bf16[512]{0:T(512)(128)(2,1)S(1)}, u32[]{:S(2)}) copy-start(bf16[512]{0:T(512)(128)(2,1)S(1)} %get-tuple-element.189) | copy-start | bytes 3076
  54.1 171.3 %copy-start.70 = (f32[1024]{0:T(1024)}, f32[1024]{0:T(1024)S(1)}, u32[]{:S(2)}) copy-start(f32[1024]{0:T(1024)S(1)} %convert_element_type.341) | copy-start | bytes 12292
  56.2 169.2 %copy-start.73 = (f32[512]{0:T(512)}, f32[512]{0:T(512)S(1)}, u32[]{:S(2)}) copy-start(f32[512]{0:T(512)S(1)} %fusion.139) | copy-start | bytes 6148
  73.5 55.2 %copy-start.21 = (bf16[2,128,1024]{2,1,0:T(8,128)(2,1)S(1)}, bf16[2,128,1024]{2,1,0:T(8,128)(2,1)}, u32[]{:S(2)}) copy-start(bf16[2,128,1024]{2,1,0:T(8,128)(2,1)} %param.26) | copy-start | bytes 1572868
  73.5 55.2 %copy-start.24 = (bf16[2,128,1024]{2,1,0:T(8,128)(2,1)S(1)}, bf16[2,128,1024]{2,1,0:T(8,128)(2,1)}, u32[]{:S(2)}) copy-start(bf16[2,128,1024]{2,1,0:T(8,128)(2,1)} %param.25) | copy-start | bytes 1572868
  75.4 192.5 %all-gather.13.cloned.1.call-start = ((), (), s32[]{:S(2)}) async-start(), calls=%async_computation.15 | async-start | bytes 2621440 | tf_op jit(solution)/shard_map/all_gather | solution.py:172
  133.5 161.6 %all-gather.21.cloned.1.call-start = ((), (), s32[]{:S(2)}) async-start(), calls=%async_computation.19 | async-start | bytes 2162688 | tf_op jit(solution)/shard_map/all_gather | solution.py:143
  134.1 261.6 %all-gather.27.cloned.1.call-start = ((), (), s32[]{:S(2)}) async-start(), calls=%async_computation.22 | async-start | bytes 7208960 | tf_op jit(solution)/shard_map/all_gather | solution.py:152
  134.8 274.4 %all-gather.25.cloned.1.call-start = ((), (), s32[]{:S(2)}) async-start(), calls=%async_computation.21 | async-start | bytes 7208960 | tf_op jit(solution)/shard_map/all_gather | solution.py:151
  135.6 163.9 %copy-start.56 = (s32[512,2]{0,1:T(2,128)}, s32[512,2]{0,1:T(2,128)S(1)}, u32[]{:S(2)}) copy-start(s32[512,2]{0,1:T(2,128)S(1)} %get-tuple-element.228) | copy-start | bytes 12292
  143.8 108.6 %copy-start.50 = (pred[2,512]{1,0:T(4,128)(4,1)}, pred[2,512]{1,0:T(4,128)(4,1)S(1)}, u32[]{:S(2)}) copy-start(pred[2,512]{1,0:T(4,128)(4,1)S(1)} %iota_compare_fusion.19) | copy-start | bytes 3076
  143.8 154.3 %copy-start.52 = (f32[1024]{0:T(1024)}, f32[1024]{0:T(1024)S(1)}, u32[]{:S(2)}) copy-start(f32[1024]{0:T(1024)S(1)} %convert_element_type.367) | copy-start | bytes 12292
  211.0 88.0 %copy-start.48 = (bf16[1024,8]{0,1:T(8,128)(2,1)}, bf16[1024,8]{0,1:T(8,128)(2,1)S(1)}, u32[]{:S(2)}) copy-start(bf16[1024,8]{0,1:T(8,128)(2,1)S(1)} %reshape.759) | copy-start | bytes 49156
  274.9 23.2 %copy-start.17 = (bf16[512,1024]{0,1:T(8,128)(2,1)}, bf16[512,1024]{0,1:T(8,128)(2,1)S(1)}, u32[]{:S(2)}) copy-start(bf16[512,1024]{0,1:T(8,128)(2,1)S(1)} %bitcast_dynamic-update-slice_fusion) | copy-start | bytes 3145732
  299.0 11.0 copy-start.2
  299.4 10.6 copy-start.62
  299.5 10.5 copy-start.58
  326.7 64.2 %all-to-all-start.2 = ((bf16[8,160,1024]{2,1,0:T(8,128)(2,1)}), bf16[8,160,1024]{2,1,0:T(8,128)(2,1)S(1)}, u32[]{:S(2)}, u32[]{:S(2)}) async-start(bf16[8,160,1024]{2,1,0:T(8,128)(2,1)} %get-tuple-element.233), calls=%async_computation.2 | async-start | bytes 5242880 | tf_op jit(solution)/shard_map/all_to_all | solution.py:278
  331.0 137.5 %all-gather.23.cloned.1.call-start = ((), (), s32[]{:S(2)}) async-start(), calls=%async_computation.20 | async-start | bytes 7208960 | tf_op jit(solution)/shard_map/all_gather | solution.py:150
  391.0 63.8 %all-to-all-start = ((bf16[8,160,1024]{2,1,0:T(8,128)(2,1)}), bf16[8,160,1024]{2,1,0:T(8,128)(2,1)}, u32[]{:S(2)}, u32[]{:S(2)}) async-start(bf16[8,160,1024]{2,1,0:T(8,128)(2,1)} %get-tuple-element.234), calls=%async_computation | async-start | bytes 5242880 | tf_op jit(solution)/shard_map/all_to_all | solution.py:210
  468.5 24.6 %copy-start.85 = (bf16[1,1024,2816]{2,1,0:T(8,128)(2,1)S(1)}, bf16[1,1024,2816]{2,1,0:T(8,128)(2,1)}, u32[]{:S(2)}) copy-start(bf16[1,1024,2816]{2,1,0:T(8,128)(2,1)} %all-gather.23.cloned.1.call-done) | copy-start | bytes 17301508
  493.1 14.4 copy-start.92
  493.1 14.4 copy-start.84
  518.5 63.3 %all-to-all-start.3 = ((bf16[8,160,1024]{2,1,0:T(8,128)(2,1)}), bf16[8,160,1024]{2,1,0:T(8,128)(2,1)S(1)}, u32[]{:S(2)}, u32[]{:S(2)}) async-start(bf16[8,160,1024]{2,1,0:T(8,128)(2,1)} %add_convert_fusion), calls=%async_computation.3 | async-start | bytes 5242880 | tf_op jit(solution)/shard_map/all_to_all | solution.py:294
  534.7 51.5 %copy-start.79 = (bf16[512]{0:T(512)(128)(2,1)S(1)}, bf16[512]{0:T(512)(128)(2,1)}, u32[]{:S(2)}) copy-start(bf16[512]{0:T(512)(128)(2,1)} %copy-done.78) | copy-start | bytes 3076
  581.7 63.4 %all-to-all-start.1 = ((bf16[8,160,1024]{2,1,0:T(8,128)(2,1)}), bf16[8,160,1024]{2,1,0:T(8,128)(2,1)}, u32[]{:S(2)}, u32[]{:S(2)}) async-start(bf16[8,160,1024]{2,1,0:T(8,128)(2,1)} %fusion.83), calls=%async_computation.1 | async-start | bytes 5242880 | tf_op jit(solution)/shard_map/all_to_all | solution.py:219
  586.1 271.5 %reduce-scatter.15.cloned.1.call-start = ((), (), s32[]{:S(2)}) async-start(), calls=%async_computation.24 | async-start | bytes 2621440 | tf_op jit(solution)/shard_map/reduce_scatter | solution.py:386
  665.2 9.7 copy-start.10
  665.2 9.7 copy-start.49
  665.2 9.7 copy-start.53
  665.2 9.7 copy-start.65
  784.4 83.9 %reduce-scatter.13.cloned.1.call-start = ((), (), s32[]{:S(2)}) async-start(), calls=%async_computation.23 | async-start | bytes 2621440 | tf_op jit(solution)/shard_map/reduce_scatter | solution.py:383
  785.1 199.6 %reduce-scatter.31.cloned.1.call-start = ((), (), s32[]{:S(2)}) async-start(), calls=%async_computation.32 | async-start | bytes 540672
  786.9 252.8 %reduce-scatter.25.cloned.1.call-start = ((), (), s32[]{:S(2)}) async-start(), calls=%async_computation.29 | async-start | bytes 7208960 | tf_op jit(solution)/shard_map/reduce_scatter | solution.py:313
  800.8 296.1 %reduce-scatter.27.cloned.1.call-start = ((), (), s32[]{:S(2)}) async-start(), calls=%async_computation.30 | async-start | bytes 7208960 | tf_op jit(solution)/shard_map/reduce_scatter | solution.py:316
  813.9 340.5 %reduce-scatter.29.cloned.1.call-start = ((), (), s32[]{:S(2)}) async-start(), calls=%async_computation.31 | async-start | bytes 7208960 | tf_op jit(solution)/shard_map/reduce_scatter | solution.py:319
  828.2 473.0 %reduce-scatter.23.cloned.1.call-start = ((), (), s32[]{:S(2)}) async-start(), calls=%async_computation.28 | async-start | bytes 4325376 | tf_op jit(solution)/shard_map/reduce_scatter | solution.py:429
  833.4 611.3 %reduce-scatter.17.cloned.1.call-start = ((), (), s32[]{:S(2)}) async-start(), calls=%async_computation.25 | async-start | bytes 4325376 | tf_op jit(solution)/shard_map/reduce_scatter | solution.py:426
  851.5 737.2 %reduce-scatter.21.cloned.1.call-start = ((), (), s32[]{:S(2)}) async-start(), calls=%async_computation.27 | async-start | bytes 4325376 | tf_op jit(solution)/shard_map/reduce_scatter | solution.py:428
  862.3 870.6 %reduce-scatter.19.cloned.1.call-start = ((), (), s32[]{:S(2)}) async-start(), calls=%async_computation.26 | async-start | bytes 4325376 | tf_op jit(solution)/shard_map/reduce_scatter | solution.py:427
  876.9 109.2 %copy-start.41 = (bf16[256,1024]{1,0:T(8,128)(2,1)S(1)}, bf16[256,1024]{1,0:T(8,128)(2,1)}, u32[]{:S(2)}) copy-start(bf16[256,1024]{1,0:T(8,128)(2,1)} %reshape.777) | copy-start | bytes 1572868
  876.9 109.2 %copy-start.89 = (bf16[2,128,1024]{2,1,0:T(8,128)(2,1)S(1)}, bf16[2,128,1024]{2,1,0:T(8,128)(2,1)}, u32[]{:S(2)}) copy-start(bf16[2,128,1024]{2,1,0:T(8,128)(2,1)} %reduce-scatter.13.cloned.1.call-done) | copy-start | bytes 1572868
  989.9 42.2 %copy-start.67 = (f32[512]{0:T(512)S(1)}, f32[512]{0:T(512)}, u32[]{:S(2)}) copy-start(f32[512]{0:T(512)} %copy-done.66) | copy-start | bytes 6148
  989.9 42.2 %copy-start.16 = (f32[512,1024]{1,0:T(8,128)S(1)}, f32[512,1024]{1,0:T(8,128)}, u32[]{:S(2)}) copy-start(f32[512,1024]{1,0:T(8,128)} %copy-done.14) | copy-start | bytes 6291460
  (75 other events, 243.0 us)
Sparse Core Ops, SparseCore 0:
  11.0 59.2 all-gather.16
  73.3 55.3 all-gather.10
  131.7 55.4 all-gather.14
  189.2 21.6 all-gather.18
  212.8 22.8 all-gather.12
  238.5 56.5 all-gather.20
  296.7 42.2 all-gather.26
  340.5 43.3 all-gather.24
  385.5 43.3 all-gather.22
  784.5 30.0 reduce-scatter.14
  817.3 31.4 reduce-scatter.12
  850.8 133.8 reduce-scatter.30
  987.5 52.1 reduce-scatter.24
  1042.0 54.8 reduce-scatter.26
  1099.5 54.8 reduce-scatter.28
  1157.1 144.1 reduce-scatter.22
  1304.0 140.6 reduce-scatter.16
  1447.4 141.3 reduce-scatter.20
  1591.6 141.3 reduce-scatter.18
where the time goes:
time: 1750 us; the launch traced here: 1740 us
  waiting for transfers between devices  1090 us (62%)
  matrix products  248 us (14%)
  local copies, waits for them, and re-layouts  181 us (10%)
  blocking collectives  146 us (8%)
  other arithmetic  40 us (2%)
  starting transfers between devices  18.3 us (1%)
    reduce_scatter x1, waiting for transfers between devices, on_device(): lax.psum_scatter(key_local, ('seq', 'dp'), scatter_dimension=0, tiled=True)  144 us
    reduce_scatter x1, waiting for transfers between devices, on_device(): lax.psum_scatter(value_local, ('seq', 'dp'), scatter_dimension=0, tiled=T...  144 us
    reduce_scatter x1, waiting for transfers between devices, on_device(): lax.psum_scatter(output_local, ('seq', 'dp'), scatter_dimension=0, tiled=...  144 us
    reduce_scatter x1, waiting for transfers between devices, on_device(): lax.psum_scatter(query_local, ('seq', 'dp'), scatter_dimension=0, tiled=T...  143 us
    unnamed x20, waiting for transfers between devices  110 us
    unnamed x2, blocking collectives  79.4 us
    all_gather x1, blocking collectives, on_device(): lax.all_gather(router_weight, ('seq', 'dp'), axis=0, tiled=True)  67 us
    all_to_all x1, waiting for transfers between devices, on_device(): lax.all_to_all(out_slots, 'dp', split_axis=0, concat_axis=0, tiled=True)  59.2 us
  transfers between devices with their start and end apart: 23, of which 15 were waited for; matrix products, arithmetic and copies ran while one was open for 15% of the time, Pallas kernels for 0%

commit v1 on v0

--- a/solution.py
+++ b/solution.py
@@ -1,7 +1,13 @@
+import functools
+
 import jax
 import jax.numpy as jnp
 from jax import lax
+from jax.experimental import pallas as pl
+from jax.experimental.pallas import tpu as pltpu
 from jax.sharding import PartitionSpec as P
+
+MESH = pl.DeviceIdType.MESH
 
 HEADS = 16
 HEAD = 64
@@ -102,6 +108,149 @@
     ).reshape(batch_size, columns, model_width)
     table_part = jnp.einsum("bhqk,bqkn->hn", score_grad, onehot, preferred_element_type=jnp.float32)
     return (query_part, key_part, value_part, table_part)
+
+
+def gather_kernel(dims, pieces, na, *refs):
+    X, C, Z, Y = dims
+    n = len(pieces)
+    lsem, zs, zr, hs, hr, cs, cr = refs[2*na:]
+    routes = [p[3] for p in pieces]
+    ins = [refs[m].at[pl.ds(r0, nr)] for m, r0, nr, _ in pieces]
+    class V:
+        def __init__(self, ref, r0, nr): self.ref, self.r0, self.nr = ref, r0, nr
+        @property
+        def at(self): return self
+        def __getitem__(self, k):
+            k = k + (slice(None),) * (4 - len(k)) + (pl.ds(self.r0, self.nr),)
+            return self.ref.at[k]
+    outs = [V(refs[na + m], r0, nr) for m, r0, nr, _ in pieces]
+    s = lax.axis_index("seq"); g = lax.axis_index("dp")
+    x, c = s // C, lax.rem(s, C)
+    z, y = g // Y, lax.rem(g, Y)
+    def zdev(k): return (s, lax.rem(z + k, Z) * Y + y)
+    ydev = (s, z * Y + (1 - y)); xdev = ((1 - x) * C + c, g); cdev = (x * C + 1 - c, g)
+    bar = pltpu.get_barrier_semaphore()
+    for d in [zdev(k) for k in range(1, Z)] + [ydev, xdev, cdev]:
+        pl.semaphore_signal(bar, inc=1, device_id=d, device_id_type=MESH)
+    pl.semaphore_wait(bar, Z + 2)
+    def rc(src, dst, ss, rs, dev):
+        cp = pltpu.make_async_remote_copy(src_ref=src, dst_ref=dst, send_sem=ss, recv_sem=rs, device_id=dev, device_id_type=MESH)
+        cp.start(); return cp
+    sends = []
+    local = []; zc = []
+    for m in range(n):
+        lc = pltpu.make_async_copy(ins[m], outs[m].at[x, c, z, y], lsem.at[m]); lc.start(); local.append(lc)
+        zc.append([rc(ins[m], outs[m].at[x, c, z, y], zs.at[m, k], zr.at[m, k], zdev(k)) for k in range(1, Z)])
+    h = [[None, None] for _ in range(n)]
+    cc = [[None]*3 for _ in range(n)]
+    for t in range(n + 2):
+        for stage in range(3):
+            m = t - stage
+            if not 0 <= m < n: continue
+            o = outs[m]; route = routes[m]
+            if stage == 0:
+                local[m].wait()
+                for q in zc[m]: q.wait_recv()
+                mine = o.at[x, c, :, y]
+                h[m][0] = rc(mine, mine, hs.at[m,0], hr.at[m,0], xdev if route == 0 else ydev)
+                cc[m][0] = rc(mine, mine, cs.at[m,0], cr.at[m,0], cdev)
+            elif stage == 1:
+                h[m][0].wait_recv()
+                if route == 0:
+                    both = o.at[:, c, :, y]; got = o.at[1 - x, c, :, y]
+                else:
+                    both = o.at[x, c]; got = o.at[x, c, :, 1 - y]
+                h[m][1] = rc(both, both, hs.at[m,1], hr.at[m,1], ydev if route == 0 else xdev)
+                cc[m][1] = rc(got, got, cs.at[m,1], cr.at[m,1], cdev)
+            else:
+                h[m][1].wait_recv()
+                got = o.at[:, c, :, 1 - y] if route == 0 else o.at[1 - x, c]
+                cc[m][2] = rc(got, got, cs.at[m,2], cr.at[m,2], cdev)
+    for m in range(n):
+        for q in zc[m]: q.wait_send()
+        for q in h[m]: q.wait_send()
+        for q in cc[m]: q.wait()
+def gather_all(arrays, pieces, dims, cid):
+    X, C, Z, Y = dims; na = len(arrays); n = len(pieces)
+    sem = pltpu.SemaphoreType.DMA
+    return pl.pallas_call(functools.partial(gather_kernel, dims, pieces, na),
+        out_shape=[jax.ShapeDtypeStruct((X, C, Z, Y) + a.shape, a.dtype) for a in arrays],
+        in_specs=[pl.BlockSpec(memory_space=pl.ANY)] * na, out_specs=[pl.BlockSpec(memory_space=pl.ANY)] * na,
+        scratch_shapes=[sem((n,)), sem((n, Z)), sem((n, Z)), sem((n, 2)), sem((n, 2)), sem((n, 3)), sem((n, 3))],
+        compiler_params=pltpu.CompilerParams(collective_id=cid, has_side_effects=True))(*arrays)
+
+
+def scatter_kernel(dims, pieces, n, *refs):
+    X, C, Z, Y = dims
+    ins, outs = refs[:n], refs[n:2*n]
+    np_ = len(pieces)
+    bufs = refs[2*n:2*n+7*np_]
+    sems = refs[2*n+7*np_:]
+    cs, cr, hs, hr, zs, zr = sems
+    s = lax.axis_index("seq"); g = lax.axis_index("dp")
+    x, c = s // C, lax.rem(s, C)
+    z, y = g // Y, lax.rem(g, Y)
+    def zdev(k): return (s, lax.rem(z + k, Z) * Y + y)
+    ydev = (s, z * Y + (1 - y)); xdev = ((1 - x) * C + c, g); cdev = (x * C + 1 - c, g)
+    bar = pltpu.get_barrier_semaphore()
+    for d in [zdev(k) for k in range(1, Z)] + [ydev, xdev, cdev]:
+        pl.semaphore_signal(bar, inc=1, device_id=d, device_id_type=MESH)
+    pl.semaphore_wait(bar, Z + 2)
+    def rc(src, dst, ss, rs, dev):
+        cp = pltpu.make_async_remote_copy(src_ref=src, dst_ref=dst, send_sem=ss, recv_sem=rs, device_id=dev, device_id_type=MESH)
+        cp.start(); return cp
+    def add(dst, a, b):
+        dst[...] = (a.astype(jnp.float32) + b.astype(jnp.float32)).astype(dst.dtype)
+    first = []
+    for i, (m, r0, nr, route) in enumerate(pieces):
+        cb = bufs[7*i]
+        src = ins[m].at[:, 1 - c, :, :, pl.ds(r0, nr)]
+        first.append(rc(src, cb, cs.at[i], cr.at[i], cdev))
+    hh = [[None, None] for _ in pieces]; zz = [None] * np_
+    for t in range(np_ + 3):
+        for stage in range(4):
+            i = t - stage
+            if not 0 <= i < np_: continue
+            m, r0, nr, route = pieces[i]
+            cb, a1, b1, a2, b2, a3, b3 = bufs[7*i:7*i+7]
+            if stage == 0:
+                first[i].wait_recv()
+                add(a1, ins[m][:, c, :, :, pl.ds(r0, nr)], cb[...])
+                src = a1.at[:, :, 1 - y] if route == 0 else a1.at[1 - x]
+                hh[i][0] = rc(src, b1, hs.at[i, 0], hr.at[i, 0], ydev if route == 0 else xdev)
+            elif stage == 1:
+                hh[i][0].wait_recv()
+                add(a2, a1[:, :, y] if route == 0 else a1[x], b1[...])
+                src = a2.at[1 - x] if route == 0 else a2.at[:, 1 - y]
+                hh[i][1] = rc(src, b2, hs.at[i, 1], hr.at[i, 1], xdev if route == 0 else ydev)
+            elif stage == 2:
+                hh[i][1].wait_recv()
+                add(a3, a2[x] if route == 0 else a2[:, y], b2[...])
+                zz[i] = [rc(a3.at[lax.rem(z + k, Z)], b3.at[k - 1], zs.at[i, k], zr.at[i, k], zdev(k)) for k in range(1, Z)]
+            else:
+                tot = a3[z].astype(jnp.float32)
+                for k in range(1, Z):
+                    zz[i][k-1].wait_recv()
+                    tot += b3[k - 1].astype(jnp.float32)
+                outs[m][pl.ds(r0, nr), :] = tot
+    for i in range(np_):
+        first[i].wait_send()
+        for q in hh[i]: q.wait_send()
+        for q in zz[i]: q.wait_send()
+def scatter_all(arrays, pieces, dims, cid):
+    X, C, Z, Y = dims; n = len(arrays); q = len(pieces)
+    sem = pltpu.SemaphoreType.DMA
+    scr = []
+    for m, r0, nr, route in pieces:
+        w = arrays[m].shape[-1]; dt = arrays[m].dtype
+        h1 = (X, Z) if route == 0 else (Z, Y)
+        for lead in ((X, Z, Y), (X, Z, Y), h1, h1, (Z,), (Z,), (Z - 1,)):
+            scr.append(pltpu.VMEM(lead + (nr, w), dt))
+    return pl.pallas_call(functools.partial(scatter_kernel, dims, pieces, n),
+        out_shape=[jax.ShapeDtypeStruct(a.shape[-2:], jnp.float32) for a in arrays],
+        in_specs=[pl.BlockSpec(memory_space=pltpu.VMEM)] * n, out_specs=[pl.BlockSpec(memory_space=pltpu.VMEM)] * n,
+        scratch_shapes=scr + [sem((q,)), sem((q,)), sem((q, 2)), sem((q, 2)), sem((q, Z)), sem((q, Z))],
+        compiler_params=pltpu.CompilerParams(collective_id=cid, has_side_effects=True, vmem_limit_bytes=48*2**20))(*arrays)
 
 
 def on_device(
@@ -136,15 +285,30 @@
     experts = local_experts * dp_size
     capacity = (5 * tokens + 2 * experts - 1) // (2 * experts)
     seq_index = lax.axis_index("seq")
-    attn_set = (
-        lax.all_gather(query_weight, ("seq", "dp"), axis=0, tiled=True),
-        lax.all_gather(key_weight, ("seq", "dp"), axis=0, tiled=True),
-        lax.all_gather(value_weight, ("seq", "dp"), axis=0, tiled=True),
-        lax.all_gather(output_weight, ("seq", "dp"), axis=0, tiled=True),
-        lax.all_gather(attn_gain, ("seq", "dp"), axis=0, tiled=True),
-        lax.all_gather(ffn_gain, ("seq", "dp"), axis=0, tiled=True),
-        lax.all_gather(rel_table, ("seq", "dp"), axis=0, tiled=True),
-        lax.all_gather(router_weight, ("seq", "dp"), axis=0, tiled=True),
+    seq_size = lax.axis_size("seq")
+    dims = (seq_size // 2, 2, dp_size // 2, 2)
+    devices = seq_size * dp_size
+    table_part, router_part = rel_table.shape[0], router_weight.size
+    gain_part = attn_gain.shape[0]
+    small_size = 2 * gain_part + table_part + router_part
+    small = jnp.concatenate([attn_gain, ffn_gain, rel_table, router_weight.reshape(-1)])
+    small = jnp.pad(small, (0, -small_size % 2048)).reshape(-1, 128)
+    rows_part = query_weight.shape[0]
+    cuts = 2 if rows_part % 32 == 0 else 1
+    cut = rows_part // cuts
+    pieces = tuple((m, h * cut, cut, (m + h) % 2) for m in range(4) for h in range(cuts))
+    gathered = gather_all(
+        (query_weight, key_weight, value_weight, output_weight, small),
+        pieces[: 3 * cuts] + ((4, 0, small.shape[0], 0),) + pieces[3 * cuts :],
+        dims,
+        0,
+    )
+    small_all = gathered[4].reshape(devices, -1)
+    attn_set = tuple(block.reshape(devices * rows_part, model_width) for block in gathered[:4]) + (
+        small_all[:, :gain_part].reshape(-1),
+        small_all[:, gain_part : 2 * gain_part].reshape(-1),
+        small_all[:, 2 * gain_part : 2 * gain_part + table_part].reshape(-1),
+        small_all[:, 2 * gain_part + table_part : small_size].reshape(model_width, experts),
     )
     expert_set = (
         lax.all_gather(gate_weight, "seq", axis=1, tiled=True),
@@ -259,21 +423,7 @@
     out_slots = jnp.where(slot_used[:, None], jnp.take(pair_grad, slot_pair, axis=0), 0).reshape(
         experts, capacity, model_width
     )
-    attn_back = (
-        lax.all_gather(query_weight, ("seq", "dp"), axis=0, tiled=True),
-        lax.all_gather(key_weight, ("seq", "dp"), axis=0, tiled=True),
-        lax.all_gather(value_weight, ("seq", "dp"), axis=0, tiled=True),
-        lax.all_gather(output_weight, ("seq", "dp"), axis=0, tiled=True),
-        lax.all_gather(attn_gain, ("seq", "dp"), axis=0, tiled=True),
-        lax.all_gather(ffn_gain, ("seq", "dp"), axis=0, tiled=True),
-        lax.all_gather(rel_table, ("seq", "dp"), axis=0, tiled=True),
-        lax.all_gather(router_weight, ("seq", "dp"), axis=0, tiled=True),
-    )
-    expert_back = (
-        lax.all_gather(gate_weight, "seq", axis=1, tiled=True),
-        lax.all_gather(up_weight, "seq", axis=1, tiled=True),
-        lax.all_gather(down_weight, "seq", axis=1, tiled=True),
-    )
+    attn_back, expert_back = attn_set, expert_set
     gate_back, up_back, down_back = expert_back
     arrived_grad = lax.all_to_all(out_slots, "dp", split_axis=0, concat_axis=0, tiled=True)
     shape_four = (dp_size, local_experts, capacity, -1)
@@ -422,16 +572,31 @@
     input_grad_all = middle_grad + in_norm_grad
     long_grad_in = input_grad_all[:long_rows].reshape(long_items, quarter, model_width)
     short_grad_in = input_grad_all[long_rows:].reshape(short_items, short_len, model_width)
-    summed = (
-        lax.psum_scatter(query_local, ("seq", "dp"), scatter_dimension=0, tiled=True),
-        lax.psum_scatter(key_local, ("seq", "dp"), scatter_dimension=0, tiled=True),
-        lax.psum_scatter(value_local, ("seq", "dp"), scatter_dimension=0, tiled=True),
-        lax.psum_scatter(output_local, ("seq", "dp"), scatter_dimension=0, tiled=True),
-        lax.psum_scatter(attn_gain_local, ("seq", "dp"), scatter_dimension=0, tiled=True),
-        lax.psum_scatter(ffn_gain_local, ("seq", "dp"), scatter_dimension=0, tiled=True),
-        lax.psum_scatter(table_local, ("seq", "dp"), scatter_dimension=0, tiled=True),
-        lax.psum_scatter(router_local, ("seq", "dp"), scatter_dimension=0, tiled=True),
-    )
+    shares = (gain_part, gain_part, table_part, router_part)
+    small_local = jnp.concatenate(
+        [
+            part.reshape(devices, -1)
+            for part in (attn_gain_local, ffn_gain_local, table_local, router_local)
+        ],
+        1,
+    )
+    small_local = jnp.pad(small_local, ((0, 0), (0, -small_size % 1024)))
+    small_rows = small_local.shape[1] // 128
+    mats = tuple(
+        part.astype(jnp.bfloat16).reshape(dims + (rows_part, model_width))
+        for part in (output_local, query_local, key_local, value_local)
+    )
+    scattered = scatter_all(
+        mats + (small_local.reshape(dims + (small_rows, 128)),),
+        pieces[:cuts] + ((4, 0, small_rows, 0),) + pieces[cuts:],
+        dims,
+        1,
+    )
+    small_sum = scattered[4].reshape(-1)
+    edges = [sum(shares[:k]) for k in range(5)]
+    summed = (scattered[1], scattered[2], scattered[3], scattered[0]) + tuple(
+        small_sum[edges[k] : edges[k + 1]] for k in range(3)
+    ) + (small_sum[edges[3] : edges[4]].reshape(rows_part, experts),)
     return (
         long_out,
         short_out,

time: 1750 us -> 921 us (0.53)
  waiting for transfers between devices: 1090 us -> 274 us
  blocking collectives: 146 us -> 0 us
  Pallas kernels: 0 us -> 132 us
    reduce_scatter x4 -> x0, waiting for transfers between devices: 575 us -> none  [the longest x1 144 us: on_device(): lax.psum_scatter(key_local, ('seq', 'dp'), scatter_dimension=0, tiled=True)]
    pallas_call x0 -> x2, Pallas kernels: none -> 132 us  [the longest x1 72 us: scatter_all(): pl.pallas_call(functools.partial(scatter_kernel, dims, pieces, n), out_sh...]
    unnamed x20 -> x10, waiting for transfers between devices: 110 us -> 2.32 us
    all_gather x4 -> x0, waiting for transfers between devices: 87.6 us -> none  [the longest x1 53.2 us: on_device(): lax.all_gather(value_weight, ('seq', 'dp'), axis=0, tiled=True)]
    unnamed x2 -> x0, blocking collectives: 79.4 us -> none
    all_gather x1 -> x0, blocking collectives: 67 us -> none  [on_device(): lax.all_gather(router_weight, ('seq', 'dp'), axis=0, tiled=True)]
    reduce_scatter x1, waiting for transfers between devices: 54.2 us -> 12.1 us  [on_device(): lax.psum_scatter(up_local.astype(jnp.bfloat16), 'seq', scatter_dimension=...]
  transfers between devices with their start and end apart: 23 -> 14, of which waited for: 15 -> 6; matrix products, arithmetic and copies ran while one was open for 15% -> 28% of each run, Pallas kernels for 0% -> 8%
where the time goes in v1:
time: 921 us; the launch traced here: 915 us
  waiting for transfers between devices  274 us (30%)
  matrix products  246 us (27%)
  local copies, waits for them, and re-layouts  184 us (20%)
  Pallas kernels  132 us (14%)
  other arithmetic  42.8 us (5%)
  starting transfers between devices  19.8 us (2%)
  between operations  16 us (2%)
    pallas_call x1, Pallas kernels, scatter_all(): pl.pallas_call(functools.partial(scatter_kernel, dims, pieces, n), out_sh...  72 us
    pallas_call x1, Pallas kernels, gather_all(): pl.pallas_call(functools.partial(gather_kernel, dims, pieces, na), out_sh...  60.1 us
    all_to_all x1, waiting for transfers between devices, on_device(): lax.all_to_all(out_slots, 'dp', split_axis=0, concat_axis=0, tiled=True)  59.6 us
    reduce_scatter x1, waiting for transfers between devices, on_device(): lax.psum_scatter(down_local.astype(jnp.bfloat16), 'seq', scatter_dimensio...  53.9 us
    all_to_all x1, waiting for transfers between devices, on_device(): lax.all_to_all(result.reshape(experts, slot_count, model_width), 'dp', sp...  52.9 us
    all_to_all x1, waiting for transfers between devices, on_device(): lax.all_to_all(input_grad.reshape(experts, capacity, model_width), 'dp',...  46.9 us
    all_to_all x1, waiting for transfers between devices, on_device(): lax.all_to_all(outgoing, 'dp', split_axis=0, concat_axis=0, tiled=True)  45.9 us
    dot_general x1, matrix products, on_device(): jnp.einsum('slcd,ldf->slcf', inputs, gate_full, preferred_element_type=jn...  24.6 us
  transfers between devices with their start and end apart: 14, of which 6 were waited for; matrix products, arithmetic and copies ran while one was open for 28% of the time, Pallas kernels for 8%

profile of v1, /device:TPU:0, one launch (start us, length us, event | category | flops | bytes accessed | tf_op | source)
XLA Modules:
  0.0 915.4 jit_solution(10194445197610212179)
XLA Ops:
  11.5 60.1 %shard_map.316 = (bf16[2,2,4,2,32,1024]{5,4,3,2,1,0:T(8,128)(2,1)}, bf16[2,2,4,2,32,1024]{5,4,3,2,1,0:T(8,128)(2,1)}, bf16[2,2,4,2,32,1024]{5,4,3,2,1,0:T(8,128)...) custom-call(bf16[32,1024]{1,0:T(8,128)(2,1)} %refs_0_.1, bf16[32,1024]{1,0:T(8,128)(2,1)} %refs_1_.1, ...), custom_call_target="tpu_custom_call" | custom-call | tf_op jit(solution)/shard_map/pallas_call | solution.py:176
  93.9 4.9 copy.128
  116.3 5.9 fusion.21
  130.6 6.4 mul.343
  137.0 10.1 %fusion.164 = (f32[2,16,128]{2,1,0:T(8,128)S(1)}, f32[2,16,128,512]{3,2,1,0:T(8,128)S(1)}) fusion(f32[16,2,128,512]{3,0,2,1:T(8,128)} %fusion.21, bf16[2,512,16,64]{1,3,2,0:T(8,128)(2,1)} %bitcast.381, bf16[2,128,16,64]{3,2,1,0:T(8,128)(2,1)S(1)} %reshape.846, pred[2,512]{1,0:T(4,128)(4,1)S(1)} %iota_compare_fusion.15), kind=kOutput, calls=%fused_computation.308 | convolution fusion | flops 274722816 | bytes 19416064 | tf_op jit(solution)/shard_map/bqhd,bkhd->bhqk/dot_general | solution.py:50
  152.5 6.3 fusion.85
  164.2 4.5 scatter_custom_fusion.1
  168.8 5.1 gather_fusion
  174.0 4.3 scatter_custom_fusion
  181.4 5.1 gather_fusion.1
  186.5 4.5 select_select_fusion
  191.0 6.3 all-to-all-start.2
  197.9 59.6 %all-to-all-done.2 = bf16[8,160,1024]{2,1,0:T(8,128)(2,1)S(1)} async-done(((bf16[8,160,1024]{2,1,0:T(8,128)(2,1)}), bf16[8,160,1024]{2,1,0:T(8,128)(2,1)S(1)}, u32[]{:S(2)}, u32[]{:S(2)}) %all-to-all-start.2) | async-done | bytes 2621472 | tf_op jit(solution)/shard_map/all_to_all | solution.py:428
  257.5 4.8 all-to-all-start
  262.3 13.4 %fusion.43 = f32[8,160,2816]{2,1,0:T(8,128)} fusion(bf16[8,160,1024]{2,1,0:T(8,128)(2,1)S(1)} %all-to-all-done.2, bf16[1,1024,2816]{2,1,0:T(8,128)(2,1)} %all-gather.14.cloned.1.call-done), kind=kOutput, calls=%fused_computation.81 | convolution fusion | flops 7381975040 | bytes 22806528 | tf_op jit(solution)/shard_map/slcd,ldf->slcf/dot_general | solution.py:431
  275.7 45.9 %all-to-all-done = bf16[8,160,1024]{2,1,0:T(8,128)(2,1)} async-done(((bf16[8,160,1024]{2,1,0:T(8,128)(2,1)}), bf16[8,160,1024]{2,1,0:T(8,128)(2,1)}, u32[]{:S(2)}, u32[]{:S(2)}) %all-to-all-start) | async-done | bytes 2621472 | tf_op jit(solution)/shard_map/all_to_all | solution.py:374
  321.7 13.8 %fusion.49 = f32[8,160,2816]{2,1,0:T(8,128)} fusion(bf16[8,160,1024]{2,1,0:T(8,128)(2,1)} %all-to-all-done, bf16[1,1024,2816]{2,1,0:T(8,128)(2,1)} %all-gather.12.cloned.1.call-done), kind=kOutput, calls=%fused_computation.87 | convolution fusion | flops 7381975040 | bytes 22806528 | tf_op jit(solution)/shard_map/slcd,ldf->slcf/dot_general | solution.py:378
  335.5 24.6 %fusion.37 = (bf16[8,160,2816]{2,1,0:T(8,128)(2,1)S(1)}, bf16[8,1,160,2816]{3,2,0,1:T(8,128)(2,1)}, bf16[8,160,2816]{2,1,0:T(8,128)(2,1)}) fusion(f32[8,160,2816]{2,1,0:T(8,128)} %fusion.43, f32[8,160,2816]{2,1,0:T(8,128)} %fusion.49, bf16[8,160,1024]{2,1,0:T(8,128)(2,1)} %all-to-all-done, bf16[1,1024,2816]{2,1,0:T(8,128)(2,1)} %all-gather.10.cloned.1.call-done), kind=kOutput, calls=%fused_computation.75 | convolution fusion | flops 7475691520 | bytes 58851328 | tf_op jit(solution)/shard_map/slcd,ldf->slcf/dot_general | solution.py:377
  360.2 14.3 %fusion.40 = f32[8,160,1024]{2,1,0:T(8,128)} fusion(bf16[8,1,160,2816]{3,2,0,1:T(8,128)(2,1)} %get-tuple-element.228, bf16[1,1024,2816]{2,1,0:T(8,128)(2,1)S(1)} %copy-done.85), kind=kOutput, calls=%fused_computation.78 | convolution fusion | flops 7381975040 | bytes 18219008 | tf_op jit(solution)/shard_map/slcf,ldf->slcd/dot_general | solution.py:441
  374.5 10.9 %add_convert_fusion = bf16[8,160,1024]{2,1,0:T(8,128)(2,1)} fusion(f32[8,160,1024]{2,1,0:T(8,128)} %fusion.40, bf16[8,160,2816]{2,1,0:T(8,128)(2,1)S(1)} %get-tuple-element.227, bf16[1,1024,2816]{2,1,0:T(8,128)(2,1)S(1)} %copy-done.84), kind=kOutput, calls=%fused_computation.92 | convolution fusion | flops 7384596480 | bytes 20840448 | tf_op jit(solution)/shard_map/slcf,ldf->slcd/dot_general | solution.py:442
  385.4 3.6 all-to-all-start.3
  389.0 12.7 %fusion.79 = bf16[8,160,1024]{2,1,0:T(8,128)(2,1)} fusion(bf16[8,160,2816]{2,1,0:T(8,128)(2,1)} %get-tuple-element.229, bf16[1,1024,2816]{2,1,0:T(8,128)(2,1)} %all-gather.14.cloned.1.call-done), kind=kOutput, calls=%fused_computation.142 | convolution fusion | flops 7383285760 | bytes 15597568 | tf_op jit(solution)/shard_map/slcf,ldf->slcd/dot_general | solution.py:380
  401.7 46.9 %all-to-all-done.3 = bf16[8,160,1024]{2,1,0:T(8,128)(2,1)S(1)} async-done(((bf16[8,160,1024]{2,1,0:T(8,128)(2,1)}), bf16[8,160,1024]{2,1,0:T(8,128)(2,1)S(1)}, u32[]{:S(2)}, u32[]{:S(2)}) %all-to-all-start.3) | async-done | bytes 2621472 | tf_op jit(solution)/shard_map/all_to_all | solution.py:444
  448.7 4.4 all-to-all-start.1
  453.7 5.6 gather_fusion.3
  459.2 52.9 %all-to-all-done.1 = bf16[8,160,1024]{2,1,0:T(8,128)(2,1)} async-done(((bf16[8,160,1024]{2,1,0:T(8,128)(2,1)}), bf16[8,160,1024]{2,1,0:T(8,128)(2,1)}, u32[]{:S(2)}, u32[]{:S(2)}) %all-to-all-start.1) | async-done | bytes 2621472 | tf_op jit(solution)/shard_map/all_to_all | solution.py:383
  512.1 7.1 gather_fusion.2
  522.2 4.1 fusion.77
  526.3 5.8 reshape.779
  532.2 9.2 %fusion.154 = (f32[512,1,1024]{2,1,0:T(1,128)}, f32[512,1,1024]{2,1,0:T(1,128)}) fusion(f32[512,2,1024]{2,1,0:T(2,128)} %reshape.779), kind=kLoop, calls=%fused_computation.298 | loop fusion | bytes 8388608 | tf_op jit(solution)/shard_map/slice | solution.py:483
  542.0 5.3 multiply_reduce_fusion.2
  547.3 6.1 reshape.778
  553.4 7.2 fusion.155
  565.5 86.7 %while.16 = (s32[]{:T(128)}, bf16[2,128,1024]{2,1,0:T(8,128)(2,1)}, bf16[2,512,1024]{2,1,0:T(8,128)(2,1)}, bf16[2,512,1024]{2,1,0:T(8,128)(2,1)}, f32[2,16,32]{2...) while((s32[]{:T(128)}, bf16[2,128,1024]{2,1,0:T(8,128)(2,1)}, ...), condition=%wide.region_22.24_spmd, body=%wide.region_20.23_spmd.sunk | while | flops 820770816 | bytes 123792768 | solution.py:519
  570.4 5.3 copy.265
  582.3 4.5 multiply_reduce_fusion.9
  592.5 3.6 fusion.259
  613.5 5.3 copy.265
  625.4 4.5 multiply_reduce_fusion.9
  653.0 13.6 %fusion.42 = bf16[1,1024,2816]{2,1,0:T(8,128)(2,1)} fusion(bf16[8,160,1024]{2,1,0:T(8,128)(2,1)} %all-to-all-done, bf16[8,1,160,2816]{3,2,0,1:T(8,128)(2,1)} %get-tuple-element.228), kind=kOutput, calls=%fused_computation.80 | convolution fusion | flops 7384858624 | bytes 15597568 | tf_op jit(solution)/shard_map/slcd,slcf->ldf/dot_general | solution.py:453
  666.7 13.3 %fusion.56 = bf16[1,1024,2816]{2,1,0:T(8,128)(2,1)} fusion(bf16[8,160,1024]{2,1,0:T(8,128)(2,1)} %all-to-all-done, bf16[8,160,2816]{2,1,0:T(8,128)(2,1)} %copy-done.90), kind=kOutput, calls=%fused_computation.93 | convolution fusion | flops 7384858624 | bytes 15597568 | tf_op jit(solution)/shard_map/slcd,slcf->ldf/dot_general | solution.py:456
  681.7 12.8 %fusion.57 = bf16[1,1024,2816]{2,1,0:T(8,128)(2,1)} fusion(bf16[8,160,1024]{2,1,0:T(8,128)(2,1)S(1)} %copy-done.27, bf16[8,160,2816]{2,1,0:T(8,128)(2,1)} %get-tuple-element.229), kind=kOutput, calls=%fused_computation.94 | convolution fusion | flops 7384858624 | bytes 15597568 | tf_op jit(solution)/shard_map/slcd,slcf->ldf/dot_general | solution.py:459
  733.0 4.5 fusion.102
  737.6 7.2 fusion.64
  745.0 4.0 convolution_convert_fusion
  751.7 72.0 %shard_map.317 = (f32[32,1024]{1,0:T(8,128)S(1)}, f32[32,1024]{1,0:T(8,128)S(1)}, f32[32,1024]{1,0:T(8,128)S(1)}, f32[32,1024]{1,0:T(8,128)S(1)}, f32[8,128]{1,0:T(8,128)S(1)}) custom-call(bf16[2,2,4,2,32,1024]{5,4,3,2,1,0:T(8,128)(2,1)S(1)} %bitcast.366, bf16[2,2,4,2,32,1024]{5,4,3,2,1,0:T(8,128)(2,1)S(1)} %bitcast.365, ...), custom_call_target="tpu_custom_call" | custom-call | tf_op jit(solution)/shard_map/pallas_call | solution.py:249
  833.1 12.1 %reduce-scatter.12.cloned.1.call-done = bf16[1,256,2816]{2,1,0:T(8,128)(2,1)} async-done(((bf16[1,1024,2816]{2,1,0:T(8,128)(2,1)}), bf16[1,256,2816]{2,1,0:T(8,128)(2,1)}) %reduce-scatter.12.cloned.1.call-update) | async-done | bytes 1441808 | tf_op jit(solution)/shard_map/reduce_scatter | solution.py:466
  848.3 53.9 %reduce-scatter.14.cloned.1.call-done = bf16[1,256,2816]{2,1,0:T(8,128)(2,1)} async-done(((bf16[1,1024,2816]{2,1,0:T(8,128)(2,1)}), bf16[1,256,2816]{2,1,0:T(8,128)(2,1)}) %reduce-scatter.14.cloned.1.call-update) | async-done | bytes 1441808 | tf_op jit(solution)/shard_map/reduce_scatter | solution.py:469
  (419 shorter events, 200.4 us)
Async XLA Ops:
  7.2 129.8 %all-gather.8.cloned.1.call-start = ((), (), s32[]{:S(2)}) async-start(), calls=%async_computation.10 | async-start | bytes 2621440 | tf_op jit(solution)/shard_map/all_gather | solution.py:335
  9.3 74.6 %copy-start.76 = (f32[512]{0:T(512)}, f32[512]{0:T(512)S(1)}, u32[]{:S(2)}) copy-start(f32[512]{0:T(512)S(1)} %fusion.140) | copy-start | bytes 6148
  72.7 11.2 %copy-start.73 = (f32[1024]{0:T(1024)}, f32[1024]{0:T(1024)S(1)}, u32[]{:S(2)}) copy-start(f32[1024]{0:T(1024)S(1)} %reshape.776) | copy-start | bytes 12292
  77.1 75.4 %all-gather.6.cloned.1.call-start = ((), (), s32[]{:S(2)}) async-start(), calls=%async_computation.9 | async-start | bytes 2621440 | tf_op jit(solution)/shard_map/all_gather | solution.py:336
  81.9 180.4 %all-gather.14.cloned.1.call-start = ((), (), s32[]{:S(2)}) async-start(), calls=%async_computation.13 | async-start | bytes 7208960 | tf_op jit(solution)/shard_map/all_gather | solution.py:316
  82.6 239.0 %all-gather.12.cloned.1.call-start = ((), (), s32[]{:S(2)}) async-start(), calls=%async_computation.12 | async-start | bytes 7208960 | tf_op jit(solution)/shard_map/all_gather | solution.py:315
  83.3 9.1 copy-start.51
  83.4 80.4 %copy-start.59 = (s32[512,2]{0,1:T(2,128)}, s32[512,2]{0,1:T(2,128)S(1)}, u32[]{:S(2)}) copy-start(s32[512,2]{0,1:T(2,128)S(1)} %get-tuple-element.262) | copy-start | bytes 12292
  116.3 5.9 copy-start.83
  116.3 9.5 %copy-start.36 = (bf16[2,128,1024]{2,1,0:T(8,128)(2,1)S(1)}, bf16[2,128,1024]{2,1,0:T(8,128)(2,1)}, u32[]{:S(2)}) copy-start(bf16[2,128,1024]{2,1,0:T(8,128)(2,1)} %param.28) | copy-start | bytes 1572868
  122.2 14.8 %copy-start.49 = (pred[2,512]{1,0:T(4,128)(4,1)}, pred[2,512]{1,0:T(4,128)(4,1)S(1)}, u32[]{:S(2)}) copy-start(pred[2,512]{1,0:T(4,128)(4,1)S(1)} %iota_compare_fusion.15) | copy-start | bytes 3076
  122.3 39.6 %copy-start.55 = (f32[1024]{0:T(1024)}, f32[1024]{0:T(1024)S(1)}, u32[]{:S(2)}) copy-start(f32[1024]{0:T(1024)S(1)} %reshape.777) | copy-start | bytes 12292
  122.7 40.1 %copy-start.28 = (bf16[1024,8]{1,0:T(8,128)(2,1)}, bf16[1024,8]{1,0:T(8,128)(2,1)S(1)}, u32[]{:S(2)}) copy-start(bf16[1024,8]{1,0:T(8,128)(2,1)S(1)} %reshape.747) | copy-start | bytes 49156
  152.5 7.0 copy-start.40
  161.8 12.0 %copy-start.71 = (f32[512]{0:T(512)}, f32[512]{0:T(512)S(1)}, u32[]{:S(2)}) copy-start(f32[512]{0:T(512)S(1)} %get-tuple-element.273) | copy-start | bytes 6148
  162.7 11.1 %copy-start.3 = (bf16[512,1024]{1,0:T(8,128)(2,1)}, bf16[512,1024]{1,0:T(8,128)(2,1)S(1)}, u32[]{:S(2)}) copy-start(bf16[512,1024]{1,0:T(8,128)(2,1)S(1)} %multiply_convert_fusion.3) | copy-start | bytes 3145732
  163.8 10.1 %copy-start.61 = (f32[512,2]{0,1:T(2,128)}, f32[512,2]{0,1:T(2,128)S(1)}, u32[]{:S(2)}) copy-start(f32[512,2]{0,1:T(2,128)S(1)} %get-tuple-element.192) | copy-start | bytes 12292
  191.0 66.5 %all-to-all-start.2 = ((bf16[8,160,1024]{2,1,0:T(8,128)(2,1)}), bf16[8,160,1024]{2,1,0:T(8,128)(2,1)S(1)}, u32[]{:S(2)}, u32[]{:S(2)}) async-start(bf16[8,160,1024]{2,1,0:T(8,128)(2,1)} %get-tuple-element.267), calls=%async_computation.2 | async-start | bytes 5242880 | tf_op jit(solution)/shard_map/all_to_all | solution.py:428
  197.3 138.2 %all-gather.10.cloned.1.call-start = ((), (), s32[]{:S(2)}) async-start(), calls=%async_computation.11 | async-start | bytes 7208960 | tf_op jit(solution)/shard_map/all_gather | solution.py:314
  257.5 4.9 copy-start.26
  257.5 64.2 %all-to-all-start = ((bf16[8,160,1024]{2,1,0:T(8,128)(2,1)}), bf16[8,160,1024]{2,1,0:T(8,128)(2,1)}, u32[]{:S(2)}, u32[]{:S(2)}) async-start(bf16[8,160,1024]{2,1,0:T(8,128)(2,1)} %get-tuple-element.268), calls=%async_computation | async-start | bytes 5242880 | tf_op jit(solution)/shard_map/all_to_all | solution.py:374
  335.5 24.7 %copy-start.85 = (bf16[1,1024,2816]{2,1,0:T(8,128)(2,1)S(1)}, bf16[1,1024,2816]{2,1,0:T(8,128)(2,1)}, u32[]{:S(2)}) copy-start(bf16[1,1024,2816]{2,1,0:T(8,128)(2,1)} %all-gather.10.cloned.1.call-done) | copy-start | bytes 17301508
  360.2 14.3 %copy-start.90 = (bf16[8,160,2816]{2,1,0:T(8,128)(2,1)}, bf16[8,160,2816]{2,1,0:T(8,128)(2,1)S(1)}, u32[]{:S(2)}) copy-start(bf16[8,160,2816]{2,1,0:T(8,128)(2,1)S(1)} %get-tuple-element.227) | copy-start | bytes 21626884
  360.2 14.3 %copy-start.84 = (bf16[1,1024,2816]{2,1,0:T(8,128)(2,1)S(1)}, bf16[1,1024,2816]{2,1,0:T(8,128)(2,1)}, u32[]{:S(2)}) copy-start(bf16[1,1024,2816]{2,1,0:T(8,128)(2,1)} %all-gather.12.cloned.1.call-done) | copy-start | bytes 17301508
  385.4 63.3 %all-to-all-start.3 = ((bf16[8,160,1024]{2,1,0:T(8,128)(2,1)}), bf16[8,160,1024]{2,1,0:T(8,128)(2,1)S(1)}, u32[]{:S(2)}, u32[]{:S(2)}) async-start(bf16[8,160,1024]{2,1,0:T(8,128)(2,1)} %add_convert_fusion), calls=%async_computation.3 | async-start | bytes 5242880 | tf_op jit(solution)/shard_map/all_to_all | solution.py:444
  401.7 51.4 %copy-start.52 = (bf16[32,16]{1,0:T(8,128)(2,1)S(1)}, bf16[32,16]{1,0:T(8,128)(2,1)}, u32[]{:S(2)}) copy-start(bf16[32,16]{1,0:T(8,128)(2,1)} %copy-done.51) | copy-start | bytes 3076
  448.7 63.4 %all-to-all-start.1 = ((bf16[8,160,1024]{2,1,0:T(8,128)(2,1)}), bf16[8,160,1024]{2,1,0:T(8,128)(2,1)}, u32[]{:S(2)}, u32[]{:S(2)}) async-start(bf16[8,160,1024]{2,1,0:T(8,128)(2,1)} %fusion.79), calls=%async_computation.1 | async-start | bytes 5242880 | tf_op jit(solution)/shard_map/all_to_all | solution.py:383
  453.1 280.0 %reduce-scatter.6.cloned.1.call-start = ((), (), s32[]{:S(2)}) async-start(), calls=%async_computation.14 | async-start | bytes 2621440 | tf_op jit(solution)/shard_map/reduce_scatter | solution.py:533
  532.1 9.6 %copy-start.62 = (f32[512,2]{0,1:T(2,128)S(1)}, f32[512,2]{0,1:T(2,128)}, u32[]{:S(2)}) copy-start(f32[512,2]{0,1:T(2,128)} %copy-done.61) | copy-start | bytes 12292
  532.2 9.6 %copy-start.60 = (s32[512,2]{0,1:T(2,128)S(1)}, s32[512,2]{0,1:T(2,128)}, u32[]{:S(2)}) copy-start(s32[512,2]{0,1:T(2,128)} %copy-done.59) | copy-start | bytes 12292
  532.2 9.7 %copy-start.46 = (f32[512,8]{0,1:T(8,128)S(1)}, f32[512,8]{0,1:T(8,128)}, u32[]{:S(2)}) copy-start(f32[512,8]{0,1:T(8,128)} %copy-done.45) | copy-start | bytes 49156
  532.2 9.7 %copy-start.66 = (f32[512]{0:T(512)S(1)}, f32[512]{0:T(512)}, u32[]{:S(2)}) copy-start(f32[512]{0:T(512)} %copy-done.65) | copy-start | bytes 6148
  532.2 9.8 %copy-start.11 = (f32[512,1024]{1,0:T(8,128)S(1)}, f32[512,1024]{1,0:T(8,128)}, u32[]{:S(2)}) copy-start(f32[512,1024]{1,0:T(8,128)} %copy-done.10) | copy-start | bytes 6291460
  532.2 9.8 %copy-start.29 = (bf16[1024,8]{1,0:T(8,128)(2,1)S(1)}, bf16[1024,8]{1,0:T(8,128)(2,1)}, u32[]{:S(2)}) copy-start(bf16[1024,8]{1,0:T(8,128)(2,1)} %copy-done.28) | copy-start | bytes 49156
  532.2 9.8 %copy-start.56 = (f32[1024]{0:T(1024)S(1)}, f32[1024]{0:T(1024)}, u32[]{:S(2)}) copy-start(f32[1024]{0:T(1024)} %copy-done.55) | copy-start | bytes 12292
  532.2 9.8 %copy-start.68 = (f32[512]{0:T(512)S(1)}, f32[512]{0:T(512)}, u32[]{:S(2)}) copy-start(f32[512]{0:T(512)} %copy-done.67) | copy-start | bytes 6148
  541.9 5.3 copy-start.53
  542.0 5.3 copy-start.72
  553.3 7.2 copy-start.17
  553.3 7.2 copy-start.37
  553.4 7.2 copy-start.38
  582.3 4.7 copy-start.1
  652.2 85.3 %reduce-scatter.8.cloned.1.call-start = ((), (), s32[]{:S(2)}) async-start(), calls=%async_computation.15 | async-start | bytes 2621440 | tf_op jit(solution)/shard_map/reduce_scatter | solution.py:536
  653.0 177.0 %reduce-scatter.10.cloned.1.call-start = ((), (), s32[]{:S(2)}) async-start(), calls=%async_computation.16 | async-start | bytes 7208960 | tf_op jit(solution)/shard_map/reduce_scatter | solution.py:463
  666.6 178.5 %reduce-scatter.12.cloned.1.call-start = ((), (), s32[]{:S(2)}) async-start(), calls=%async_computation.17 | async-start | bytes 7208960 | tf_op jit(solution)/shard_map/reduce_scatter | solution.py:466
  680.0 222.3 %reduce-scatter.14.cloned.1.call-start = ((), (), s32[]{:S(2)}) async-start(), calls=%async_computation.18 | async-start | bytes 7208960 | tf_op jit(solution)/shard_map/reduce_scatter | solution.py:469
  712.3 5.6 copy-start.24
  751.7 73.9 %copy-start.70 = (f32[512]{0:T(512)S(1)}, f32[512]{0:T(512)}, u32[]{:S(2)}) copy-start(f32[512]{0:T(512)} %copy-done.69) | copy-start | bytes 6148
  (64 other events, 134.0 us)
Sparse Core Ops, SparseCore 0:
  77.2 23.3 all-gather.7
  102.7 22.8 all-gather.5
  127.2 43.3 all-gather.13
  172.0 43.3 all-gather.11
  216.9 43.3 all-gather.9
  652.3 29.5 reduce-scatter.5
  684.6 31.3 reduce-scatter.7
  718.6 64.3 reduce-scatter.9
  785.7 59.4 reduce-scatter.11
  847.6 54.6 reduce-scatter.13

commit v2 on v1

--- a/solution.py
+++ b/solution.py
@@ -14,19 +14,8 @@
 BUCKETS = 32
 
 
-far_edges = (12, 16, 23, 32, 46, 64, 91)
 epsilon = 1e-06
 masked = -1e30
-
-
-def bucket_of(query_pos, key_pos):
-    offset = key_pos[..., None, :] - query_pos[..., :, None]
-    distance = jnp.abs(offset)
-    beyond = jnp.zeros_like(distance)
-    for border in far_edges:
-        beyond = beyond + (distance >= border).astype(jnp.int32)
-    inner = jnp.where(distance < 8, distance, 8 + beyond)
-    return inner + jnp.where(offset > 0, BUCKETS // 2, 0)
 
 
 def rms_norm(hidden, gain):
@@ -42,72 +31,6 @@
     probs = jax.nn.softmax(logits, axis=-1)
     chosen = jnp.sum(choose * probs[:, None, :], axis=-1)
     return chosen / jnp.sum(chosen, axis=-1, keepdims=True)
-
-
-def score_block(queries, key_rows, query_pos, key_pos, key_ok, bias_table):
-    batch_size, rows, model_width = queries.shape
-    columns = key_rows.shape[1]
-    scores = jnp.einsum(
-        "bqhd,bkhd->bhqk",
-        queries.reshape(batch_size, rows, HEADS, HEAD),
-        key_rows.reshape(batch_size, columns, HEADS, HEAD),
-        preferred_element_type=jnp.float32,
-    )
-    onehot = (
-        bucket_of(query_pos, key_pos)[..., None] == jnp.arange(BUCKETS, dtype=jnp.int32)
-    ).astype(jnp.bfloat16)
-    rel_bias = jnp.einsum("bqkn,hn->bhqk", onehot, bias_table, preferred_element_type=jnp.float32)
-    return (jnp.where(key_ok[:, None, None, :], scores + rel_bias, masked), onehot)
-
-
-def attention_forward(queries, key_rows, value_rows, query_pos, key_pos, key_ok, bias_table):
-    scores, onehot = score_block(queries, key_rows, query_pos, key_pos, key_ok, bias_table)
-    batch_size, rows, model_width = queries.shape
-    columns = key_rows.shape[1]
-    row_peak = jnp.max(scores, axis=-1, keepdims=True)
-    lifted = jnp.exp(scores - row_peak)
-    row_total = jnp.sum(lifted, axis=-1, keepdims=True)
-    probs = lifted / row_total
-    mixed = jnp.einsum(
-        "bhqk,bkhd->bqhd",
-        probs.astype(jnp.bfloat16),
-        value_rows.reshape(batch_size, columns, HEADS, HEAD),
-        preferred_element_type=jnp.float32,
-    )
-    return (
-        mixed.astype(jnp.bfloat16).reshape(batch_size, rows, model_width),
-        (row_peak + jnp.log(row_total))[..., 0],
-    )
-
-
-def attention_backward(
-    queries, key_rows, value_rows, mixed_grad, log_total, query_pos, key_pos, key_ok, bias_table
-):
-    scores, onehot = score_block(queries, key_rows, query_pos, key_pos, key_ok, bias_table)
-    batch_size, rows, model_width = queries.shape
-    columns = key_rows.shape[1]
-    probs = jnp.exp(scores - log_total[..., None])
-    grad_four = mixed_grad.reshape(batch_size, rows, HEADS, HEAD)
-    value_four = value_rows.reshape(batch_size, columns, HEADS, HEAD)
-    query_four = queries.reshape(batch_size, rows, HEADS, HEAD)
-    key_four = key_rows.reshape(batch_size, columns, HEADS, HEAD)
-    prob_grad = jnp.einsum(
-        "bqhd,bkhd->bhqk", grad_four, value_four, preferred_element_type=jnp.float32
-    )
-    score_grad = (probs * (prob_grad - jnp.sum(probs * prob_grad, axis=-1, keepdims=True))).astype(
-        jnp.bfloat16
-    )
-    query_part = jnp.einsum(
-        "bhqk,bkhd->bqhd", score_grad, key_four, preferred_element_type=jnp.float32
-    ).reshape(batch_size, rows, model_width)
-    key_part = jnp.einsum(
-        "bhqk,bqhd->bkhd", score_grad, query_four, preferred_element_type=jnp.float32
-    ).reshape(batch_size, columns, model_width)
-    value_part = jnp.einsum(
-        "bhqk,bqhd->bkhd", probs.astype(jnp.bfloat16), grad_four, preferred_element_type=jnp.float32
-    ).reshape(batch_size, columns, model_width)
-    table_part = jnp.einsum("bhqk,bqkn->hn", score_grad, onehot, preferred_element_type=jnp.float32)
-    return (query_part, key_part, value_part, table_part)
 
 
 def gather_kernel(dims, pieces, na, *refs):
@@ -253,6 +176,201 @@
         compiler_params=pltpu.CompilerParams(collective_id=cid, has_side_effects=True, vmem_limit_bytes=48*2**20))(*arrays)
 
 
+EDGES = (-90, -63, -45, -31, -22, -15, -11, -7, -6, -5, -4, -3, -2, -1, 0, 1, 2, 3, 4, 5, 6, 7, 8, 12, 16, 23, 32, 46, 64, 91)
+ORDER = (15, 14, 13, 12, 11, 10, 9, 8, 7, 6, 5, 4, 3, 2, 1, 0, 17, 18, 19, 20, 21, 22, 23, 24, 25, 26, 27, 28, 29, 30, 31)
+FAR = (12, 16, 23, 32, 46, 64, 91)
+def fill_buckets(out, q_col, k_row, length, base):
+    r = k_row - q_col
+    n = jnp.abs(r)
+    far = jnp.full(r.shape, 8, jnp.int32)
+    for e in FAR:
+        far += (n >= e).astype(jnp.int32)
+    b = jnp.where(n < 8, n, far) + jnp.where(r > 0, 16, 0)
+    j = lax.broadcasted_iota(jnp.int32, r.shape, 1) + base
+    out[...] = jnp.where(j < length, b, 32)
+def dot(a, b, ca, cb):
+    return lax.dot_general(a, b, (((ca,), (cb,)), ((), ())), preferred_element_type=jnp.float32)
+def probs_of(qs, kk, tabs, bucket_ref, blocks):
+    s = dot(qs, kk, 1, 1)
+    t = [jnp.broadcast_to(tab, (128, 128)) for tab in tabs]
+    bias = [jnp.concatenate([jnp.take_along_axis(x, bucket_ref[c], axis=1) for x in t], axis=0) for c in range(blocks)]
+    s = s + (jnp.concatenate(bias, axis=1) if blocks > 1 else bias[0])
+    p = jnp.exp(s - jnp.max(s, axis=1, keepdims=True))
+    return p * (1.0 / jnp.sum(p, axis=1, keepdims=True))
+def stack_heads(rows, first):
+    return jnp.concatenate([jnp.where(first, rows, 0), jnp.where(first, 0, rows)], axis=0)
+def attn_setup(nl, ns, blocks, ll, sl, lcol, lrow, scol, srow, lb, sb):
+    me = lax.axis_index("seq")
+    for b in range(nl):
+        for c in range(blocks):
+            fill_buckets(lb.at[b, c], lcol[b, me], lrow[b, c], ll[b], c * 128)
+    for b in range(ns):
+        fill_buckets(sb.at[b, 0], scol[b, 0], srow[b, 0], sl[b], 0)
+def attn_fwd_kernel(nl, ns, blocks, ll, sl, q, k, v, kl, vl, tab, lcol, lrow, scol, srow, mixed, lb, sb):
+    attn_setup(nl, ns, blocks, ll, sl, lcol, lrow, scol, srow, lb, sb)
+    first = lax.broadcasted_iota(jnp.int32, (128, 128), 1) < 64
+    @pl.loop(0, 8)
+    def _(hp):
+        cols = pl.ds(pl.multiple_of(hp * 128, 128), 128)
+        for b in range(nl + ns):
+            rows = pl.ds(b * 128, 128)
+            n = blocks if b < nl else 1
+            if b < nl:
+                kk = kl[:, b, :, cols].reshape(n * 128, 128); vv = vl[:, b, :, cols].reshape(n * 128, 128)
+            else:
+                kk = k[rows, cols]; vv = v[rows, cols]
+            qq = q[rows, cols]
+            p = probs_of(stack_heads(qq, first), kk, (tab[2 * hp], tab[2 * hp + 1]), lb.at[b] if b < nl else sb.at[b - nl], n)
+            out = dot(p.astype(jnp.bfloat16), vv, 1, 0)
+            mixed[rows, cols] = jnp.where(first, out[:128], out[128:]).astype(jnp.bfloat16)
+def attn_bwd_kernel(nl, ns, blocks, ll, sl, q, k, v, kl, vl, mg, tab, lcol, lrow, scol, srow, dq, dk, dv, dkl, dvl, seg, lb, sb, li, si):
+    attn_setup(nl, ns, blocks, ll, sl, lcol, lrow, scol, srow, lb, sb)
+    me = lax.axis_index("seq")
+    lane = lax.broadcasted_iota(jnp.int32, (128, 128), 1)
+    edge = jnp.full((128, 128), 4096, jnp.int32)
+    for i, e in enumerate(EDGES):
+        edge = jnp.where(lane == i, e, edge)
+    edge = jnp.where(lane > len(EDGES), -4096, edge)
+    def places(out, q_col, k_col, k_first):
+        t = lax.broadcasted_iota(jnp.int32, (128, 256), 1) + k_first
+        below = jnp.sum((k_col < t).astype(jnp.int32), axis=0, keepdims=True)
+        at = jnp.clip(q_col + edge - k_first, 0, 255)
+        lo = jnp.take_along_axis(jnp.broadcast_to(below[:, :128], (128, 128)), at & 127, axis=1)
+        hi = jnp.take_along_axis(jnp.broadcast_to(below[:, 128:], (128, 128)), at & 127, axis=1)
+        out[...] = jnp.where(at < 128, lo, hi) - 1
+    for b in range(nl):
+        for c in range(blocks):
+            places(li.at[b, c], lcol[b, me], lcol[b, c], lrow[b, c, 0, 0])
+    for b in range(ns):
+        places(si.at[b, 0], scol[b, 0], scol[b, 0], srow[b, 0, 0, 0])
+    seg[...] = jnp.zeros_like(seg)
+    first = lane < 64
+    row = lax.broadcasted_iota(jnp.int32, (128, 128), 0)
+    tri = jnp.where(row <= lane, 1.0, 0.0).astype(jnp.bfloat16)
+    @pl.loop(0, 8)
+    def _(hp):
+        cols = pl.ds(pl.multiple_of(hp * 128, 128), 128)
+        for b in range(nl + ns):
+            rows = pl.ds(b * 128, 128)
+            n = blocks if b < nl else 1
+            if b < nl:
+                kk = kl[:, b, :, cols].reshape(n * 128, 128); vv = vl[:, b, :, cols].reshape(n * 128, 128)
+            else:
+                kk = k[rows, cols]; vv = v[rows, cols]
+            qq = q[rows, cols]; gg = mg[rows, cols]
+            idx = li.at[b] if b < nl else si.at[b - nl]
+            qs = stack_heads(qq, first); gs = stack_heads(gg, first)
+            p = probs_of(qs, kk, (tab[2 * hp], tab[2 * hp + 1]), lb.at[b] if b < nl else sb.at[b - nl], n)
+            dp = dot(gs, vv, 1, 1)
+            ds = (p * (dp - jnp.sum(p * dp, axis=1, keepdims=True))).astype(jnp.bfloat16)
+            dqs = dot(ds, kk, 1, 0)
+            dkt = dot(qs, ds, 0, 0)
+            dvt = dot(gs, p.astype(jnp.bfloat16), 0, 0)
+            sums = [0, 0]
+            for c in range(n):
+                pre = dot(ds[:, c * 128:(c + 1) * 128], tri, 1, 0)
+                at = idx[c]
+                for e in range(2):
+                    sums[e] += jnp.where(at >= 0, jnp.take_along_axis(pre[e * 128:(e + 1) * 128], jnp.maximum(at, 0), axis=1), 0.0)
+            for e in range(2):
+                seg[2 * hp + e] += jnp.sum(sums[e], axis=0, keepdims=True)
+            dq[rows, cols] = jnp.where(first, dqs[:128], dqs[128:]).astype(jnp.bfloat16)
+            dkt = dkt.T.astype(jnp.bfloat16); dvt = dvt.T.astype(jnp.bfloat16)
+            if b < nl:
+                dkl[:, b, :, cols] = dkt.reshape(n, 128, 128); dvl[:, b, :, cols] = dvt.reshape(n, 128, 128)
+            else:
+                dk[pl.ds((b - nl) * 128, 128), cols] = dkt; dv[pl.ds((b - nl) * 128, 128), cols] = dvt
+def attention(backward, nl, ns, blocks, arrays, tokens, width):
+    sm, vm = pl.BlockSpec(memory_space=pltpu.SMEM), pl.BlockSpec(memory_space=pltpu.VMEM)
+    bf = jnp.bfloat16
+    rows = jax.ShapeDtypeStruct((tokens, width), bf)
+    buckets = [pltpu.VMEM((nl, blocks, 128, 128), jnp.int32), pltpu.VMEM((ns, 1, 128, 128), jnp.int32)]
+    if backward:
+        short = jax.ShapeDtypeStruct((ns * 128, width), bf)
+        long = jax.ShapeDtypeStruct((blocks, nl, 128, width), bf)
+        outs = [rows, short, short, long, long, jax.ShapeDtypeStruct((16, 1, 128), jnp.float32)]
+        body = functools.partial(attn_bwd_kernel, nl, ns, blocks); scr = buckets * 2
+    else:
+        outs = [rows]; body = functools.partial(attn_fwd_kernel, nl, ns, blocks); scr = buckets
+    return pl.pallas_call(body, out_shape=outs, in_specs=[sm, sm] + [vm] * (len(arrays) - 2), out_specs=[vm] * len(outs),
+        scratch_shapes=scr, compiler_params=pltpu.CompilerParams(vmem_limit_bytes=56 * 2**20))(*arrays)
+
+
+def seq_places(C):
+    s = lax.axis_index("seq"); g = lax.axis_index("dp")
+    x, c = s // C, lax.rem(s, C)
+    return s, x, c, ((1 - x) * C + c, g), (x * C + 1 - c, g)
+def greet(devs):
+    bar = pltpu.get_barrier_semaphore()
+    for d in devs:
+        pl.semaphore_signal(bar, inc=1, device_id=d, device_id_type=MESH)
+    pl.semaphore_wait(bar, len(devs))
+def remote(src, dst, ss, rs, dev):
+    cp = pltpu.make_async_remote_copy(src_ref=src, dst_ref=dst, send_sem=ss, recv_sem=rs, device_id=dev, device_id_type=MESH)
+    cp.start()
+    return cp
+def seq_gather_kernel(n, items, rows, *refs):
+    ins, outs = refs[:n], refs[n:2 * n]
+    lsem, ss, rs = refs[2 * n:]
+    s, x, c, xdev, cdev = seq_places(2)
+    far = (1 - x) * 2 + c
+    greet([xdev, cdev])
+    local, a, b = [], [], []
+    pieces = [(m, i) for m in range(n) for i in range(items)]
+    for k, (m, i) in enumerate(pieces):
+        src = ins[m].at[pl.ds(i * rows, rows)]
+        a.append(remote(src, outs[m].at[s, i], ss.at[k, 0], rs.at[k, 0], xdev))
+        b.append(remote(src, outs[m].at[s, i], ss.at[k, 1], rs.at[k, 1], cdev))
+        cp = pltpu.make_async_copy(src, outs[m].at[s, i], lsem.at[k]); cp.start(); local.append(cp)
+    f = []
+    for k, (m, i) in enumerate(pieces):
+        a[k].wait_recv()
+        f.append(remote(outs[m].at[far, i], outs[m].at[far, i], ss.at[k, 2], rs.at[k, 2], cdev))
+    for k in range(len(pieces)):
+        local[k].wait(); a[k].wait_send(); b[k].wait(); f[k].wait()
+def seq_gather(arrays, items, rows, seq, cid):
+    n = len(arrays); q = n * items
+    sem = pltpu.SemaphoreType.DMA
+    any_ = pl.BlockSpec(memory_space=pltpu.VMEM)
+    return pl.pallas_call(functools.partial(seq_gather_kernel, n, items, rows),
+        out_shape=[jax.ShapeDtypeStruct((seq, items, rows, a.shape[-1]), a.dtype) for a in arrays],
+        in_specs=[any_] * n, out_specs=[any_] * n,
+        scratch_shapes=[sem((q,)), sem((q, 3)), sem((q, 3))],
+        compiler_params=pltpu.CompilerParams(collective_id=cid, has_side_effects=True, vmem_limit_bytes=48*2**20))(*arrays)
+def seq_sum_kernel(n, items, *refs):
+    ins, outs = refs[:n], refs[n:2 * n]
+    cb, a1, b1, ss, rs = refs[2 * n:]
+    s, x, c, xdev, cdev = seq_places(2)
+    greet([xdev, cdev])
+    pieces = [(m, i) for m in range(n) for i in range(items)]
+    first = [[None, None] for _ in pieces]
+    second = []
+    f32 = jnp.float32
+    for far in range(2):
+        xx = 1 - x if far == 0 else x
+        for k, (m, i) in enumerate(pieces):
+            first[k][far] = remote(ins[m].at[xx * 2 + 1 - c, i], cb.at[k, far], ss.at[k, far], rs.at[k, far], cdev)
+    for k, (m, i) in enumerate(pieces):
+        first[k][0].wait_recv()
+        a1[k] = (ins[m][(1 - x) * 2 + c, i].astype(f32) + cb[k, 0].astype(f32)).astype(a1.dtype)
+        second.append(remote(a1.at[k], b1.at[k], ss.at[k, 2], rs.at[k, 2], xdev))
+    for k, (m, i) in enumerate(pieces):
+        first[k][1].wait_recv()
+        second[k].wait_recv()
+        outs[m][i] = (ins[m][s, i].astype(f32) + cb[k, 1].astype(f32) + b1[k].astype(f32)).astype(outs[m].dtype)
+    for k in range(len(pieces)):
+        first[k][0].wait_send(); first[k][1].wait_send(); second[k].wait_send()
+def seq_sum(arrays, cid):
+    n = len(arrays); seq, items, rows, w = arrays[0].shape; q = n * items
+    sem = pltpu.SemaphoreType.DMA; dt = arrays[0].dtype
+    vm = pl.BlockSpec(memory_space=pltpu.VMEM)
+    return pl.pallas_call(functools.partial(seq_sum_kernel, n, items),
+        out_shape=[jax.ShapeDtypeStruct((items, rows, w), dt) for a in arrays],
+        in_specs=[vm] * n, out_specs=[vm] * n,
+        scratch_shapes=[pltpu.VMEM((q, 2, rows, w), dt), pltpu.VMEM((q, rows, w), dt), pltpu.VMEM((q, rows, w), dt), sem((q, 3)), sem((q, 3))],
+        compiler_params=pltpu.CompilerParams(collective_id=cid, has_side_effects=True, vmem_limit_bytes=48 * 2**20))(*arrays)
+
+
 def on_device(
     long_tokens,
     short_tokens,
@@ -324,29 +442,20 @@
         jnp.dot(normed, matrix, preferred_element_type=jnp.float32).astype(jnp.bfloat16)
         for matrix in attn_set[:3]
     ]
-    long_q, long_k, long_v = [
-        block[:long_rows].reshape(long_items, quarter, model_width) for block in projected
-    ]
-    short_q, short_k, short_v = [
-        block[long_rows:].reshape(short_items, short_len, model_width) for block in projected
-    ]
-    bias_table = attn_set[6].reshape(HEADS, BUCKETS)
-    long_keys, long_values = (
-        lax.all_gather(long_k, "seq", axis=1, tiled=True),
-        lax.all_gather(long_v, "seq", axis=1, tiled=True),
-    )
-    key_span = long_keys.shape[1]
-    query_pos = lax.dynamic_slice_in_dim(long_positions, seq_index * quarter, quarter, 1)
-    long_ok = jnp.arange(key_span, dtype=jnp.int32)[None, :] < long_lengths[:, None]
-    short_ok = jnp.arange(short_len, dtype=jnp.int32)[None, :] < short_lengths[:, None]
-    long_mix, long_lse = attention_forward(
-        long_q, long_keys, long_values, query_pos, long_positions, long_ok, bias_table
-    )
-    short_mix, short_lse = attention_forward(
-        short_q, short_k, short_v, short_positions, short_positions, short_ok, bias_table
-    )
-    mixed_all = jnp.concatenate(
-        [long_mix.reshape(long_rows, model_width), short_mix.reshape(-1, model_width)], 0
+    queries, keys, values = projected
+    long_keys, long_values = seq_gather((keys, values), long_items, quarter, seq_size, 2)
+    table = attn_set[6].reshape(HEADS, 1, BUCKETS).astype(jnp.float32)
+    table = jnp.pad(table, ((0, 0), (0, 0), (0, 128 - BUCKETS)), constant_values=masked)
+    attn_args = (
+        table,
+        long_positions.reshape(long_items, seq_size, quarter, 1),
+        long_positions.reshape(long_items, seq_size, 1, quarter),
+        short_positions.reshape(short_items, 1, short_len, 1),
+        short_positions.reshape(short_items, 1, 1, short_len),
+    )
+    lead_args = (long_lengths, short_lengths, queries, keys, values, long_keys, long_values)
+    (mixed_all,) = attention(
+        False, long_items, short_items, seq_size, lead_args + attn_args, tokens, model_width
     )
     resid_mid = resid_in + jnp.dot(mixed_all, attn_set[3], preferred_element_type=jnp.float32)
     gain_second = attn_set[5].astype(jnp.float32)
@@ -497,68 +606,27 @@
     mix_grad = jnp.einsum(
         "te,de->td", branch_grad, attn_back[3], preferred_element_type=jnp.float32
     ).astype(jnp.bfloat16)
-    long_mix_grad = mix_grad[:long_rows].reshape(long_items, quarter, model_width)
-    short_mix_grad = mix_grad[long_rows:].reshape(short_items, short_len, model_width)
-    table_back = attn_back[6].reshape(HEADS, BUCKETS)
-
-    def long_item(pack):
-        single = [member_item[None] for member_item in pack]
-        parts = attention_backward(
-            single[0],
-            single[1],
-            single[2],
-            single[3],
-            single[4],
-            single[5],
-            single[6],
-            single[7],
-            table_back,
-        )
-        return (parts[0][0], parts[1][0], parts[2][0], parts[3])
-
-    long_parts = lax.map(
-        long_item,
-        (
-            long_q,
-            long_keys,
-            long_values,
-            long_mix_grad,
-            long_lse,
-            query_pos,
-            long_positions,
-            long_ok,
-        ),
-    )
-    long_key_grad, long_value_grad = (
-        lax.psum_scatter(
-            long_parts[1].astype(jnp.bfloat16), "seq", scatter_dimension=1, tiled=True
-        ).astype(jnp.float32),
-        lax.psum_scatter(
-            long_parts[2].astype(jnp.bfloat16), "seq", scatter_dimension=1, tiled=True
-        ).astype(jnp.float32),
-    )
-    short_parts = attention_backward(
-        short_q,
-        short_k,
-        short_v,
-        short_mix_grad,
-        short_lse,
-        short_positions,
-        short_positions,
-        short_ok,
-        table_back,
-    )
-    query_act = jnp.concatenate(
-        [long_parts[0].reshape(long_rows, model_width), short_parts[0].reshape(-1, model_width)], 0
-    ).astype(jnp.bfloat16)
-    key_act = jnp.concatenate(
-        [long_key_grad.reshape(long_rows, model_width), short_parts[1].reshape(-1, model_width)], 0
-    ).astype(jnp.bfloat16)
-    value_act = jnp.concatenate(
-        [long_value_grad.reshape(long_rows, model_width), short_parts[2].reshape(-1, model_width)],
-        0,
-    ).astype(jnp.bfloat16)
-    table_local = (jnp.sum(long_parts[3], axis=0) + short_parts[3]).reshape(-1)
+    query_act, short_key, short_value, long_key, long_value, table_sums = attention(
+        True,
+        long_items,
+        short_items,
+        seq_size,
+        lead_args + (mix_grad,) + attn_args,
+        tokens,
+        model_width,
+    )
+    long_key, long_value = seq_sum((long_key, long_value), 3)
+    key_act = jnp.concatenate([long_key.reshape(long_rows, model_width), short_key], 0)
+    value_act = jnp.concatenate([long_value.reshape(long_rows, model_width), short_value], 0)
+    upto = table_sums.reshape(HEADS, 128)[:, : len(ORDER)]
+    within = upto - jnp.pad(upto[:, :-1], ((0, 0), (1, 0)))
+    table_local = jnp.stack(
+        [
+            within[:, ORDER.index(n)] if n in ORDER else jnp.zeros(HEADS, jnp.float32)
+            for n in range(BUCKETS)
+        ],
+        1,
+    ).reshape(-1)
     normed_grad = (
         jnp.einsum("te,de->td", query_act, attn_back[0], preferred_element_type=jnp.float32)
         + jnp.einsum("te,de->td", key_act, attn_back[1], preferred_element_type=jnp.float32)

time: 921 us -> 807 us (0.88)
  Pallas kernels: 132 us -> 287 us
  matrix products: 246 us -> 154 us
  local copies, waits for them, and re-layouts: 184 us -> 93.5 us
  waiting for transfers between devices: 274 us -> 193 us
    pallas_call x0 -> x4, Pallas kernels: none -> 143 us  [the longest x2 67.7 us: attention(): pl.pallas_call(body, out_shape=outs, in_specs=[sm, sm] + [vm] * (len(arra...]
    dot_general x25 -> x0, matrix products: 73.5 us -> none  [the longest x4 21 us: score_block(): jnp.einsum('bqhd,bkhd->bhqk', queries.reshape(batch_size, rows, HEADS, HE...]
    reduce_scatter x1, waiting for transfers between devices: 53.9 us -> 0.01 us  [on_device(): lax.psum_scatter(down_local.astype(jnp.bfloat16), 'seq', scatter_dimensio...]
    another operation x17 -> x2, local copies, waits for them, and re-layouts: 29.7 us -> 0.11 us  [the longest x1 0.11 us: on_device(): jnp.stack([within[:, ORDER.index(n)] if n in ORDER else jnp.zeros(HEADS,...]
    pallas_call x1, Pallas kernels: 60.1 us -> 81.8 us  [gather_all(): pl.pallas_call(functools.partial(gather_kernel, dims, pieces, na), out_sh...]
    dynamic_update_slice x10 -> x0, local copies, waits for them, and re-layouts: 17.2 us -> none  [on_device(): lax.map(long_item, (long_q, long_keys, long_values, long_mix_grad, long_l...]
    all_to_all x1, waiting for transfers between devices: 52.9 us -> 39.5 us  [on_device(): lax.all_to_all(result.reshape(experts, slot_count, model_width), 'dp', sp...]
    dot_general x3 -> x0, local copies, waits for them, and re-layouts: 13 us -> none  [score_block(): jnp.einsum('bqkn,hn->bhqk', onehot, bias_table, preferred_element_type=jn...]
  transfers between devices with their start and end apart: 14 -> 10, of which waited for: 6 -> 4; matrix products, arithmetic and copies ran while one was open for 28% -> 29% of each run, Pallas kernels for 8% -> 36%
where the time goes in v2:
time: 807 us; the launch traced here: 797 us
  Pallas kernels  287 us (36%)
  waiting for transfers between devices  193 us (24%)
  matrix products  154 us (19%)
  local copies, waits for them, and re-layouts  93.5 us (12%)
  other arithmetic  35 us (4%)
  starting transfers between devices  19.1 us (2%)
  between operations  15.8 us (2%)
    pallas_call x1, Pallas kernels, gather_all(): pl.pallas_call(functools.partial(gather_kernel, dims, pieces, na), out_sh...  81.8 us
    pallas_call x2, Pallas kernels, attention(): pl.pallas_call(body, out_shape=outs, in_specs=[sm, sm] + [vm] * (len(arra...  67.7 us
    pallas_call x1, Pallas kernels, scatter_all(): pl.pallas_call(functools.partial(scatter_kernel, dims, pieces, n), out_sh...  62.1 us
    all_to_all x1, waiting for transfers between devices, on_device(): lax.all_to_all(out_slots, 'dp', split_axis=0, concat_axis=0, tiled=True)  59.3 us
    pallas_call x1, Pallas kernels, seq_gather(): pl.pallas_call(functools.partial(seq_gather_kernel, n, items, rows), out_...  49.2 us
    all_to_all x1, waiting for transfers between devices, on_device(): lax.all_to_all(input_grad.reshape(experts, capacity, model_width), 'dp',...  46.6 us
    all_to_all x1, waiting for transfers between devices, on_device(): lax.all_to_all(outgoing, 'dp', split_axis=0, concat_axis=0, tiled=True)  45.3 us
    all_to_all x1, waiting for transfers between devices, on_device(): lax.all_to_all(result.reshape(experts, slot_count, model_width), 'dp', sp...  39.5 us
  transfers between devices with their start and end apart: 10, of which 4 were waited for; matrix products, arithmetic and copies ran while one was open for 29% of the time, Pallas kernels for 36%

profile of v2, /device:TPU:0, one launch (start us, length us, event | category | flops | bytes accessed | tf_op | source)
XLA Modules:
  0.0 797.0 jit_solution(4648203482693217740)
XLA Ops:
  11.4 81.8 %shard_map.316 = (bf16[2,2,4,2,32,1024]{5,4,3,2,1,0:T(8,128)(2,1)}, bf16[2,2,4,2,32,1024]{5,4,3,2,1,0:T(8,128)(2,1)}, bf16[2,2,4,2,32,1024]{5,4,3,2,1,0:T(8,128)...) custom-call(bf16[32,1024]{1,0:T(8,128)(2,1)} %refs_0_.1, bf16[32,1024]{1,0:T(8,128)(2,1)} %refs_1_.1, ...), custom_call_target="tpu_custom_call" | custom-call | tf_op jit(solution)/shard_map/pallas_call | solution.py:99
  96.7 3.0 convolution_convert_fusion.5.refs_1_.v
  101.1 49.2 %shard_map.317 = (bf16[4,2,128,1024]{3,2,1,0:T(8,128)(2,1)S(1)}, bf16[4,2,128,1024]{3,2,1,0:T(8,128)(2,1)}) custom-call(bf16[512,1024]{1,0:T(8,128)(2,1)S(1)} %convolution_convert_fusion.6.refs_0_.k, bf16[512,1024]{1,0:T(8,128)(2,1)S(1)} %convolution_convert_fusion.5.refs_1_.v), custom_call_target="tpu_custom_call" | custom-call | tf_op jit(solution)/shard_map/pallas_call | solution.py:335
  153.2 26.3 %shard_map.318 = bf16[512,1024]{1,0:T(8,128)(2,1)} custom-call(s32[2]{0:T(128)} %ll.3, s32[2]{0:T(128)} %sl.3, bf16[512,1024]{1,0:T(8,128)(2,1)} %convolution_convert_fusion.7.q, bf16[512,1024]{1,0:T(8,128)(2,1)} %copy-done.1, bf16[512,1024]{1,0:T(8,128)(2,1)} %copy-done, bf16[4,2,128,1024]{3,2,1,0:T(8,128)(2,1)} %copy-done.2, ...), custom_call_target="tpu_custom_call" | custom-call | tf_op jit(solution)/shard_map/pallas_call | solution.py:295
  179.5 2.6 multiply_reduce_fusion.3
  189.5 4.5 scatter_custom_fusion.1
  194.1 5.1 gather_fusion
  199.4 3.4 mul.324
  202.8 6.0 mul.325
  208.9 4.3 scatter_custom_fusion
  213.4 2.5 multiply_convert_fusion
  215.9 5.1 gather_fusion.1
  220.9 4.5 select_select_fusion
  225.5 5.6 all-to-all-start.2
  231.8 59.3 %all-to-all-done.2 = bf16[8,160,1024]{2,1,0:T(8,128)(2,1)S(1)} async-done(((bf16[8,160,1024]{2,1,0:T(8,128)(2,1)}), bf16[8,160,1024]{2,1,0:T(8,128)(2,1)S(1)}, u32[]{:S(2)}, u32[]{:S(2)}) %all-to-all-start.2) | async-done | bytes 2621472 | tf_op jit(solution)/shard_map/all_to_all | solution.py:537
  291.1 4.4 all-to-all-start
  296.0 13.3 %fusion.18 = f32[8,160,2816]{2,1,0:T(8,128)} fusion(bf16[8,160,1024]{2,1,0:T(8,128)(2,1)S(1)} %all-to-all-done.2, bf16[1,1024,2816]{2,1,0:T(8,128)(2,1)} %all-gather.8.cloned.1.call-done), kind=kOutput, calls=%fused_computation.34 | convolution fusion | flops 7381975040 | bytes 22806528 | tf_op jit(solution)/shard_map/slcd,ldf->slcf/dot_general | solution.py:540
  309.3 45.3 %all-to-all-done = bf16[8,160,1024]{2,1,0:T(8,128)(2,1)} async-done(((bf16[8,160,1024]{2,1,0:T(8,128)(2,1)}), bf16[8,160,1024]{2,1,0:T(8,128)(2,1)}, u32[]{:S(2)}, u32[]{:S(2)}) %all-to-all-start) | async-done | bytes 2621472 | tf_op jit(solution)/shard_map/all_to_all | solution.py:483
  354.7 13.8 %fusion.24 = f32[8,160,2816]{2,1,0:T(8,128)} fusion(bf16[8,160,1024]{2,1,0:T(8,128)(2,1)} %all-to-all-done, bf16[1,1024,2816]{2,1,0:T(8,128)(2,1)} %all-gather.6.cloned.1.call-done), kind=kOutput, calls=%fused_computation.40 | convolution fusion | flops 7381975040 | bytes 22806528 | tf_op jit(solution)/shard_map/slcd,ldf->slcf/dot_general | solution.py:487
  368.5 24.5 %fusion.12 = (bf16[8,160,2816]{2,1,0:T(8,128)(2,1)}, bf16[8,1,160,2816]{3,2,0,1:T(8,128)(2,1)S(1)}, bf16[8,160,2816]{2,1,0:T(8,128)(2,1)}) fusion(f32[8,160,2816]{2,1,0:T(8,128)} %fusion.18, f32[8,160,2816]{2,1,0:T(8,128)} %fusion.24, bf16[8,160,1024]{2,1,0:T(8,128)(2,1)} %all-to-all-done, bf16[1,1024,2816]{2,1,0:T(8,128)(2,1)} %all-gather.4.cloned.1.call-done), kind=kOutput, calls=%fused_computation.28 | convolution fusion | flops 7475691520 | bytes 58851328 | tf_op jit(solution)/shard_map/slcd,ldf->slcf/dot_general | solution.py:486
  393.0 2.9 copy-done.77
  395.9 11.6 %fusion.17 = bf16[1,1024,2816]{2,1,0:T(8,128)(2,1)} fusion(bf16[8,160,1024]{2,1,0:T(8,128)(2,1)} %all-to-all-done, bf16[8,1,160,2816]{3,2,0,1:T(8,128)(2,1)S(1)} %get-tuple-element.95), kind=kOutput, calls=%fused_computation.33 | convolution fusion | flops 7384858624 | bytes 15597568 | tf_op jit(solution)/shard_map/slcd,slcf->ldf/dot_general | solution.py:562
  407.5 13.0 %fusion.31 = bf16[1,1024,2816]{2,1,0:T(8,128)(2,1)} fusion(bf16[8,160,1024]{2,1,0:T(8,128)(2,1)} %all-to-all-done, bf16[8,160,2816]{2,1,0:T(8,128)(2,1)} %get-tuple-element.94), kind=kOutput, calls=%fused_computation.46 | convolution fusion | flops 7384858624 | bytes 15597568 | tf_op jit(solution)/shard_map/slcd,slcf->ldf/dot_general | solution.py:565
  420.5 11.7 %fusion.15 = f32[8,160,1024]{2,1,0:T(8,128)S(1)} fusion(bf16[8,1,160,2816]{3,2,0,1:T(8,128)(2,1)} %copy-done.77, bf16[1,1024,2816]{2,1,0:T(8,128)(2,1)} %all-gather.4.cloned.1.call-done), kind=kOutput, calls=%fused_computation.31 | convolution fusion | flops 7381975040 | bytes 18219008 | tf_op jit(solution)/shard_map/slcf,ldf->slcd/dot_general | solution.py:550
  432.3 11.0 %add_convert_fusion = bf16[8,160,1024]{2,1,0:T(8,128)(2,1)} fusion(f32[8,160,1024]{2,1,0:T(8,128)S(1)} %fusion.15, bf16[8,160,2816]{2,1,0:T(8,128)(2,1)} %get-tuple-element.94, bf16[1,1024,2816]{2,1,0:T(8,128)(2,1)S(1)} %bitcast.273), kind=kOutput, calls=%fused_computation.45 | convolution fusion | flops 7384596480 | bytes 20840448 | tf_op jit(solution)/shard_map/slcf,ldf->slcd/dot_general | solution.py:551
  443.3 4.0 all-to-all-start.3
  447.3 12.7 %fusion.52 = bf16[8,160,1024]{2,1,0:T(8,128)(2,1)} fusion(bf16[8,160,2816]{2,1,0:T(8,128)(2,1)} %get-tuple-element.96, bf16[1,1024,2816]{2,1,0:T(8,128)(2,1)} %all-gather.8.cloned.1.call-done), kind=kOutput, calls=%fused_computation.86 | convolution fusion | flops 7383285760 | bytes 15597568 | tf_op jit(solution)/shard_map/slcf,ldf->slcd/dot_general | solution.py:489
  460.0 46.6 %all-to-all-done.3 = bf16[8,160,1024]{2,1,0:T(8,128)(2,1)S(1)} async-done(((bf16[8,160,1024]{2,1,0:T(8,128)(2,1)}), bf16[8,160,1024]{2,1,0:T(8,128)(2,1)S(1)}, u32[]{:S(2)}, u32[]{:S(2)}) %all-to-all-start.3) | async-done | bytes 2621472 | tf_op jit(solution)/shard_map/all_to_all | solution.py:553
  506.6 4.4 all-to-all-start.1
  511.1 13.0 %fusion.32 = bf16[1,1024,2816]{2,1,0:T(8,128)(2,1)} fusion(bf16[8,160,1024]{2,1,0:T(8,128)(2,1)} %copy-done.12, bf16[8,160,2816]{2,1,0:T(8,128)(2,1)} %get-tuple-element.96), kind=kOutput, calls=%fused_computation.47 | convolution fusion | flops 7384858624 | bytes 15597568 | tf_op jit(solution)/shard_map/slcd,slcf->ldf/dot_general | solution.py:568
  525.2 5.3 gather_fusion.3
  530.5 39.5 %all-to-all-done.1 = bf16[8,160,1024]{2,1,0:T(8,128)(2,1)} async-done(((bf16[8,160,1024]{2,1,0:T(8,128)(2,1)}), bf16[8,160,1024]{2,1,0:T(8,128)(2,1)}, u32[]{:S(2)}, u32[]{:S(2)}) %all-to-all-start.1) | async-done | bytes 2621472 | tf_op jit(solution)/shard_map/all_to_all | solution.py:492
  570.0 7.1 gather_fusion.2
  577.1 5.2 fusion.50
  582.3 5.8 reshape.499
  588.1 2.9 multiply_reduce_fusion
  591.5 6.0 reshape.498
  597.6 7.2 fusion.92
  607.0 3.2 fusion.93
  616.4 41.4 %shard_map.319 = (bf16[512,1024]{1,0:T(8,128)(2,1)}, bf16[256,1024]{1,0:T(8,128)(2,1)}, bf16[256,1024]{1,0:T(8,128)(2,1)}, bf16[4,2,128,1024]{3,2,1,0:T(8,128)(2...) custom-call(s32[2]{0:T(128)} %ll.3, s32[2]{0:T(128)} %sl.3, ...), custom_call_target="tpu_custom_call" | custom-call | tf_op jit(solution)/shard_map/pallas_call | solution.py:295
  662.3 26.0 %shard_map.320 = (bf16[2,128,1024]{2,1,0:T(8,128)(2,1)S(1)}, bf16[2,128,1024]{2,1,0:T(8,128)(2,1)S(1)}) custom-call(bf16[4,2,128,1024]{3,2,1,0:T(8,128)(2,1)S(1)} %copy-done.3, bf16[4,2,128,1024]{3,2,1,0:T(8,128)(2,1)S(1)} %copy-done.4), custom_call_target="tpu_custom_call" | custom-call | tf_op jit(solution)/shard_map/pallas_call | solution.py:367
  692.1 3.0 fusion.38
  698.1 3.9 convolution_convert_fusion
  701.9 2.7 convolution_convert_fusion.1
  707.9 62.1 %shard_map.321 = (f32[32,1024]{1,0:T(8,128)S(1)}, f32[32,1024]{1,0:T(8,128)S(1)}, f32[32,1024]{1,0:T(8,128)S(1)}, f32[32,1024]{1,0:T(8,128)S(1)}, f32[8,128]{1,0:T(8,128)S(1)}) custom-call(bf16[2,2,4,2,32,1024]{5,4,3,2,1,0:T(8,128)(2,1)S(1)} %bitcast.212, bf16[2,2,4,2,32,1024]{5,4,3,2,1,0:T(8,128)(2,1)S(1)} %bitcast.211, ...), custom_call_target="tpu_custom_call" | custom-call | tf_op jit(solution)/shard_map/pallas_call | solution.py:172
  777.7 3.1 convert_element_type.206
  780.8 3.1 convert_element_type.209
  784.0 3.1 convert_element_type.212
  (277 shorter events, 55.0 us)
Async XLA Ops:
  7.2 3.3 copy-start.59
  7.2 3.5 copy-start.64
  7.2 3.5 copy-start.63
  7.2 3.5 copy-start.62
  7.2 87.1 %copy-start.61 = (s32[2,128,2]{1,2,0:T(2,128)S(1)}, s32[2,128,2]{1,2,0:T(2,128)}, u32[]{:S(2)}) copy-start(s32[2,128,2]{1,2,0:T(2,128)} %param.42) | copy-start | bytes 6148
  7.2 87.1 %copy-start.60 = (s32[2,128,2]{1,2,0:T(2,128)S(1)}, s32[2,128,2]{1,2,0:T(2,128)}, u32[]{:S(2)}) copy-start(s32[2,128,2]{1,2,0:T(2,128)} %param.43) | copy-start | bytes 6148
  7.3 288.7 %all-gather.8.cloned.1.call-start = ((), (), s32[]{:S(2)}) async-start(), calls=%async_computation.9 | async-start | bytes 7208960 | tf_op jit(solution)/shard_map/all_gather | solution.py:434
  8.0 87.1 %copy-start.54 = (s32[2,128]{1,0:T(2,128)S(1)}, s32[2,128]{1,0:T(2,128)}, u32[]{:S(2)}) copy-start(s32[2,128]{1,0:T(2,128)} %param.39) | copy-start | bytes 3076
  8.0 88.3 %copy-start.15 = (bf16[2,128,1024]{2,1,0:T(8,128)(2,1)S(1)}, bf16[2,128,1024]{2,1,0:T(8,128)(2,1)}, u32[]{:S(2)}) copy-start(bf16[2,128,1024]{2,1,0:T(8,128)(2,1)} %param.24) | copy-start | bytes 1572868
  8.0 88.3 %copy-start.17 = (bf16[2,128,1024]{2,1,0:T(8,128)(2,1)S(1)}, bf16[2,128,1024]{2,1,0:T(8,128)(2,1)}, u32[]{:S(2)}) copy-start(bf16[2,128,1024]{2,1,0:T(8,128)(2,1)} %param.23) | copy-start | bytes 1572868
  8.0 346.6 %all-gather.6.cloned.1.call-start = ((), (), s32[]{:S(2)}) async-start(), calls=%async_computation.8 | async-start | bytes 7208960 | tf_op jit(solution)/shard_map/all_gather | solution.py:433
  94.4 90.3 %copy-start.32 = (s32[512,2]{0,1:T(2,128)}, s32[512,2]{0,1:T(2,128)S(1)}, u32[]{:S(2)}) copy-start(s32[512,2]{0,1:T(2,128)S(1)} %get-tuple-element.137) | copy-start | bytes 12292
  94.9 94.0 %copy-start.30 = (s32[1024]{0:T(1024)}, s32[1024]{0:T(1024)S(1)}, u32[]{:S(2)}) copy-start(s32[1024]{0:T(1024)S(1)} %eq.38) | copy-start | bytes 12292
  95.0 56.0 %copy-start.51 = (f32[1024]{0:T(1024)}, f32[1024]{0:T(1024)S(1)}, u32[]{:S(2)}) copy-start(f32[1024]{0:T(1024)S(1)} %reshape.495) | copy-start | bytes 12292
  96.0 86.7 %copy-start.28 = (f32[1024]{0:T(1024)}, f32[1024]{0:T(1024)S(1)}, u32[]{:S(2)}) copy-start(f32[1024]{0:T(1024)S(1)} %reshape.497) | copy-start | bytes 12292
  96.3 87.2 %copy-start.13 = (bf16[1024,8]{1,0:T(8,128)(2,1)}, bf16[1024,8]{1,0:T(8,128)(2,1)S(1)}, u32[]{:S(2)}) copy-start(bf16[1024,8]{1,0:T(8,128)(2,1)S(1)} %reshape.468) | copy-start | bytes 49156
  96.7 54.3 %copy-start.55 = (f32[512]{0:T(512)}, f32[512]{0:T(512)S(1)}, u32[]{:S(2)}) copy-start(f32[512]{0:T(512)S(1)} %fusion.80) | copy-start | bytes 6148
  101.1 52.1 %copy-start.1 = (bf16[512,1024]{1,0:T(8,128)(2,1)}, bf16[512,1024]{1,0:T(8,128)(2,1)S(1)}, u32[]{:S(2)}) copy-start(bf16[512,1024]{1,0:T(8,128)(2,1)S(1)} %convolution_convert_fusion.6.refs_0_.k) | copy-start | bytes 3145732
  101.1 49.9 %copy-start.66 = (bf16[2,2,4,2,32,1024]{5,4,3,2,1,0:T(8,128)(2,1)S(1)}, bf16[2,2,4,2,32,1024]{5,4,3,2,1,0:T(8,128)(2,1)}, u32[]{:S(2)}) copy-start(bf16[2,2,4,2,32,1024]{5,4,3,2,1,0:T(8,128)(2,1)} %get-tuple-element.37) | copy-start | bytes 6291460
  153.2 26.3 %copy-start.70 = (bf16[2,2,4,2,32,1024]{5,4,3,2,1,0:T(8,128)(2,1)S(1)}, bf16[2,2,4,2,32,1024]{5,4,3,2,1,0:T(8,128)(2,1)}, u32[]{:S(2)}) copy-start(bf16[2,2,4,2,32,1024]{5,4,3,2,1,0:T(8,128)(2,1)} %get-tuple-element.42) | copy-start | bytes 6291460
  183.6 15.6 %copy-start.5 = (bf16[512,1024]{1,0:T(8,128)(2,1)}, bf16[512,1024]{1,0:T(8,128)(2,1)S(1)}, u32[]{:S(2)}) copy-start(bf16[512,1024]{1,0:T(8,128)(2,1)S(1)} %multiply_convert_fusion.1) | copy-start | bytes 3145732
  188.8 5.2 copy-start.34
  188.8 5.2 copy-start.41
  194.1 5.1 copy-start.21
  194.1 5.1 copy-start.23
  225.5 65.6 %all-to-all-start.2 = ((bf16[8,160,1024]{2,1,0:T(8,128)(2,1)}), bf16[8,160,1024]{2,1,0:T(8,128)(2,1)S(1)}, u32[]{:S(2)}, u32[]{:S(2)}) async-start(bf16[8,160,1024]{2,1,0:T(8,128)(2,1)} %get-tuple-element.142), calls=%async_computation.2 | async-start | bytes 5242880 | tf_op jit(solution)/shard_map/all_to_all | solution.py:537
  231.1 137.4 %all-gather.4.cloned.1.call-start = ((), (), s32[]{:S(2)}) async-start(), calls=%async_computation.7 | async-start | bytes 7208960 | tf_op jit(solution)/shard_map/all_gather | solution.py:432
  291.1 4.9 copy-start.12
  291.1 63.5 %all-to-all-start = ((bf16[8,160,1024]{2,1,0:T(8,128)(2,1)}), bf16[8,160,1024]{2,1,0:T(8,128)(2,1)}, u32[]{:S(2)}, u32[]{:S(2)}) async-start(bf16[8,160,1024]{2,1,0:T(8,128)(2,1)} %get-tuple-element.143), calls=%async_computation | async-start | bytes 5242880 | tf_op jit(solution)/shard_map/all_to_all | solution.py:483
  295.5 482.2 %reduce-scatter.4.cloned.1.call-start = ((), (), s32[]{:S(2)}) async-start(), calls=%async_computation.10 | async-start | bytes 7208960 | tf_op jit(solution)/shard_map/reduce_scatter | solution.py:572
  407.5 373.4 %reduce-scatter.6.cloned.1.call-start = ((), (), s32[]{:S(2)}) async-start(), calls=%async_computation.11 | async-start | bytes 7208960 | tf_op jit(solution)/shard_map/reduce_scatter | solution.py:575
  420.5 11.8 %slice-start = ((s8[5767168]{0:T(1024)(128)(4,1)}), s8[1572864]{0:T(1024)(128)(4,1)S(1)}, s32[]{:S(2)}) async-start(s8[5767168]{0:T(1024)(128)(4,1)} %bitcast.272), calls=%async_computation.13 | async-start | bytes 3145728
  420.5 11.8 %slice-start.1 = ((s8[5767168]{0:T(1024)(128)(4,1)}), s8[4194304]{0:T(1024)(128)(4,1)S(1)}, s32[]{:S(2)}) async-start(s8[5767168]{0:T(1024)(128)(4,1)} %bitcast.272), calls=%async_computation.14 | async-start | bytes 8388608
  443.3 63.3 %all-to-all-start.3 = ((bf16[8,160,1024]{2,1,0:T(8,128)(2,1)}), bf16[8,160,1024]{2,1,0:T(8,128)(2,1)S(1)}, u32[]{:S(2)}, u32[]{:S(2)}) async-start(bf16[8,160,1024]{2,1,0:T(8,128)(2,1)} %add_convert_fusion), calls=%async_computation.3 | async-start | bytes 5242880 | tf_op jit(solution)/shard_map/all_to_all | solution.py:553
  506.6 63.4 %all-to-all-start.1 = ((bf16[8,160,1024]{2,1,0:T(8,128)(2,1)}), bf16[8,160,1024]{2,1,0:T(8,128)(2,1)}, u32[]{:S(2)}, u32[]{:S(2)}) async-start(bf16[8,160,1024]{2,1,0:T(8,128)(2,1)} %fusion.52), calls=%async_computation.1 | async-start | bytes 5242880 | tf_op jit(solution)/shard_map/all_to_all | solution.py:492
  511.0 272.9 %reduce-scatter.8.cloned.1.call-start = ((), (), s32[]{:S(2)}) async-start(), calls=%async_computation.12 | async-start | bytes 7208960 | tf_op jit(solution)/shard_map/reduce_scatter | solution.py:578
  588.1 3.3 copy-start.27
  588.1 3.3 copy-start.39
  597.5 7.2 copy-start.8
  597.5 7.2 copy-start.14
  597.5 7.2 copy-start.29
  597.5 7.2 copy-start.48
  610.3 3.8 copy-start.71
  662.2 26.0 %copy-start.69 = (bf16[2,2,4,2,32,1024]{5,4,3,2,1,0:T(8,128)(2,1)S(1)}, bf16[2,2,4,2,32,1024]{5,4,3,2,1,0:T(8,128)(2,1)}, u32[]{:S(2)}) copy-start(bf16[2,2,4,2,32,1024]{5,4,3,2,1,0:T(8,128)(2,1)} %get-tuple-element.38) | copy-start | bytes 6291460
  662.3 26.0 %copy-start.74 = (bf16[256,1024]{1,0:T(8,128)(2,1)S(1)}, bf16[256,1024]{1,0:T(8,128)(2,1)}, u32[]{:S(2)}) copy-start(bf16[256,1024]{1,0:T(8,128)(2,1)} %get-tuple-element.47) | copy-start | bytes 1572868
  698.1 3.9 copy-start.75
  707.8 64.0 %copy-start.50 = (f32[512]{0:T(512)S(1)}, f32[512]{0:T(512)}, u32[]{:S(2)}) copy-start(f32[512]{0:T(512)} %copy-done.49) | copy-start | bytes 6148
  770.7 3.4 copy-start.20
  (42 other events, 73.8 us)
Sparse Core Ops, SparseCore 0:
  9.6 70.8 all-gather.7
  82.1 65.6 all-gather.5
  233.5 43.8 all-gather.3
  407.6 52.9 reduce-scatter.3
  463.1 54.8 reduce-scatter.5
  524.3 55.2 reduce-scatter.7

commit v3 on v2

--- a/solution.py
+++ b/solution.py
@@ -21,10 +21,6 @@
 def rms_norm(hidden, gain):
     scale = lax.rsqrt(jnp.mean(hidden * hidden, axis=-1, keepdims=True) + epsilon)
     return hidden * scale * gain
-
-
-def gelu_mul(gate_pre, up_pre):
-    return jax.nn.gelu(gate_pre, approximate=True) * up_pre
 
 
 def gate_values(logits, choose):
@@ -371,6 +367,129 @@
         compiler_params=pltpu.CompilerParams(collective_id=cid, has_side_effects=True, vmem_limit_bytes=48 * 2**20))(*arrays)
 
 
+def gelu_parts(v):
+    c, a = 0.7978845608, 0.044715
+    v2 = v * v
+    t = jnp.tanh(c * v * (1.0 + a * v2))
+    half = 0.5 * (1.0 + t)
+    return v * half, half + 0.5 * v * (1.0 - t * t) * (c * (1.0 + 3.0 * a * v2))
+def expert_kernel(cap, per, order, wcut, tile, xs, gs, wgi, wui, wdi, eo_out, ri_out, dg_out, du_out, dd_out,
+                  wg, wu, wd, xr, gr, hid, gg, ug, eo, ri, xt, gt, stage,
+                  lsem, xss, xrs, gss, grs, ess, ers, rss, rrs, wss, wrs, wls, osem, ssem):
+    dp = lax.axis_size("dp")
+    f32, bf = jnp.float32, jnp.bfloat16
+    s, x, c, xdev, cdev = seq_places(2)
+    g = lax.axis_index("dp")
+    def peer(k): return (s, g ^ k)
+    greet([xdev, cdev] + [peer(k) for k in range(1, dp)])
+    rows_w = wgi.shape[0]; ff = wgi.shape[1]; width = xs.shape[2]
+    piece = rows_w // wcut
+    own, far = s * rows_w, ((1 - x) * 2 + c) * rows_w
+    mats = ((wgi, wg), (wui, wu), (wdi, wd))
+    wx, wc, wl = [], [], []
+    for h in range(wcut):
+        for m, (src, dst) in enumerate(mats):
+            n = len(wx)
+            a = src.at[pl.ds(h * piece, piece)]
+            b = dst.at[pl.ds(own + h * piece, piece)]
+            wx.append(remote(a, b, wss.at[n, 0], wrs.at[n, 0], xdev))
+            wc.append(remote(a, b, wss.at[n, 1], wrs.at[n, 1], cdev))
+            cp = pltpu.make_async_copy(a, b, wls.at[n]); cp.start(); wl.append(cp)
+    sx, sg = {}, {}
+    for k in [k for p in order for k in range(p * per, (p + 1) * per)]:
+        at = pl.ds(k * cap, cap)
+        if k == 0:
+            sx[0] = pltpu.make_async_copy(xs.at[g], xr.at[at], lsem.at[0]); sx[0].start()
+            sg[0] = pltpu.make_async_copy(gs.at[g], gr.at[at], lsem.at[1]); sg[0].start()
+        else:
+            sx[k] = remote(xs.at[g ^ k], xr.at[at], xss.at[k], xrs.at[k], peer(k))
+            sg[k] = remote(gs.at[g ^ k], gr.at[at], gss.at[k], grs.at[k], peer(k))
+    wf = []
+    for h in range(wcut):
+        for m, (src, dst) in enumerate(mats):
+            n = len(wf)
+            wx[n].wait_recv()
+            b = dst.at[pl.ds(far + h * piece, piece)]
+            wf.append(remote(b, b, wss.at[n, 2], wrs.at[n, 2], cdev))
+    for n in range(len(wf)):
+        wl[n].wait(); wc[n].wait_recv(); wf[n].wait_recv()
+    ntile = ff // tile
+    re, rr = {}, {}
+    for p in order:
+        ks = list(range(p * per, (p + 1) * per))
+        for k in ks:
+            if k == 0: sx[0].wait(); sg[0].wait()
+            else: sx[k].wait_recv(); sg[k].wait_recv()
+        rows = pl.ds(p * per * cap, per * cap)
+        @pl.loop(0, ntile)
+        def _(t):
+            cols = pl.ds(pl.multiple_of(t * tile, 128), tile)
+            gp = jnp.dot(xr[rows, :], wg[:, cols], preferred_element_type=f32)
+            up = jnp.dot(xr[rows, :], wu[:, cols], preferred_element_type=f32)
+            hg = jnp.dot(gr[rows, :], wd[:, cols], preferred_element_type=f32)
+            act, der = gelu_parts(gp)
+            hid[rows, cols] = (act * up).astype(bf)
+            gg[rows, cols] = (hg * up * der).astype(bf)
+            ug[rows, cols] = (hg * act).astype(bf)
+        @pl.loop(0, width // 256)
+        def _(t):
+            part = pl.ds(pl.multiple_of(t * 256, 256), 256)
+            eo[rows, part] = dot(hid[rows, :], wd[part, :], 1, 1).astype(bf)
+            ri[rows, part] = (dot(gg[rows, :], wg[part, :], 1, 1) + dot(ug[rows, :], wu[part, :], 1, 1)).astype(bf)
+        for k in ks:
+            at = pl.ds(k * cap, cap)
+            if k == 0:
+                re[0] = pltpu.make_async_copy(eo.at[at], eo_out.at[g], lsem.at[2]); re[0].start()
+                rr[0] = pltpu.make_async_copy(ri.at[at], ri_out.at[g], lsem.at[3]); rr[0].start()
+            else:
+                re[k] = remote(eo.at[at], eo_out.at[g], ess.at[k], ers.at[k], peer(k))
+                rr[k] = remote(ri.at[at], ri_out.at[g], rss.at[k], rrs.at[k], peer(k))
+    total = dp * cap
+    @pl.loop(0, total // 256)
+    def _(t):
+        at = pl.ds(pl.multiple_of(t * 256, 256), 256)
+        xt[:, at] = xr[at, :].T
+        gt[:, at] = gr[at, :].T
+    for m, (lhs, rhs, out) in enumerate(((gt, hid, dd_out), (xt, gg, dg_out), (xt, ug, du_out))):
+        @pl.loop(0, ntile)
+        def _(t):
+            cols = pl.ds(pl.multiple_of(t * tile, 128), tile)
+            res = jnp.dot(lhs[...], rhs[:, cols], preferred_element_type=f32).astype(bf)
+            stage[...] = res
+            cp = pltpu.make_async_copy(stage, out.at[:, cols], osem.at[0])
+            cp.start(); cp.wait()
+    for n in range(len(wf)):
+        wx[n].wait_send(); wc[n].wait_send(); wf[n].wait_send()
+    for k in range(dp):
+        if k == 0:
+            re[0].wait(); rr[0].wait()
+        else:
+            sx[k].wait_send(); sg[k].wait_send(); re[k].wait(); rr[k].wait()
+def expert_all(xs, gs, wg, wu, wd, seq, cid):
+    dp, cap, width = xs.shape
+    ff = wg.shape[1]; total = dp * cap
+    group = 320
+    per = group // cap
+    ng = dp // per
+    order = [p for p in range(ng // 2, ng)] + [p for p in range(ng // 2 - 1, -1, -1)]
+    sem = pltpu.SemaphoreType.DMA
+    bf = jnp.bfloat16
+    any_ = pl.BlockSpec(memory_space=pl.ANY)
+    V = pltpu.VMEM
+    tile = 256
+    wcut = 2
+    full = (seq * wg.shape[0], ff)
+    back = jax.ShapeDtypeStruct((dp, cap, width), bf)
+    loc = jax.ShapeDtypeStruct(full, bf)
+    return pl.pallas_call(functools.partial(expert_kernel, cap, per, order, wcut, tile),
+        out_shape=[back, back, loc, loc, loc],
+        in_specs=[any_] * 5, out_specs=[any_] * 5,
+        scratch_shapes=[V(full, bf)] * 3 + [V((total, width), bf)] * 2 + [V((total, ff), bf)] * 3 + [V((total, width), bf)] * 2
+        + [V((width, total), bf)] * 2 + [V((width, tile), bf)]
+        + [sem((4,))] + [sem((dp,))] * 8 + [sem((3 * wcut, 3))] * 2 + [sem((3 * wcut,)), sem((1,)), sem((1,))],
+        compiler_params=pltpu.CompilerParams(collective_id=cid, has_side_effects=True, vmem_limit_bytes=63 * 2**20))(xs, gs, wg, wu, wd)
+
+
 def on_device(
     long_tokens,
     short_tokens,
@@ -428,11 +547,6 @@
         small_all[:, 2 * gain_part : 2 * gain_part + table_part].reshape(-1),
         small_all[:, 2 * gain_part + table_part : small_size].reshape(model_width, experts),
     )
-    expert_set = (
-        lax.all_gather(gate_weight, "seq", axis=1, tiled=True),
-        lax.all_gather(up_weight, "seq", axis=1, tiled=True),
-        lax.all_gather(down_weight, "seq", axis=1, tiled=True),
-    )
     resid_in = jnp.concatenate(
         [long_tokens.reshape(long_rows, model_width), short_tokens.reshape(-1, model_width)], 0
     ).astype(jnp.float32)
@@ -479,30 +593,21 @@
     outgoing = jnp.where(
         slot_used[:, None], jnp.take(normed_two, slot_pair // 2, axis=0), 0
     ).reshape(experts, capacity, model_width)
-    gate_full, up_full, down_full = expert_set
-    arrived = lax.all_to_all(outgoing, "dp", split_axis=0, concat_axis=0, tiled=True)
-    slot_count = arrived.shape[1]
-    inputs = arrived.reshape(dp_size, local_experts, slot_count, model_width)
-    gate_pre = jnp.einsum("slcd,ldf->slcf", inputs, gate_full, preferred_element_type=jnp.float32)
-    up_pre = jnp.einsum("slcd,ldf->slcf", inputs, up_full, preferred_element_type=jnp.float32)
-    hidden = gelu_mul(gate_pre, up_pre).astype(jnp.bfloat16)
-    result = jnp.einsum(
-        "slcf,ldf->slcd", hidden, down_full, preferred_element_type=jnp.float32
-    ).astype(jnp.bfloat16)
-    returned = lax.all_to_all(
-        result.reshape(experts, slot_count, model_width),
-        "dp",
-        split_axis=0,
-        concat_axis=0,
-        tiled=True,
-    )
-    ffn_width = hidden.shape[-1]
-    back_rows, expert_in, gate_pre, up_pre, hidden = (
-        returned,
-        arrived,
-        gate_pre.reshape(experts, slot_count, ffn_width),
-        up_pre.reshape(experts, slot_count, ffn_width),
-        hidden.reshape(experts, slot_count, ffn_width),
+    kept_two = route_kept.reshape(tokens, 2).astype(jnp.float32)
+    weighting = gate_share * kept_two
+    grad_out = jnp.concatenate(
+        [long_grad_out.reshape(long_rows, model_width), short_grad_out.reshape(-1, model_width)], 0
+    ).astype(jnp.float32)
+    pair_grad = (
+        (weighting[:, :, None] * grad_out[:, None, :])
+        .astype(jnp.bfloat16)
+        .reshape(2 * tokens, model_width)
+    )
+    out_slots = jnp.where(slot_used[:, None], jnp.take(pair_grad, slot_pair, axis=0), 0).reshape(
+        experts, capacity, model_width
+    )
+    back_rows, returned_grad, gate_local, up_local, down_local = expert_all(
+        outgoing, out_slots, gate_weight[0], up_weight[0], down_weight[0], seq_size, 4
     )
     pair_out = (
         jnp.where(
@@ -513,71 +618,16 @@
         .reshape(tokens, 2, model_width)
         .astype(jnp.float32)
     )
-    kept_two = route_kept.reshape(tokens, 2).astype(jnp.float32)
-    weighting = gate_share * kept_two
     final = resid_mid + weighting[:, 0:1] * pair_out[:, 0] + weighting[:, 1:2] * pair_out[:, 1]
     final_low = final.astype(jnp.bfloat16)
     long_out = final_low[:long_rows].reshape(long_items, quarter, model_width)
     short_out = final_low[long_rows:].reshape(short_items, short_len, model_width)
-    grad_out = jnp.concatenate(
-        [long_grad_out.reshape(long_rows, model_width), short_grad_out.reshape(-1, model_width)], 0
-    ).astype(jnp.float32)
-    pair_grad = (
-        (weighting[:, :, None] * grad_out[:, None, :])
-        .astype(jnp.bfloat16)
-        .reshape(2 * tokens, model_width)
-    )
     share_grad = kept_two * jnp.sum(grad_out[:, None, :] * pair_out, axis=-1)
     logit_grad = gate_pull(share_grad)[0].astype(jnp.bfloat16)
-    out_slots = jnp.where(slot_used[:, None], jnp.take(pair_grad, slot_pair, axis=0), 0).reshape(
-        experts, capacity, model_width
-    )
-    attn_back, expert_back = attn_set, expert_set
-    gate_back, up_back, down_back = expert_back
-    arrived_grad = lax.all_to_all(out_slots, "dp", split_axis=0, concat_axis=0, tiled=True)
-    shape_four = (dp_size, local_experts, capacity, -1)
-    grad_four = arrived_grad.reshape(dp_size, local_experts, capacity, model_width)
-    hidden_grad = jnp.einsum(
-        "slcd,ldf->slcf", grad_four, down_back, preferred_element_type=jnp.float32
-    )
-    unused_geglu, geglu_pull = jax.vjp(
-        gelu_mul, gate_pre.reshape(shape_four), up_pre.reshape(shape_four)
-    )
-    gate_pre_grad, up_pre_grad = geglu_pull(hidden_grad)
-    gate_pre_grad = gate_pre_grad.astype(jnp.bfloat16)
-    up_pre_grad = up_pre_grad.astype(jnp.bfloat16)
-    input_grad = (
-        jnp.einsum("slcf,ldf->slcd", gate_pre_grad, gate_back, preferred_element_type=jnp.float32)
-        + jnp.einsum("slcf,ldf->slcd", up_pre_grad, up_back, preferred_element_type=jnp.float32)
-    ).astype(jnp.bfloat16)
-    returned_grad = lax.all_to_all(
-        input_grad.reshape(experts, capacity, model_width),
-        "dp",
-        split_axis=0,
-        concat_axis=0,
-        tiled=True,
-    )
-    inputs_four = expert_in.reshape(dp_size, local_experts, capacity, model_width)
-    hidden_four = hidden.reshape(shape_four)
-    gate_local = jnp.einsum(
-        "slcd,slcf->ldf", inputs_four, gate_pre_grad, preferred_element_type=jnp.float32
-    )
-    up_local = jnp.einsum(
-        "slcd,slcf->ldf", inputs_four, up_pre_grad, preferred_element_type=jnp.float32
-    )
-    down_local = jnp.einsum(
-        "slcd,slcf->ldf", grad_four, hidden_four, preferred_element_type=jnp.float32
-    )
+    attn_back = attn_set
     gate_grad, up_grad, down_grad = (
-        lax.psum_scatter(
-            gate_local.astype(jnp.bfloat16), "seq", scatter_dimension=1, tiled=True
-        ).astype(jnp.float32),
-        lax.psum_scatter(
-            up_local.astype(jnp.bfloat16), "seq", scatter_dimension=1, tiled=True
-        ).astype(jnp.float32),
-        lax.psum_scatter(
-            down_local.astype(jnp.bfloat16), "seq", scatter_dimension=1, tiled=True
-        ).astype(jnp.float32),
+        lax.psum_scatter(part[None], "seq", scatter_dimension=1, tiled=True).astype(jnp.float32)
+        for part in (gate_local, up_local, down_local)
     )
     route_grad = (
         jnp.where(

time: 807 us -> 726 us (0.90)
  Pallas kernels: 287 us -> 534 us
  waiting for transfers between devices: 193 us -> 0.71 us
  matrix products: 154 us -> 28.5 us
    pallas_call x0 -> x1, Pallas kernels: none -> 235 us  [expert_all(): pl.pallas_call(functools.partial(expert_kernel, cap, per, order, wcut, ti...]
    all_to_all x4 -> x0, waiting for transfers between devices: 191 us -> none  [the longest x1 59.3 us: on_device(): lax.all_to_all(out_slots, 'dp', split_axis=0, concat_axis=0, tiled=True)]
    dot_general x9 -> x0, matrix products: 125 us -> none  [the longest x1 24.5 us: on_device(): jnp.einsum('slcd,ldf->slcf', inputs, gate_full, preferred_element_type=jn...]
    pallas_call x1, Pallas kernels: 62.1 us -> 97.6 us  [scatter_all(): pl.pallas_call(functools.partial(scatter_kernel, dims, pieces, n), out_sh...]
    pallas_call x1, Pallas kernels: 81.8 us -> 60.1 us  [gather_all(): pl.pallas_call(functools.partial(gather_kernel, dims, pieces, na), out_sh...]
    pallas_call x1, Pallas kernels: 49.2 us -> 28.8 us  [seq_gather(): pl.pallas_call(functools.partial(seq_gather_kernel, n, items, rows), out_...]
    pallas_call x1, Pallas kernels: 26 us -> 44.6 us  [seq_sum(): pl.pallas_call(functools.partial(seq_sum_kernel, n, items), out_shape=[ja...]
    all_to_all x4 -> x0, starting transfers between devices: 18.5 us -> none  [the longest x1 5.64 us: on_device(): lax.all_to_all(out_slots, 'dp', split_axis=0, concat_axis=0, tiled=True)]
  transfers between devices with their start and end apart: 10 -> 3, of which waited for: 4 -> 0; matrix products, arithmetic and copies ran while one was open for 29% -> 11% of each run, Pallas kernels for 36% -> 25%
where the time goes in v3:
time: 726 us; the launch traced here: 723 us
  Pallas kernels  534 us (74%)
  local copies, waits for them, and re-layouts  94.4 us (13%)
  other arithmetic  36.3 us (5%)
  matrix products  28.5 us (4%)
  between operations  14.9 us (2%)
  starting transfers between devices  13.7 us (2%)
    pallas_call x1, Pallas kernels, expert_all(): pl.pallas_call(functools.partial(expert_kernel, cap, per, order, wcut, ti...  235 us
    pallas_call x1, Pallas kernels, scatter_all(): pl.pallas_call(functools.partial(scatter_kernel, dims, pieces, n), out_sh...  97.6 us
    pallas_call x2, Pallas kernels, attention(): pl.pallas_call(body, out_shape=outs, in_specs=[sm, sm] + [vm] * (len(arra...  67.8 us
    pallas_call x1, Pallas kernels, gather_all(): pl.pallas_call(functools.partial(gather_kernel, dims, pieces, na), out_sh...  60.1 us
    pallas_call x1, Pallas kernels, seq_sum(): pl.pallas_call(functools.partial(seq_sum_kernel, n, items), out_shape=[ja...  44.6 us
    pallas_call x1, Pallas kernels, seq_gather(): pl.pallas_call(functools.partial(seq_gather_kernel, n, items, rows), out_...  28.8 us
  transfers between devices with their start and end apart: 3, of which 0 were waited for; matrix products, arithmetic and copies ran while one was open for 11% of the time, Pallas kernels for 25%

profile of v3, /device:TPU:0, one launch (start us, length us, event | category | flops | bytes accessed | tf_op | source)
XLA Modules:
  0.0 722.5 jit_solution(7229965659887173347)
XLA Ops:
  8.2 1.4 fusion.37.refs_4_
  9.6 60.1 %shard_map.316 = (bf16[2,2,4,2,32,1024]{5,4,3,2,1,0:T(8,128)(2,1)}, bf16[2,2,4,2,32,1024]{5,4,3,2,1,0:T(8,128)(2,1)}, bf16[2,2,4,2,32,1024]{5,4,3,2,1,0:T(8,128)...) custom-call(bf16[32,1024]{1,0:T(8,128)(2,1)} %refs_0_.1, bf16[32,1024]{1,0:T(8,128)(2,1)} %refs_1_.1, ...), custom_call_target="tpu_custom_call" | custom-call | tf_op jit(solution)/shard_map/pallas_call | solution.py:95
  70.7 1.8 reshape.488.lcol
  72.6 1.3 reshape.401.lrow
  75.1 2.5 reduce-window.6
  78.8 4.0 convolution_convert_fusion.7.q
  82.9 1.3 convolution_convert_fusion.6.refs_0_.k
  84.5 1.3 convolution_convert_fusion.5.refs_1_.v
  86.8 28.8 %shard_map.317 = (bf16[4,2,128,1024]{3,2,1,0:T(8,128)(2,1)S(1)}, bf16[4,2,128,1024]{3,2,1,0:T(8,128)(2,1)}) custom-call(bf16[512,1024]{1,0:T(8,128)(2,1)S(1)} %convolution_convert_fusion.6.refs_0_.k, bf16[512,1024]{1,0:T(8,128)(2,1)S(1)} %convolution_convert_fusion.5.refs_1_.v), custom_call_target="tpu_custom_call" | custom-call | tf_op jit(solution)/shard_map/pallas_call | solution.py:331
  115.6 1.3 copy-done.2
  117.5 26.3 %shard_map.318 = bf16[512,1024]{1,0:T(8,128)(2,1)} custom-call(s32[2]{0:T(128)} %ll.3, s32[2]{0:T(128)} %sl.3, bf16[512,1024]{1,0:T(8,128)(2,1)} %convolution_convert_fusion.7.q, bf16[512,1024]{1,0:T(8,128)(2,1)} %copy-done, bf16[512,1024]{1,0:T(8,128)(2,1)} %copy-done.1, bf16[4,2,128,1024]{3,2,1,0:T(8,128)(2,1)} %copy-done.2, ...), custom_call_target="tpu_custom_call" | custom-call | tf_op jit(solution)/shard_map/pallas_call | solution.py:291
  143.8 2.7 multiply_reduce_fusion.3
  147.0 3.4 mul.257
  150.4 6.1 mul.258
  158.3 4.6 scatter_custom_fusion.1
  163.0 8.6 %scatter_custom_fusion = pred[1281]{0:T(1024)(128)(4,1)S(1)} fusion(s32[1024]{0:T(1024)S(1)} %bitcast.170, pred[1024]{0:T(1024)(128)(4,1)S(1)} %broadcast.274, pred[]{:T(512)} %constant.87.clone.1), kind=kCustom, calls=%fused_computation.127 | custom fusion | bytes 1282 | tf_op jit(solution)/shard_map/scatter | solution.py:591
  171.7 5.1 gather_fusion
  176.7 2.5 multiply_convert_fusion
  179.2 5.1 gather_fusion.1
  184.3 4.5 select_select_fusion
  188.8 235.1 %shard_map.319 = (bf16[8,160,1024]{2,1,0:T(8,128)(2,1)}, bf16[8,160,1024]{2,1,0:T(8,128)(2,1)}, bf16[1024,2816]{1,0:T(8,128)(2,1)}, bf16[1024,2816]{1,0:T(8,128)(2,1)}, bf16[1024,2816]{1,0:T(8,128)(2,1)}) custom-call(bf16[8,160,1024]{2,1,0:T(8,128)(2,1)} %get-tuple-element.150.xs, bf16[8,160,1024]{2,1,0:T(8,128)(2,1)} %get-tuple-element.149.gs, ...), custom_call_target="tpu_custom_call" | custom-call | tf_op jit(solution)/shard_map/pallas_call | solution.py:484
  423.9 13.6 %reduce-scatter.6.cloned.1.call-start = ((), (), s32[]{:S(2)}) async-start(), calls=%async_computation.4 | async-start | bytes 7208960 | tf_op jit(solution)/shard_map/reduce_scatter | solution.py:629
  439.4 5.3 gather_fusion.2
  444.7 3.6 multiply_reduce_fusion
  448.7 5.3 gather_fusion.3
  454.1 5.6 fusion.15
  459.6 5.9 reshape.431
  465.5 6.2 reshape.430
  471.7 8.5 %fusion.54 = (f32[512,1,1024]{2,1,0:T(1,128)S(1)}, f32[512,1,1024]{2,1,0:T(1,128)S(1)}) fusion(f32[512,2,1024]{2,1,0:T(2,128)} %reshape.431), kind=kLoop, calls=%fused_computation.148 | loop fusion | bytes 8388608 | tf_op jit(solution)/shard_map/slice | solution.py:642
  482.4 3.2 fusion.55
  485.7 2.5 fusion.4
  488.2 1.3 copy-done.12
  489.5 2.3 convolution_convert_fusion.4.mg
  491.8 41.5 %shard_map.320 = (bf16[512,1024]{1,0:T(8,128)(2,1)}, bf16[256,1024]{1,0:T(8,128)(2,1)}, bf16[256,1024]{1,0:T(8,128)(2,1)}, bf16[4,2,128,1024]{3,2,1,0:T(8,128)(2...) custom-call(s32[2]{0:T(128)} %ll.3, s32[2]{0:T(128)} %sl.3, ...), custom_call_target="tpu_custom_call" | custom-call | tf_op jit(solution)/shard_map/pallas_call | solution.py:291
  535.1 1.6 copy-done.4
  536.7 44.6 %shard_map.321 = (bf16[2,128,1024]{2,1,0:T(8,128)(2,1)S(1)}, bf16[2,128,1024]{2,1,0:T(8,128)(2,1)S(1)}) custom-call(bf16[4,2,128,1024]{3,2,1,0:T(8,128)(2,1)S(1)} %copy-done.3, bf16[4,2,128,1024]{3,2,1,0:T(8,128)(2,1)S(1)} %copy-done.4), custom_call_target="tpu_custom_call" | custom-call | tf_op jit(solution)/shard_map/pallas_call | solution.py:363
  585.2 3.1 fusion.3
  588.4 3.8 convolution_convert_fusion.1
  592.2 2.8 convolution_convert_fusion
  595.0 1.4 convolution_convert_fusion.2
  596.8 1.3 convolution_convert_fusion.3
  598.1 97.6 %shard_map.322 = (f32[32,1024]{1,0:T(8,128)S(1)}, f32[32,1024]{1,0:T(8,128)S(1)}, f32[32,1024]{1,0:T(8,128)S(1)}, f32[32,1024]{1,0:T(8,128)S(1)}, f32[8,128]{1,0:T(8,128)S(1)}) custom-call(bf16[2,2,4,2,32,1024]{5,4,3,2,1,0:T(8,128)(2,1)S(1)} %bitcast.106, bf16[2,2,4,2,32,1024]{5,4,3,2,1,0:T(8,128)(2,1)S(1)} %bitcast.105, ...), custom_call_target="tpu_custom_call" | custom-call | tf_op jit(solution)/shard_map/pallas_call | solution.py:168
  697.7 2.2 fusion.57
  699.9 2.1 fusion.5
  702.1 1.5 fusion.56
  703.5 3.1 convert_element_type.160
  706.7 3.1 convert_element_type.161
  709.8 3.1 convert_element_type.162
  (173 shorter events, 24.0 us)
Async XLA Ops:
  7.2 71.4 %copy-start.14 = (bf16[2,128,1024]{2,1,0:T(8,128)(2,1)S(1)}, bf16[2,128,1024]{2,1,0:T(8,128)(2,1)}, u32[]{:S(2)}) copy-start(bf16[2,128,1024]{2,1,0:T(8,128)(2,1)} %param.24) | copy-start | bytes 1572868
  7.2 71.3 %copy-start.18 = (bf16[2,128,1024]{2,1,0:T(8,128)(2,1)S(1)}, bf16[2,128,1024]{2,1,0:T(8,128)(2,1)}, u32[]{:S(2)}) copy-start(bf16[2,128,1024]{2,1,0:T(8,128)(2,1)} %param.23) | copy-start | bytes 1572868
  7.2 696.3 %reduce-scatter.4.cloned.1.call-start = ((), (), s32[]{:S(2)}) async-start(), calls=%async_computation.3 | async-start | bytes 7208960 | tf_op jit(solution)/shard_map/reduce_scatter | solution.py:629
  78.8 4.0 copy-start.33
  82.9 1.6 copy-start.30
  84.2 2.6 copy-start
  84.5 1.4 copy-start.29
  85.8 31.7 %copy-start.1 = (bf16[512,1024]{1,0:T(8,128)(2,1)}, bf16[512,1024]{1,0:T(8,128)(2,1)S(1)}, u32[]{:S(2)}) copy-start(bf16[512,1024]{1,0:T(8,128)(2,1)S(1)} %convolution_convert_fusion.5.refs_1_.v) | copy-start | bytes 3145732
  115.6 1.3 copy-start.2
  117.5 26.3 %copy-start.15 = (bf16[2,128,1024]{2,1,0:T(8,128)(2,1)S(1)}, bf16[2,128,1024]{2,1,0:T(8,128)(2,1)}, u32[]{:S(2)}) copy-start(bf16[2,128,1024]{2,1,0:T(8,128)(2,1)} %param.24) | copy-start | bytes 1572868
  117.5 26.3 %copy-start.19 = (bf16[2,128,1024]{2,1,0:T(8,128)(2,1)S(1)}, bf16[2,128,1024]{2,1,0:T(8,128)(2,1)}, u32[]{:S(2)}) copy-start(bf16[2,128,1024]{2,1,0:T(8,128)(2,1)} %param.23) | copy-start | bytes 1572868
  117.5 26.3 %copy-start.35 = (bf16[2,2,4,2,32,1024]{5,4,3,2,1,0:T(8,128)(2,1)S(1)}, bf16[2,2,4,2,32,1024]{5,4,3,2,1,0:T(8,128)(2,1)}, u32[]{:S(2)}) copy-start(bf16[2,2,4,2,32,1024]{5,4,3,2,1,0:T(8,128)(2,1)} %get-tuple-element.47) | copy-start | bytes 6291460
  143.8 2.9 copy-start.23
  143.8 2.9 copy-start.25
  146.5 10.3 %copy-start.9 = (f32[512,1024]{1,0:T(8,128)}, f32[512,1024]{1,0:T(8,128)S(1)}, u32[]{:S(2)}) copy-start(f32[512,1024]{1,0:T(8,128)S(1)} %get-tuple-element.152) | copy-start | bytes 6291460
  157.0 19.7 %copy-start.5 = (bf16[512,1024]{1,0:T(8,128)(2,1)}, bf16[512,1024]{1,0:T(8,128)(2,1)S(1)}, u32[]{:S(2)}) copy-start(bf16[512,1024]{1,0:T(8,128)(2,1)S(1)} %multiply_convert_fusion.1) | copy-start | bytes 3145732
  423.9 282.8 %reduce-scatter.6.cloned.1.call-start = ((), (), s32[]{:S(2)}) async-start(), calls=%async_computation.4 | async-start | bytes 7208960 | tf_op jit(solution)/shard_map/reduce_scatter | solution.py:629
  437.6 272.2 %reduce-scatter.8.cloned.1.call-start = ((), (), s32[]{:S(2)}) async-start(), calls=%async_computation.5 | async-start | bytes 7208960 | tf_op jit(solution)/shard_map/reduce_scatter | solution.py:629
  437.6 1.7 copy-start.8
  444.7 4.0 copy-start.7
  471.7 8.5 %copy-start.10 = (f32[512,1024]{1,0:T(8,128)S(1)}, f32[512,1024]{1,0:T(8,128)}, u32[]{:S(2)}) copy-start(f32[512,1024]{1,0:T(8,128)} %copy-done.9) | copy-start | bytes 6291460
  480.2 2.2 copy-start.11
  482.4 3.2 copy-start.24
  482.4 3.3 copy-start.26
  485.7 3.8 copy-start.36
  488.2 1.3 copy-start.12
  491.8 41.5 %copy-start.6 = (bf16[512,1024]{1,0:T(8,128)(2,1)S(1)}, bf16[512,1024]{1,0:T(8,128)(2,1)}, u32[]{:S(2)}) copy-start(bf16[512,1024]{1,0:T(8,128)(2,1)} %copy-done.5) | copy-start | bytes 3145732
  533.3 0.8 copy-start.28
  533.3 1.7 copy-start.3
  535.1 1.6 copy-start.4
  536.7 44.6 %copy-start.34 = (bf16[2,2,4,2,32,1024]{5,4,3,2,1,0:T(8,128)(2,1)S(1)}, bf16[2,2,4,2,32,1024]{5,4,3,2,1,0:T(8,128)(2,1)}, u32[]{:S(2)}) copy-start(bf16[2,2,4,2,32,1024]{5,4,3,2,1,0:T(8,128)(2,1)} %get-tuple-element.43) | copy-start | bytes 6291460
  536.7 44.7 %copy-start.40 = (bf16[256,1024]{1,0:T(8,128)(2,1)S(1)}, bf16[256,1024]{1,0:T(8,128)(2,1)}, u32[]{:S(2)}) copy-start(bf16[256,1024]{1,0:T(8,128)(2,1)} %get-tuple-element.54) | copy-start | bytes 1572868
  581.3 1.6 copy-start.32
  581.3 1.8 copy-start.37
  583.2 1.3 copy-start.16
  583.2 1.3 copy-start.20
  583.2 1.9 copy-start.31
  583.2 2.0 copy-start.39
  592.2 2.8 copy-start.21
  592.2 2.8 copy-start.38
  594.9 1.6 copy-start.13
  594.9 1.9 copy-start.27
  695.7 4.2 copy-start.17
  697.1 2.8 copy-start.22
Sparse Core Ops, SparseCore 0:
  424.0 94.6 reduce-scatter.3
  521.4 73.7 reduce-scatter.5
  597.8 68.5 reduce-scatter.7

commit v4 on v3

--- a/solution.py
+++ b/solution.py
@@ -373,28 +373,29 @@
     t = jnp.tanh(c * v * (1.0 + a * v2))
     half = 0.5 * (1.0 + t)
     return v * half, half + 0.5 * v * (1.0 - t * t) * (c * (1.0 + 3.0 * a * v2))
-def expert_kernel(cap, per, order, wcut, tile, xs, gs, wgi, wui, wdi, eo_out, ri_out, dg_out, du_out, dd_out,
-                  wg, wu, wd, xr, gr, hid, gg, ug, eo, ri, xt, gt, stage,
-                  lsem, xss, xrs, gss, grs, ess, ers, rss, rrs, wss, wrs, wls, osem, ssem):
+RING, LAG = 6, 4
+def expert_kernel(cap, per, order, todo, wcut, tile, whole_down, xs, gs, wgi, wui, wdi, eo_out, ri_out, grads, eo_h, ri_h,
+                  wall, xr, gr, hall, lall, eo, ri, cb, ab, xb, ob,
+                  lsem, xss, xrs, gss, grs, ess, ers, rss, rrs, wss, wrs, wls, css, crs, ass, ars, osem, free):
     dp = lax.axis_size("dp")
     f32, bf = jnp.float32, jnp.bfloat16
     s, x, c, xdev, cdev = seq_places(2)
     g = lax.axis_index("dp")
     def peer(k): return (s, g ^ k)
     greet([xdev, cdev] + [peer(k) for k in range(1, dp)])
-    rows_w = wgi.shape[0]; ff = wgi.shape[1]; width = xs.shape[2]
+    rows_w, ff = wgi.shape; width = xs.shape[2]
     piece = rows_w // wcut
-    own, far = s * rows_w, ((1 - x) * 2 + c) * rows_w
-    mats = ((wgi, wg), (wui, wu), (wdi, wd))
     wx, wc, wl = [], [], []
-    for h in range(wcut):
-        for m, (src, dst) in enumerate(mats):
-            n = len(wx)
-            a = src.at[pl.ds(h * piece, piece)]
-            b = dst.at[pl.ds(own + h * piece, piece)]
-            wx.append(remote(a, b, wss.at[n, 0], wrs.at[n, 0], xdev))
-            wc.append(remote(a, b, wss.at[n, 1], wrs.at[n, 1], cdev))
-            cp = pltpu.make_async_copy(a, b, wls.at[n]); cp.start(); wl.append(cp)
+    shared = ((wgi, 1), (wui, 2)) if whole_down else ((wgi, 1), (wui, 2), (wdi, 0))
+    parts = [(src, m, h * piece) for h in range(wcut) for src, m in shared]
+    for n, (src, m, r0) in enumerate(parts):
+        a = src.at[pl.ds(r0, piece)]
+        b = wall.at[m, x, c, pl.ds(r0, piece)]
+        wx.append(remote(a, b, wss.at[n, 0], wrs.at[n, 0], xdev))
+        wc.append(remote(a, b, wss.at[n, 1], wrs.at[n, 1], cdev))
+        cp = pltpu.make_async_copy(a, b, wls.at[n]); cp.start(); wl.append(cp)
+    if whole_down:
+        cp = pltpu.make_async_copy(wdi, wall.at[0], wls.at[len(parts)]); cp.start(); wl.append(cp)
     sx, sg = {}, {}
     for k in [k for p in order for k in range(p * per, (p + 1) * per)]:
         at = pl.ds(k * cap, cap)
@@ -405,17 +406,17 @@
             sx[k] = remote(xs.at[g ^ k], xr.at[at], xss.at[k], xrs.at[k], peer(k))
             sg[k] = remote(gs.at[g ^ k], gr.at[at], gss.at[k], grs.at[k], peer(k))
     wf = []
-    for h in range(wcut):
-        for m, (src, dst) in enumerate(mats):
-            n = len(wf)
-            wx[n].wait_recv()
-            b = dst.at[pl.ds(far + h * piece, piece)]
-            wf.append(remote(b, b, wss.at[n, 2], wrs.at[n, 2], cdev))
-    for n in range(len(wf)):
-        wl[n].wait(); wc[n].wait_recv(); wf[n].wait_recv()
+    for n, (src, m, r0) in enumerate(parts):
+        wx[n].wait_recv()
+        b = wall.at[m, 1 - x, c, pl.ds(r0, piece)]
+        wf.append(remote(b, b, wss.at[n, 2], wrs.at[n, 2], cdev))
+    for cp in wl: cp.wait()
+    for n in range(len(parts)):
+        wc[n].wait_recv(); wf[n].wait_recv()
     ntile = ff // tile
     re, rr = {}, {}
-    for p in order:
+    wide = 4 * rows_w
+    for p in todo:
         ks = list(range(p * per, (p + 1) * per))
         for k in ks:
             if k == 0: sx[0].wait(); sg[0].wait()
@@ -424,42 +425,91 @@
         @pl.loop(0, ntile)
         def _(t):
             cols = pl.ds(pl.multiple_of(t * tile, 128), tile)
-            gp = jnp.dot(xr[rows, :], wg[:, cols], preferred_element_type=f32)
-            up = jnp.dot(xr[rows, :], wu[:, cols], preferred_element_type=f32)
-            hg = jnp.dot(gr[rows, :], wd[:, cols], preferred_element_type=f32)
+            w = lambda m: wall[m, :, :, :, cols].reshape(wide, tile)
+            gp = jnp.dot(xr[rows, :], w(1), preferred_element_type=f32)
+            up = jnp.dot(xr[rows, :], w(2), preferred_element_type=f32)
+            hg = jnp.dot(gr[rows, :], w(0), preferred_element_type=f32)
             act, der = gelu_parts(gp)
-            hid[rows, cols] = (act * up).astype(bf)
-            gg[rows, cols] = (hg * up * der).astype(bf)
-            ug[rows, cols] = (hg * act).astype(bf)
-        @pl.loop(0, width // 256)
+            hall[0, rows, cols] = (act * up).astype(bf)
+            hall[1, rows, cols] = (hg * up * der).astype(bf)
+            hall[2, rows, cols] = (hg * act).astype(bf)
+        @pl.loop(0, 4)
         def _(t):
-            part = pl.ds(pl.multiple_of(t * 256, 256), 256)
-            eo[rows, part] = dot(hid[rows, :], wd[part, :], 1, 1).astype(bf)
-            ri[rows, part] = (dot(gg[rows, :], wg[part, :], 1, 1) + dot(ug[rows, :], wu[part, :], 1, 1)).astype(bf)
+            part = pl.ds(pl.multiple_of(t * rows_w, 128), rows_w)
+            tx, tc = t // 2, lax.rem(t, 2)
+            eo[:, part] = dot(hall[0, rows, :], wall[0, tx, tc], 1, 1).astype(bf)
+            ri[:, part] = (dot(hall[1, rows, :], wall[1, tx, tc], 1, 1) + dot(hall[2, rows, :], wall[2, tx, tc], 1, 1)).astype(bf)
+        keep = [pltpu.make_async_copy(eo, eo_h.at[rows], lsem.at[4]), pltpu.make_async_copy(ri, ri_h.at[rows], lsem.at[5])]
+        for cp in keep: cp.start()
+        for cp in keep: cp.wait()
         for k in ks:
             at = pl.ds(k * cap, cap)
             if k == 0:
-                re[0] = pltpu.make_async_copy(eo.at[at], eo_out.at[g], lsem.at[2]); re[0].start()
-                rr[0] = pltpu.make_async_copy(ri.at[at], ri_out.at[g], lsem.at[3]); rr[0].start()
+                re[0] = pltpu.make_async_copy(eo_h.at[at], eo_out.at[g], lsem.at[2]); re[0].start()
+                rr[0] = pltpu.make_async_copy(ri_h.at[at], ri_out.at[g], lsem.at[3]); rr[0].start()
             else:
-                re[k] = remote(eo.at[at], eo_out.at[g], ess.at[k], ers.at[k], peer(k))
-                rr[k] = remote(ri.at[at], ri_out.at[g], rss.at[k], rrs.at[k], peer(k))
+                re[k] = remote(eo_h.at[at], eo_out.at[g], ess.at[k], ers.at[k], peer(k))
+                rr[k] = remote(ri_h.at[at], ri_out.at[g], rss.at[k], rrs.at[k], peer(k))
+    for n in range(len(parts)):
+        wx[n].wait_send(); wc[n].wait_send(); wf[n].wait_send()
     total = dp * cap
     @pl.loop(0, total // 256)
     def _(t):
         at = pl.ds(pl.multiple_of(t * 256, 256), 256)
-        xt[:, at] = xr[at, :].T
-        gt[:, at] = gr[at, :].T
-    for m, (lhs, rhs, out) in enumerate(((gt, hid, dd_out), (xt, gg, dg_out), (xt, ug, du_out))):
-        @pl.loop(0, ntile)
-        def _(t):
-            cols = pl.ds(pl.multiple_of(t * tile, 128), tile)
-            res = jnp.dot(lhs[...], rhs[:, cols], preferred_element_type=f32).astype(bf)
-            stage[...] = res
-            cp = pltpu.make_async_copy(stage, out.at[:, cols], osem.at[0])
-            cp.start(); cp.wait()
-    for n in range(len(wf)):
-        wx[n].wait_send(); wc[n].wait_send(); wf[n].wait_send()
+        lall[1, :, at] = xr[at, :].T
+        lall[0, :, at] = gr[at, :].T
+    nt = 3 * ntile
+    def place(n):
+        m = n // ntile
+        return m, pl.ds(pl.multiple_of((n - m * ntile) * tile, 128), tile)
+    def to_core(n):
+        m, cols = place(n); r = lax.rem(n, RING)
+        return pltpu.make_async_remote_copy(src_ref=wall.at[m, :, 1 - c, :, cols], dst_ref=cb.at[r], send_sem=css.at[r],
+            recv_sem=crs.at[r], device_id=cdev, device_id_type=MESH)
+    def to_chip(n):
+        r = lax.rem(n, RING)
+        return pltpu.make_async_remote_copy(src_ref=ab.at[r], dst_ref=xb.at[r], send_sem=ass.at[r],
+            recv_sem=ars.at[r], device_id=xdev, device_id_type=MESH)
+    def to_out(n):
+        m, cols = place(n); r = lax.rem(n, 2)
+        return pltpu.make_async_copy(ob.at[r], grads.at[m, :, cols], osem.at[r])
+    @pl.loop(0, nt + LAG)
+    def _(n):
+        @pl.when(n < nt)
+        def _():
+            m, cols = place(n)
+            res = jnp.dot(lall[jnp.minimum(m, 1)], hall[m, :, cols], preferred_element_type=f32)
+            wall[m, :, :, :, cols] = res.astype(bf).reshape(2, 2, rows_w, tile)
+            @pl.when(n >= RING)
+            def _(): pl.semaphore_wait(free.at[0], 1)
+            to_core(n).start()
+        @pl.when((n >= 1) & (n <= nt))
+        def _():
+            i = n - 1
+            m, cols = place(i); r = lax.rem(i, RING)
+            to_core(i).wait_recv()
+            @pl.when(i >= RING)
+            def _():
+                to_chip(i).wait_send()
+                pl.semaphore_wait(free.at[1], 1)
+            ab[r] = (wall[m, 1 - x, c, :, cols].astype(f32) + cb[r, 1 - x].astype(f32)).astype(bf)
+            to_chip(i).start()
+        @pl.when(n >= LAG)
+        def _():
+            j = n - LAG
+            m, cols = place(j); r = lax.rem(j, RING)
+            to_chip(j).wait_recv()
+            to_core(j).wait_send()
+            @pl.when(j >= 2)
+            def _(): to_out(j).wait()
+            ob[lax.rem(j, 2)] = wall[m, x, c, :, cols].astype(f32) + cb[r, x].astype(f32) + xb[r].astype(f32)
+            to_out(j).start()
+            @pl.when(j < nt - RING)
+            def _():
+                pl.semaphore_signal(free.at[0], inc=1, device_id=cdev, device_id_type=MESH)
+                pl.semaphore_signal(free.at[1], inc=1, device_id=xdev, device_id_type=MESH)
+    for j in range(nt - 2, nt): to_out(j).wait()
+    for i in range(nt - RING, nt): to_chip(i).wait_send()
     for k in range(dp):
         if k == 0:
             re[0].wait(); rr[0].wait()
@@ -467,27 +517,30 @@
             sx[k].wait_send(); sg[k].wait_send(); re[k].wait(); rr[k].wait()
 def expert_all(xs, gs, wg, wu, wd, seq, cid):
     dp, cap, width = xs.shape
-    ff = wg.shape[1]; total = dp * cap
+    rows_w, ff = wg.shape; total = dp * cap
+    whole_down = wd.shape[0] != rows_w
+    if whole_down: wd = wd.reshape(seq // 2, 2, rows_w, ff)
     group = 320
     per = group // cap
     ng = dp // per
     order = [p for p in range(ng // 2, ng)] + [p for p in range(ng // 2 - 1, -1, -1)]
+    todo = list(range(ng))
     sem = pltpu.SemaphoreType.DMA
     bf = jnp.bfloat16
     any_ = pl.BlockSpec(memory_space=pl.ANY)
     V = pltpu.VMEM
     tile = 256
     wcut = 2
-    full = (seq * wg.shape[0], ff)
     back = jax.ShapeDtypeStruct((dp, cap, width), bf)
-    loc = jax.ShapeDtypeStruct(full, bf)
-    return pl.pallas_call(functools.partial(expert_kernel, cap, per, order, wcut, tile),
-        out_shape=[back, back, loc, loc, loc],
+    flat = jax.ShapeDtypeStruct((total, width), bf)
+    return pl.pallas_call(functools.partial(expert_kernel, cap, per, order, todo, wcut, tile, whole_down),
+        out_shape=[back, back, jax.ShapeDtypeStruct((3, rows_w, ff), jnp.float32), flat, flat],
         in_specs=[any_] * 5, out_specs=[any_] * 5,
-        scratch_shapes=[V(full, bf)] * 3 + [V((total, width), bf)] * 2 + [V((total, ff), bf)] * 3 + [V((total, width), bf)] * 2
-        + [V((width, total), bf)] * 2 + [V((width, tile), bf)]
-        + [sem((4,))] + [sem((dp,))] * 8 + [sem((3 * wcut, 3))] * 2 + [sem((3 * wcut,)), sem((1,)), sem((1,))],
-        compiler_params=pltpu.CompilerParams(collective_id=cid, has_side_effects=True, vmem_limit_bytes=63 * 2**20))(xs, gs, wg, wu, wd)
+        scratch_shapes=[V((3, seq // 2, 2, rows_w, ff), bf), V((total, width), bf), V((total, width), bf), V((3, total, ff), bf),
+        V((2, width, total), bf), V((group, width), bf), V((group, width), bf),
+        V((RING, seq // 2, rows_w, tile), bf), V((RING, rows_w, tile), bf), V((RING, rows_w, tile), bf), V((2, rows_w, tile), jnp.float32)]
+        + [sem((6,))] + [sem((dp,))] * 8 + [sem((3 * wcut, 3))] * 2 + [sem((3 * wcut + 1,))] + [sem((RING,))] * 4 + [sem((2,)), pltpu.SemaphoreType.REGULAR((2,))],
+        compiler_params=pltpu.CompilerParams(collective_id=cid, has_side_effects=True, vmem_limit_bytes=63 * 2**20))(xs, gs, wg, wu, wd)[:3]
 
 
 def on_device(
@@ -606,8 +659,10 @@
     out_slots = jnp.where(slot_used[:, None], jnp.take(pair_grad, slot_pair, axis=0), 0).reshape(
         experts, capacity, model_width
     )
-    back_rows, returned_grad, gate_local, up_local, down_local = expert_all(
-        outgoing, out_slots, gate_weight[0], up_weight[0], down_weight[0], seq_size, 4
+    later_down, unused_keys = lax.optimization_barrier((down_weight[0], long_keys))
+    down_full = lax.all_gather(later_down, "seq", axis=0, tiled=True)
+    back_rows, returned_grad, expert_grads = expert_all(
+        outgoing, out_slots, gate_weight[0], up_weight[0], down_full, seq_size, 4
     )
     pair_out = (
         jnp.where(
@@ -625,10 +680,7 @@
     share_grad = kept_two * jnp.sum(grad_out[:, None, :] * pair_out, axis=-1)
     logit_grad = gate_pull(share_grad)[0].astype(jnp.bfloat16)
     attn_back = attn_set
-    gate_grad, up_grad, down_grad = (
-        lax.psum_scatter(part[None], "seq", scatter_dimension=1, tiled=True).astype(jnp.float32)
-        for part in (gate_local, up_local, down_local)
-    )
+    down_grad, gate_grad, up_grad = (expert_grads[m : m + 1] for m in range(3))
     route_grad = (
         jnp.where(
             route_kept[:, None],

time: 726 us -> 675 us (0.930)
  Pallas kernels: 534 us -> 482 us
  starting transfers between devices: 13.7 us -> 0.04 us
  matrix products: 28.5 us -> 38.9 us
  other arithmetic: 36.3 us -> 27.7 us
  local copies, waits for them, and re-layouts: 94.4 us -> 103 us
    pallas_call x1, Pallas kernels: 97.6 us -> 68.5 us  [scatter_all(): pl.pallas_call(functools.partial(scatter_kernel, dims, pieces, n), out_sh...]
    pallas_call x1, Pallas kernels: 44.6 us -> 25.8 us  [seq_sum(): pl.pallas_call(functools.partial(seq_sum_kernel, n, items), out_shape=[ja...]
    reduce_scatter x3 -> x0, starting transfers between devices: 13.7 us -> none  [on_device(): lax.psum_scatter(part[None], 'seq', scatter_dimension=1, tiled=True)]
    convert_element_type x3 -> x0, other arithmetic: 9.38 us -> none  [on_device(): lax.psum_scatter(part[None], 'seq', scatter_dimension=1, tiled=True)]
  transfers between devices with their start and end apart: 3 -> 1, of which waited for: 0 -> 0; matrix products, arithmetic and copies ran while one was open for 11% -> 8% of each run, Pallas kernels for 25% -> 4%
where the time goes in v4:
time: 675 us; the launch traced here: 668 us
  Pallas kernels  482 us (71%)
  local copies, waits for them, and re-layouts  103 us (15%)
  matrix products  38.9 us (6%)
  other arithmetic  27.7 us (4%)
  between operations  15.2 us (2%)
    pallas_call x1, Pallas kernels, expert_all(): pl.pallas_call(functools.partial(expert_kernel, cap, per, order, todo, wc...  231 us
    pallas_call x1, Pallas kernels, scatter_all(): pl.pallas_call(functools.partial(scatter_kernel, dims, pieces, n), out_sh...  68.5 us
    pallas_call x2, Pallas kernels, attention(): pl.pallas_call(body, out_shape=outs, in_specs=[sm, sm] + [vm] * (len(arra...  68 us
    pallas_call x1, Pallas kernels, gather_all(): pl.pallas_call(functools.partial(gather_kernel, dims, pieces, na), out_sh...  60.1 us
    pallas_call x1, Pallas kernels, seq_gather(): pl.pallas_call(functools.partial(seq_gather_kernel, n, items, rows), out_...  28.8 us
    pallas_call x1, Pallas kernels, seq_sum(): pl.pallas_call(functools.partial(seq_sum_kernel, n, items), out_shape=[ja...  25.8 us
    unnamed x88, local copies, waits for them, and re-layouts  14.1 us
  transfers between devices with their start and end apart: 1, of which 0 were waited for; matrix products, arithmetic and copies ran while one was open for 8% of the time, Pallas kernels for 4%

profile of v4, /device:TPU:0, one launch (start us, length us, event | category | flops | bytes accessed | tf_op | source)
XLA Modules:
  0.0 667.5 jit_solution(15255784940222411937)
XLA Ops:
  7.2 1.5 fusion.6
  9.6 1.4 fusion.37.refs_4_
  10.9 60.1 %shard_map.316 = (bf16[2,2,4,2,32,1024]{5,4,3,2,1,0:T(8,128)(2,1)}, bf16[2,2,4,2,32,1024]{5,4,3,2,1,0:T(8,128)(2,1)}, bf16[2,2,4,2,32,1024]{5,4,3,2,1,0:T(8,128)...) custom-call(bf16[32,1024]{1,0:T(8,128)(2,1)} %refs_0_.1, bf16[32,1024]{1,0:T(8,128)(2,1)} %refs_1_.1, ...), custom_call_target="tpu_custom_call" | custom-call | tf_op jit(solution)/shard_map/pallas_call | solution.py:95
  72.1 3.4 convolution_convert_fusion.5.refs_1_.v
  75.5 1.3 convolution_convert_fusion.6.refs_0_.k
  76.9 28.8 %shard_map.317 = (bf16[4,2,128,1024]{3,2,1,0:T(8,128)(2,1)S(1)}, bf16[4,2,128,1024]{3,2,1,0:T(8,128)(2,1)}) custom-call(bf16[512,1024]{1,0:T(8,128)(2,1)S(1)} %convolution_convert_fusion.6.refs_0_.k, bf16[512,1024]{1,0:T(8,128)(2,1)S(1)} %convolution_convert_fusion.5.refs_1_.v), custom_call_target="tpu_custom_call" | custom-call | tf_op jit(solution)/shard_map/pallas_call | solution.py:331
  105.8 1.3 copy-done.2
  110.5 2.3 reduce-window.6
  115.0 4.3 scatter_custom_fusion.1
  119.4 3.9 convolution_convert_fusion.7.q
  123.2 26.4 %shard_map.318 = bf16[512,1024]{1,0:T(8,128)(2,1)} custom-call(s32[2]{0:T(128)} %ll.3, s32[2]{0:T(128)} %sl.3, bf16[512,1024]{1,0:T(8,128)(2,1)} %convolution_convert_fusion.7.q, bf16[512,1024]{1,0:T(8,128)(2,1)} %copy-done.1, bf16[512,1024]{1,0:T(8,128)(2,1)} %copy-done, bf16[4,2,128,1024]{3,2,1,0:T(8,128)(2,1)} %copy-done.2, ...), custom_call_target="tpu_custom_call" | custom-call | tf_op jit(solution)/shard_map/pallas_call | solution.py:291
  149.7 2.6 multiply_reduce_fusion.3
  152.3 1.3 copy-done.10
  153.9 5.1 gather_fusion
  160.4 3.4 mul.257
  163.8 6.1 mul.258
  170.0 4.3 scatter_custom_fusion
  174.4 2.5 multiply_convert_fusion
  176.9 5.5 gather_fusion.1
  182.4 4.5 select_select_fusion
  186.9 231.3 %shard_map.319 = (bf16[8,160,1024]{2,1,0:T(8,128)(2,1)}, bf16[8,160,1024]{2,1,0:T(8,128)(2,1)}, f32[3,256,2816]{2,1,0:T(8,128)}, bf16[1280,1024]{1,0:T(8,128)(2,1)}, bf16[1280,1024]{1,0:T(8,128)(2,1)}) custom-call(bf16[8,160,1024]{2,1,0:T(8,128)(2,1)} %get-tuple-element.151.xs, bf16[8,160,1024]{2,1,0:T(8,128)(2,1)} %get-tuple-element.150.gs, ...), custom_call_target="tpu_custom_call" | custom-call | tf_op jit(solution)/shard_map/pallas_call | solution.py:536
  418.3 8.2 %gather_fusion.3 = bf16[1024,1024]{1,0:T(8,128)(2,1)} fusion(bf16[1280,1024]{1,0:T(8,128)(2,1)} %bitcast.113, s32[1024]{0:T(1024)S(1)} %get-tuple-element.144), kind=kCustom, calls=%fused_computation.1.clone | custom fusion | bytes 4198400 | tf_op jit(solution)/shard_map/jit(_take)/gather | solution.py:687
  426.5 5.3 gather_fusion.2
  431.8 3.6 multiply_reduce_fusion
  435.9 4.3 fusion.15
  440.2 5.8 reshape.435
  446.0 9.2 %fusion.55 = (f32[512,1,1024]{2,1,0:T(1,128)}, f32[512,1,1024]{2,1,0:T(1,128)}) fusion(f32[512,2,1024]{2,1,0:T(2,128)} %reshape.435), kind=kLoop, calls=%fused_computation.149 | loop fusion | bytes 8388608 | tf_op jit(solution)/shard_map/slice | solution.py:694
  455.7 4.7 multiply_reduce_fusion.1
  460.4 5.8 reshape.434
  466.3 7.2 %fusion.56 = (f32[512,1,1024]{2,1,0:T(1,128)S(1)}, f32[512,1,1024]{2,1,0:T(1,128)S(1)}) fusion(f32[512,2,1024]{2,1,0:T(2,128)} %reshape.434), kind=kLoop, calls=%fused_computation.150 | loop fusion | bytes 8388608 | tf_op jit(solution)/shard_map/slice | solution.py:676
  473.5 2.7 fusion.4
  476.2 2.4 convolution_convert_fusion.4.mg
  478.6 41.5 %shard_map.320 = (bf16[512,1024]{1,0:T(8,128)(2,1)}, bf16[256,1024]{1,0:T(8,128)(2,1)}, bf16[256,1024]{1,0:T(8,128)(2,1)}, bf16[4,2,128,1024]{3,2,1,0:T(8,128)(2...) custom-call(s32[2]{0:T(128)} %ll.3, s32[2]{0:T(128)} %sl.3, ...), custom_call_target="tpu_custom_call" | custom-call | tf_op jit(solution)/shard_map/pallas_call | solution.py:291
  522.4 1.6 copy-done.3
  524.0 1.6 copy-done.4
  525.6 25.8 %shard_map.321 = (bf16[2,128,1024]{2,1,0:T(8,128)(2,1)S(1)}, bf16[2,128,1024]{2,1,0:T(8,128)(2,1)S(1)}) custom-call(bf16[4,2,128,1024]{3,2,1,0:T(8,128)(2,1)S(1)} %copy-done.3, bf16[4,2,128,1024]{3,2,1,0:T(8,128)(2,1)S(1)} %copy-done.4), custom_call_target="tpu_custom_call" | custom-call | tf_op jit(solution)/shard_map/pallas_call | solution.py:363
  551.4 2.6 fusion.17
  554.0 2.7 convolution_convert_fusion.1
  558.7 2.6 fusion.63
  561.3 2.7 convolution_convert_fusion.2
  564.2 4.1 convolution_convert_fusion
  568.3 3.0 fusion.3
  571.4 1.3 reshape.428
  572.9 1.6 copy-done.5
  574.5 68.5 %shard_map.322 = (f32[32,1024]{1,0:T(8,128)S(1)}, f32[32,1024]{1,0:T(8,128)S(1)}, f32[32,1024]{1,0:T(8,128)S(1)}, f32[32,1024]{1,0:T(8,128)S(1)}, f32[8,128]{1,0:T(8,128)S(1)}) custom-call(bf16[2,2,4,2,32,1024]{5,4,3,2,1,0:T(8,128)(2,1)S(1)} %bitcast.103, bf16[2,2,4,2,32,1024]{5,4,3,2,1,0:T(8,128)(2,1)S(1)} %bitcast.104, ...), custom_call_target="tpu_custom_call" | custom-call | tf_op jit(solution)/shard_map/pallas_call | solution.py:168
  644.9 2.8 fusion.5
  647.8 1.5 fusion.57
  650.4 7.2 %fusion.54 = (f32[1,256,2816]{2,1,0:T(8,128)}, f32[1,256,2816]{2,1,0:T(8,128)}, f32[1,256,2816]{2,1,0:T(8,128)}) fusion(f32[3,256,2816]{2,1,0:T(8,128)} %get-tuple-element.63), kind=kLoop, calls=%fused_computation.148 | loop fusion | bytes 17301504 | tf_op jit(solution)/shard_map/slice | solution.py:683
  (163 shorter events, 20.8 us)
Async XLA Ops:
  7.2 179.7 %all-gather.2.cloned.1.call-start = ((), (), s32[]{:S(2)}) async-start(), calls=%async_computation | async-start | bytes 7208960 | tf_op jit(solution)/shard_map/all_gather | solution.py:663
  72.1 3.4 copy-start.16
  72.1 3.4 copy-start.17
  72.1 3.4 copy-start.31
  75.5 1.3 copy-start
  76.8 32.2 %copy-start.1 = (bf16[512,1024]{1,0:T(8,128)(2,1)}, bf16[512,1024]{1,0:T(8,128)(2,1)S(1)}, u32[]{:S(2)}) copy-start(bf16[512,1024]{1,0:T(8,128)(2,1)S(1)} %convolution_convert_fusion.6.refs_0_.k) | copy-start | bytes 3145732
  76.8 30.2 %copy-start.25 = (s32[2,512]{1,0:T(2,128)S(1)}, s32[2,512]{1,0:T(2,128)}, u32[]{:S(2)}) copy-start(s32[2,512]{1,0:T(2,128)} %param.38) | copy-start | bytes 12292
  76.9 32.0 %copy-start.27 = (s32[2,128,2]{1,2,0:T(2,128)S(1)}, s32[2,128,2]{1,2,0:T(2,128)}, u32[]{:S(2)}) copy-start(s32[2,128,2]{1,2,0:T(2,128)} %param.43) | copy-start | bytes 6148
  76.9 32.0 %copy-start.28 = (s32[2,128,2]{1,2,0:T(2,128)S(1)}, s32[2,128,2]{1,2,0:T(2,128)}, u32[]{:S(2)}) copy-start(s32[2,128,2]{1,2,0:T(2,128)} %param.42) | copy-start | bytes 6148
  76.9 32.7 %copy-start.26 = (s32[2,128]{1,0:T(2,128)S(1)}, s32[2,128]{1,0:T(2,128)}, u32[]{:S(2)}) copy-start(s32[2,128]{1,0:T(2,128)} %param.39) | copy-start | bytes 3076
  105.7 1.3 copy-start.2
  123.2 26.5 %copy-start.33 = (bf16[2,2,4,2,32,1024]{5,4,3,2,1,0:T(8,128)(2,1)S(1)}, bf16[2,2,4,2,32,1024]{5,4,3,2,1,0:T(8,128)(2,1)}, u32[]{:S(2)}) copy-start(bf16[2,2,4,2,32,1024]{5,4,3,2,1,0:T(8,128)(2,1)} %get-tuple-element.46) | copy-start | bytes 6291460
  152.3 1.3 copy-start.10
  153.8 5.1 copy-start.6
  158.9 1.0 copy-start.20
  158.9 1.2 copy-start.22
  418.3 8.2 %copy-start.8 = (bf16[8,160,1024]{2,1,0:T(8,128)(2,1)S(1)}, bf16[8,160,1024]{2,1,0:T(8,128)(2,1)}, u32[]{:S(2)}) copy-start(bf16[8,160,1024]{2,1,0:T(8,128)(2,1)} %get-tuple-element.48) | copy-start | bytes 7864324
  431.8 3.6 copy-start.9
  431.8 4.1 copy-start.14
  446.0 9.7 %copy-start.11 = (f32[512,1024]{1,0:T(8,128)S(1)}, f32[512,1024]{1,0:T(8,128)}, u32[]{:S(2)}) copy-start(f32[512,1024]{1,0:T(8,128)} %copy-done.10) | copy-start | bytes 6291460
  466.2 7.2 %copy-start.13 = (f32[512,1024]{1,0:T(8,128)S(1)}, f32[512,1024]{1,0:T(8,128)}, u32[]{:S(2)}) copy-start(f32[512,1024]{1,0:T(8,128)} %get-tuple-element.156) | copy-start | bytes 6291460
  466.2 7.2 %copy-start.21 = (bf16[2,128,1024]{2,1,0:T(8,128)(2,1)S(1)}, bf16[2,128,1024]{2,1,0:T(8,128)(2,1)}, u32[]{:S(2)}) copy-start(bf16[2,128,1024]{2,1,0:T(8,128)(2,1)} %param.26) | copy-start | bytes 1572868
  466.3 7.2 %copy-start.23 = (bf16[2,128,1024]{2,1,0:T(8,128)(2,1)S(1)}, bf16[2,128,1024]{2,1,0:T(8,128)(2,1)}, u32[]{:S(2)}) copy-start(bf16[2,128,1024]{2,1,0:T(8,128)(2,1)} %param.25) | copy-start | bytes 1572868
  473.5 2.7 copy-start.34
  476.2 80.6 %copy-start.12 = (f32[512,1024]{1,0:T(8,128)}, f32[512,1024]{1,0:T(8,128)S(1)}, u32[]{:S(2)}) copy-start(f32[512,1024]{1,0:T(8,128)S(1)} %get-tuple-element.113) | copy-start | bytes 6291460
  478.6 42.6 %copy-start.7 = (bf16[512,1024]{1,0:T(8,128)(2,1)S(1)}, bf16[512,1024]{1,0:T(8,128)(2,1)}, u32[]{:S(2)}) copy-start(bf16[512,1024]{1,0:T(8,128)(2,1)} %copy-done.6) | copy-start | bytes 3145732
  522.4 1.6 copy-start.3
  524.0 1.6 copy-start.4
  525.6 25.8 %copy-start.32 = (bf16[2,2,4,2,32,1024]{5,4,3,2,1,0:T(8,128)(2,1)S(1)}, bf16[2,2,4,2,32,1024]{5,4,3,2,1,0:T(8,128)(2,1)}, u32[]{:S(2)}) copy-start(bf16[2,2,4,2,32,1024]{5,4,3,2,1,0:T(8,128)(2,1)} %get-tuple-element.42) | copy-start | bytes 6291460
  525.6 25.8 %copy-start.37 = (bf16[256,1024]{1,0:T(8,128)(2,1)S(1)}, bf16[256,1024]{1,0:T(8,128)(2,1)}, u32[]{:S(2)}) copy-start(bf16[256,1024]{1,0:T(8,128)(2,1)} %get-tuple-element.54) | copy-start | bytes 1572868
  551.4 2.6 copy-start.18
  554.0 2.8 copy-start.24
  556.8 1.6 copy-start.30
  556.8 1.9 copy-start.35
  564.1 4.1 copy-start.19
  564.1 4.1 copy-start.29
  564.1 4.1 copy-start.36
  564.1 4.1 copy-start.38
  564.2 4.1 copy-start.39
  572.9 1.6 copy-start.5
  647.7 1.6 copy-start.15
Sparse Core Ops, SparseCore 0:
  107.2 43.2 all-gather.1

commit v5 on v4

--- a/solution.py
+++ b/solution.py
@@ -21,12 +21,6 @@
 def rms_norm(hidden, gain):
     scale = lax.rsqrt(jnp.mean(hidden * hidden, axis=-1, keepdims=True) + epsilon)
     return hidden * scale * gain
-
-
-def gate_values(logits, choose):
-    probs = jax.nn.softmax(logits, axis=-1)
-    chosen = jnp.sum(choose * probs[:, None, :], axis=-1)
-    return chosen / jnp.sum(chosen, axis=-1, keepdims=True)
 
 
 def gather_kernel(dims, pieces, na, *refs):
@@ -202,7 +196,14 @@
             fill_buckets(lb.at[b, c], lcol[b, me], lrow[b, c], ll[b], c * 128)
     for b in range(ns):
         fill_buckets(sb.at[b, 0], scol[b, 0], srow[b, 0], sl[b], 0)
-def attn_fwd_kernel(nl, ns, blocks, ll, sl, q, k, v, kl, vl, tab, lcol, lrow, scol, srow, mixed, lb, sb):
+def rows_of(long_ref, short_ref, t, nl, ns):
+    if t == 0:
+        return long_ref[...].reshape(nl * 128, -1)
+    return short_ref[...].reshape(ns * 128, -1)
+def rms_scale(mid):
+    return lax.rsqrt(jnp.mean(mid * mid, axis=-1, keepdims=True) + epsilon)
+def attn_fwd_kernel(nl, ns, blocks, experts, cap, ll, sl, q, k, v, kl, vl, tab, lcol, lrow, scol, srow,
+                    xl, xsh, gl, gsh, wo, gain, rt, rrow, mixed, mid, xs, gs, logits, lb, sb, n2, gb):
     attn_setup(nl, ns, blocks, ll, sl, lcol, lrow, scol, srow, lb, sb)
     first = lax.broadcasted_iota(jnp.int32, (128, 128), 1) < 64
     @pl.loop(0, 8)
@@ -215,11 +216,93 @@
                 kk = kl[:, b, :, cols].reshape(n * 128, 128); vv = vl[:, b, :, cols].reshape(n * 128, 128)
             else:
                 kk = k[rows, cols]; vv = v[rows, cols]
-            qq = q[rows, cols]
-            p = probs_of(stack_heads(qq, first), kk, (tab[2 * hp], tab[2 * hp + 1]), lb.at[b] if b < nl else sb.at[b - nl], n)
+            p = probs_of(stack_heads(q[rows, cols], first), kk, (tab[2 * hp], tab[2 * hp + 1]), lb.at[b] if b < nl else sb.at[b - nl], n)
             out = dot(p.astype(jnp.bfloat16), vv, 1, 0)
             mixed[rows, cols] = jnp.where(first, out[:128], out[128:]).astype(jnp.bfloat16)
-def attn_bwd_kernel(nl, ns, blocks, ll, sl, q, k, v, kl, vl, mg, tab, lcol, lrow, scol, srow, dq, dk, dv, dkl, dvl, seg, lb, sb, li, si):
+    f32, bf = jnp.float32, jnp.bfloat16
+    tokens = q.shape[0]
+    for t in range(2):
+        rows = pl.ds(t * 256, 256)
+        m = rows_of(xl, xsh, t, nl, ns).astype(f32) + jnp.dot(mixed[rows, :], wo[...], preferred_element_type=f32)
+        mid[rows, :] = m
+        n2[rows, :] = (m * rms_scale(m) * gain[...]).astype(bf)
+        gb[rows, :] = rows_of(gl, gsh, t, nl, ns)
+    logits[...] = dot(n2[...], rt[...], 1, 1)
+    logit_t = dot(rt[...], n2[...], 1, 1)[:experts]
+    e_iota = lax.broadcasted_iota(jnp.int32, (experts, tokens), 0)
+    member = ((e_iota == rrow[0:1, :]) | (e_iota == rrow[1:2, :])).astype(f32)
+    e = jnp.exp(logit_t - jnp.max(logit_t, axis=0, keepdims=True))
+    p = e / jnp.sum(e, axis=0, keepdims=True)
+    chosen = member * p
+    before = (lax.broadcasted_iota(jnp.int32, (tokens, tokens), 0) < lax.broadcasted_iota(jnp.int32, (tokens, tokens), 1)).astype(f32).astype(bf)
+    place = jnp.dot(member.astype(bf), before, preferred_element_type=f32)
+    kept = (member > 0.5) & (place < cap)
+    weight = jnp.where(kept, chosen / jnp.sum(chosen, axis=0, keepdims=True), 0.0)
+    slot = jnp.where(kept, place.astype(jnp.int32), -1)
+    s_iota = lax.broadcasted_iota(jnp.int32, (cap, tokens), 0)
+    for i in range(experts):
+        pick = (s_iota == slot[i:i + 1, :]).astype(f32)
+        scale = jnp.sum(pick * weight[i:i + 1, :], axis=1, keepdims=True)
+        pick = pick.astype(bf)
+        xs[i] = jnp.dot(pick, n2[...], preferred_element_type=f32).astype(bf)
+        gs[i] = (jnp.dot(pick, gb[...], preferred_element_type=f32) * scale).astype(bf)
+def attn_bwd_kernel(nl, ns, blocks, experts, cap, ll, sl, q, k, v, kl, vl, tab, lcol, lrow, scol, srow,
+                    eo, ri, mid, mixed, logits, rcol, gl, gsh, wo, gain, rt,
+                    dq, dk, dv, dkl, dvl, seg, final, midg, wog, fgg, rtg, lb, sb, li, si, mg, bg, n2, lg, fin, bk, sh):
+    f32, bf = jnp.float32, jnp.bfloat16
+    tokens = q.shape[0]
+    lane = lax.broadcasted_iota(jnp.int32, (tokens, 128), 1)
+    member = ((lane == rcol[:, 0:1]) | (lane == rcol[:, 1:2])).astype(f32)
+    after = (lax.broadcasted_iota(jnp.int32, (tokens, tokens), 1) < lax.broadcasted_iota(jnp.int32, (tokens, tokens), 0)).astype(f32).astype(bf)
+    place = jnp.dot(after, member.astype(bf), preferred_element_type=f32)
+    kept = (member > 0.5) & (place < cap)
+    slot = jnp.where(kept, place.astype(jnp.int32), -1)
+    lgt = jnp.where(lane < experts, logits[...], -1e30)
+    ex = jnp.exp(lgt - jnp.max(lgt, axis=1, keepdims=True))
+    p = ex / jnp.sum(ex, axis=1, keepdims=True)
+    chosen = member * p
+    both = jnp.sum(chosen, axis=1, keepdims=True)
+    gate = chosen / both
+    fg = jnp.zeros((1, q.shape[1]), f32)
+    for t in range(2):
+        at = slice(t * 256, t * 256 + 256)
+        rows = pl.ds(t * 256, 256)
+        g = rows_of(gl, gsh, t, nl, ns).astype(f32)
+        m = mid[rows, :]
+        fin[...] = m
+        bk[...] = jnp.zeros_like(m)
+        sh[...] = jnp.zeros_like(sh)
+        s_iota = lax.broadcasted_iota(jnp.int32, (256, cap), 1)
+        slot_t, weight_t, lane_t = slot[at], jnp.where(kept[at], gate[at], 0.0), lane[:256]
+        @pl.loop(0, experts)
+        def _(i):
+            this = lane_t == i
+            mine = jnp.sum(jnp.where(this, slot_t, 0), axis=1, keepdims=True)
+            weight = jnp.sum(jnp.where(this, weight_t, 0.0), axis=1, keepdims=True)
+            pick = (s_iota == mine).astype(f32).astype(bf)
+            pair = jnp.dot(pick, eo[i], preferred_element_type=f32)
+            fin[...] += weight * pair
+            sh[...] = jnp.where(this, jnp.sum(rows_of(gl, gsh, t, nl, ns).astype(f32) * pair, axis=1, keepdims=True), sh[...])
+            bk[...] += jnp.dot(pick, ri[i], preferred_element_type=f32)
+        final[rows, :] = fin[...].astype(bf)
+        share, back = sh[...], bk[...]
+        mean = jnp.sum(share * gate[at], axis=1, keepdims=True)
+        pg = member[at] * (share - mean) / both[at]
+        lgrad = (p[at] * (pg - jnp.sum(p[at] * pg, axis=1, keepdims=True))).astype(bf)
+        lg[rows, :] = lgrad
+        r2 = rms_scale(m)
+        u = m * r2
+        n2[rows, :] = (u * gain[...]).astype(bf)
+        back += jnp.dot(lgrad, rt[...], preferred_element_type=f32)
+        fg += jnp.sum(back * u, axis=0, keepdims=True)
+        w = back * gain[...]
+        out = g + r2 * (w - u * jnp.mean(w * u, axis=-1, keepdims=True))
+        midg[rows, :] = out
+        bg[rows, :] = out.astype(bf)
+        mg[rows, :] = dot(out.astype(bf), wo[...], 1, 1).astype(bf)
+    fgg[...] = fg
+    rtg[...] = dot(lg[...], n2[...], 0, 0)[:experts]
+    wog[...] = dot(mixed[...], bg[...], 0, 0).astype(bf)
     attn_setup(nl, ns, blocks, ll, sl, lcol, lrow, scol, srow, lb, sb)
     me = lax.axis_index("seq")
     lane = lax.broadcasted_iota(jnp.int32, (128, 128), 1)
@@ -253,9 +336,8 @@
                 kk = kl[:, b, :, cols].reshape(n * 128, 128); vv = vl[:, b, :, cols].reshape(n * 128, 128)
             else:
                 kk = k[rows, cols]; vv = v[rows, cols]
-            qq = q[rows, cols]; gg = mg[rows, cols]
             idx = li.at[b] if b < nl else si.at[b - nl]
-            qs = stack_heads(qq, first); gs = stack_heads(gg, first)
+            qs = stack_heads(q[rows, cols], first); gs = stack_heads(mg[rows, cols], first)
             p = probs_of(qs, kk, (tab[2 * hp], tab[2 * hp + 1]), lb.at[b] if b < nl else sb.at[b - nl], n)
             dp = dot(gs, vv, 1, 1)
             ds = (p * (dp - jnp.sum(p * dp, axis=1, keepdims=True))).astype(jnp.bfloat16)
@@ -276,21 +358,26 @@
                 dkl[:, b, :, cols] = dkt.reshape(n, 128, 128); dvl[:, b, :, cols] = dvt.reshape(n, 128, 128)
             else:
                 dk[pl.ds((b - nl) * 128, 128), cols] = dkt; dv[pl.ds((b - nl) * 128, 128), cols] = dvt
-def attention(backward, nl, ns, blocks, arrays, tokens, width):
+def attention(backward, nl, ns, blocks, experts, cap, arrays, tokens, width):
     sm, vm = pl.BlockSpec(memory_space=pltpu.SMEM), pl.BlockSpec(memory_space=pltpu.VMEM)
-    bf = jnp.bfloat16
-    rows = jax.ShapeDtypeStruct((tokens, width), bf)
+    bf, f32 = jnp.bfloat16, jnp.float32
+    S = jax.ShapeDtypeStruct
+    rows = S((tokens, width), bf)
     buckets = [pltpu.VMEM((nl, blocks, 128, 128), jnp.int32), pltpu.VMEM((ns, 1, 128, 128), jnp.int32)]
+    row_buf = pltpu.VMEM((tokens, width), bf)
     if backward:
-        short = jax.ShapeDtypeStruct((ns * 128, width), bf)
-        long = jax.ShapeDtypeStruct((blocks, nl, 128, width), bf)
-        outs = [rows, short, short, long, long, jax.ShapeDtypeStruct((16, 1, 128), jnp.float32)]
-        body = functools.partial(attn_bwd_kernel, nl, ns, blocks); scr = buckets * 2
+        short = S((ns * 128, width), bf)
+        long = S((blocks, nl, 128, width), bf)
+        outs = [rows, short, short, long, long, S((16, 1, 128), f32), rows, S((tokens, width), f32), S((width, width), bf),
+                S((1, width), f32), S((experts, width), f32)]
+        body = functools.partial(attn_bwd_kernel, nl, ns, blocks, experts, cap)
+        scr = buckets * 2 + [row_buf] * 3 + [pltpu.VMEM((tokens, 128), bf)] + [pltpu.VMEM((256, width), f32)] * 2 + [pltpu.VMEM((256, 128), f32)]
     else:
-        outs = [rows]; body = functools.partial(attn_fwd_kernel, nl, ns, blocks); scr = buckets
+        slots = S((experts, cap, width), bf)
+        outs = [rows, S((tokens, width), f32), slots, slots, S((tokens, 128), f32)]
+        body = functools.partial(attn_fwd_kernel, nl, ns, blocks, experts, cap); scr = buckets + [row_buf] * 2
     return pl.pallas_call(body, out_shape=outs, in_specs=[sm, sm] + [vm] * (len(arrays) - 2), out_specs=[vm] * len(outs),
-        scratch_shapes=scr, compiler_params=pltpu.CompilerParams(vmem_limit_bytes=56 * 2**20))(*arrays)
-
+        scratch_shapes=scr, compiler_params=pltpu.CompilerParams(vmem_limit_bytes=60 * 2**20))(*arrays)
 
 def seq_places(C):
     s = lax.axis_index("seq"); g = lax.axis_index("dp")
@@ -574,7 +661,6 @@
     dp_size = lax.axis_size("dp")
     experts = local_experts * dp_size
     capacity = (5 * tokens + 2 * experts - 1) // (2 * experts)
-    seq_index = lax.axis_index("seq")
     seq_size = lax.axis_size("seq")
     dims = (seq_size // 2, 2, dp_size // 2, 2)
     devices = seq_size * dp_size
@@ -613,110 +699,62 @@
     long_keys, long_values = seq_gather((keys, values), long_items, quarter, seq_size, 2)
     table = attn_set[6].reshape(HEADS, 1, BUCKETS).astype(jnp.float32)
     table = jnp.pad(table, ((0, 0), (0, 0), (0, 128 - BUCKETS)), constant_values=masked)
+    routes = jnp.concatenate([long_routes.reshape(-1, 2), short_routes.reshape(-1, 2)], 0)
+    router_t = jnp.pad(attn_set[7].T, ((0, 128 - experts), (0, 0)))
+    gain_second = attn_set[5].astype(jnp.float32).reshape(1, model_width)
+    sizes = (long_items, short_items, seq_size, experts, capacity)
     attn_args = (
+        long_lengths,
+        short_lengths,
+        queries,
+        keys,
+        values,
+        long_keys,
+        long_values,
         table,
         long_positions.reshape(long_items, seq_size, quarter, 1),
         long_positions.reshape(long_items, seq_size, 1, quarter),
         short_positions.reshape(short_items, 1, short_len, 1),
         short_positions.reshape(short_items, 1, 1, short_len),
     )
-    lead_args = (long_lengths, short_lengths, queries, keys, values, long_keys, long_values)
-    (mixed_all,) = attention(
-        False, long_items, short_items, seq_size, lead_args + attn_args, tokens, model_width
-    )
-    resid_mid = resid_in + jnp.dot(mixed_all, attn_set[3], preferred_element_type=jnp.float32)
-    gain_second = attn_set[5].astype(jnp.float32)
-    normed_two = rms_norm(resid_mid, gain_second).astype(jnp.bfloat16)
-    logits = jnp.dot(normed_two, attn_set[7], preferred_element_type=jnp.float32)
-    routes = jnp.concatenate([long_routes.reshape(-1, 2), short_routes.reshape(-1, 2)], 0)
-    choose = (routes[..., None] == jnp.arange(experts, dtype=jnp.int32)).astype(jnp.float32)
-    gate_share, gate_pull = jax.vjp(lambda logit_in: gate_values(logit_in, choose), logits)
-    flat_routes = routes.reshape(-1)
-    member = (flat_routes[:, None] == jnp.arange(experts, dtype=jnp.int32)).astype(jnp.int32)
-    queue_pos = jnp.sum(jnp.cumsum(member, axis=0) * member, axis=1) - 1
-    route_kept = queue_pos < capacity
-    slot_index = jnp.where(route_kept, flat_routes * capacity + queue_pos, experts * capacity)
-    slot_pair = (
-        jnp.zeros(experts * capacity + 1, jnp.int32)
-        .at[slot_index]
-        .set(jnp.arange(2 * tokens, dtype=jnp.int32))[:-1]
-    )
-    slot_used = jnp.zeros(experts * capacity + 1, jnp.bool_).at[slot_index].set(True)[:-1]
-    pair_slot = jnp.where(route_kept, slot_index, 0)
-    outgoing = jnp.where(
-        slot_used[:, None], jnp.take(normed_two, slot_pair // 2, axis=0), 0
-    ).reshape(experts, capacity, model_width)
-    kept_two = route_kept.reshape(tokens, 2).astype(jnp.float32)
-    weighting = gate_share * kept_two
-    grad_out = jnp.concatenate(
-        [long_grad_out.reshape(long_rows, model_width), short_grad_out.reshape(-1, model_width)], 0
-    ).astype(jnp.float32)
-    pair_grad = (
-        (weighting[:, :, None] * grad_out[:, None, :])
-        .astype(jnp.bfloat16)
-        .reshape(2 * tokens, model_width)
-    )
-    out_slots = jnp.where(slot_used[:, None], jnp.take(pair_grad, slot_pair, axis=0), 0).reshape(
-        experts, capacity, model_width
+    tail_args = (long_grad_out, short_grad_out, attn_set[3], gain_second, router_t)
+    mixed_all, resid_mid, outgoing, out_slots, logits = attention(
+        False,
+        *sizes,
+        attn_args + (long_tokens, short_tokens) + tail_args + (routes.T,),
+        tokens,
+        model_width,
     )
     later_down, unused_keys = lax.optimization_barrier((down_weight[0], long_keys))
     down_full = lax.all_gather(later_down, "seq", axis=0, tiled=True)
     back_rows, returned_grad, expert_grads = expert_all(
         outgoing, out_slots, gate_weight[0], up_weight[0], down_full, seq_size, 4
     )
-    pair_out = (
-        jnp.where(
-            route_kept[:, None],
-            jnp.take(back_rows.reshape(experts * capacity, model_width), pair_slot, axis=0),
-            0,
-        )
-        .reshape(tokens, 2, model_width)
-        .astype(jnp.float32)
-    )
-    final = resid_mid + weighting[:, 0:1] * pair_out[:, 0] + weighting[:, 1:2] * pair_out[:, 1]
-    final_low = final.astype(jnp.bfloat16)
+    (
+        query_act,
+        short_key,
+        short_value,
+        long_key,
+        long_value,
+        table_sums,
+        final_low,
+        middle_grad,
+        output_local,
+        ffn_gain_local,
+        router_local,
+    ) = attention(
+        True,
+        *sizes,
+        attn_args
+        + (back_rows, returned_grad, resid_mid, mixed_all, logits, routes)
+        + tail_args,
+        tokens,
+        model_width,
+    )
     long_out = final_low[:long_rows].reshape(long_items, quarter, model_width)
     short_out = final_low[long_rows:].reshape(short_items, short_len, model_width)
-    share_grad = kept_two * jnp.sum(grad_out[:, None, :] * pair_out, axis=-1)
-    logit_grad = gate_pull(share_grad)[0].astype(jnp.bfloat16)
+    down_grad, gate_grad, up_grad = (expert_grads[m : m + 1] for m in range(3))
     attn_back = attn_set
-    down_grad, gate_grad, up_grad = (expert_grads[m : m + 1] for m in range(3))
-    route_grad = (
-        jnp.where(
-            route_kept[:, None],
-            jnp.take(returned_grad.reshape(experts * capacity, model_width), pair_slot, axis=0),
-            0,
-        )
-        .reshape(tokens, 2, model_width)
-        .astype(jnp.float32)
-    )
-    normed_two_grad = (
-        route_grad[:, 0]
-        + route_grad[:, 1]
-        + jnp.einsum("te,de->td", logit_grad, attn_back[7], preferred_element_type=jnp.float32)
-    )
-    router_local = jnp.einsum(
-        "td,te->de", normed_two, logit_grad, preferred_element_type=jnp.float32
-    )
-    unused_mid, norm_two_pull = jax.vjp(rms_norm, resid_mid, attn_back[5].astype(jnp.float32))
-    mid_norm_grad, ffn_gain_local = norm_two_pull(normed_two_grad)
-    middle_grad = grad_out + mid_norm_grad
-    branch_grad = middle_grad.astype(jnp.bfloat16)
-    output_local = jnp.einsum(
-        "td,te->de", mixed_all, branch_grad, preferred_element_type=jnp.float32
-    )
-    mix_grad = jnp.einsum(
-        "te,de->td", branch_grad, attn_back[3], preferred_element_type=jnp.float32
-    ).astype(jnp.bfloat16)
-    query_act, short_key, short_value, long_key, long_value, table_sums = attention(
-        True,
-        long_items,
-        short_items,
-        seq_size,
-        lead_args + (mix_grad,) + attn_args,
-        tokens,
-        model_width,
-    )
     long_key, long_value = seq_sum((long_key, long_value), 3)
     key_act = jnp.concatenate([long_key.reshape(long_rows, model_width), short_key], 0)
     value_act = jnp.concatenate([long_value.reshape(long_rows, model_width), short_value], 0)
@@ -746,7 +784,7 @@
     small_local = jnp.concatenate(
         [
             part.reshape(devices, -1)
-            for part in (attn_gain_local, ffn_gain_local, table_local, router_local)
+            for part in (attn_gain_local, ffn_gain_local, table_local, router_local.T)
         ],
         1,
     )

time: 675 us -> 591 us (0.88)
  local copies, waits for them, and re-layouts: 103 us -> 30 us
  Pallas kernels: 482 us -> 508 us
  other arithmetic: 27.7 us -> 8.06 us
  matrix products: 38.9 us -> 26.5 us
    pallas_call x2, Pallas kernels: 68 us -> 92.8 us  [attention(): pl.pallas_call(body, out_shape=outs, in_specs=[sm, sm] + [vm] * (len(arra...]
    gather x4 -> x0, local copies, waits for them, and re-layouts: 24.1 us -> none  [the longest x1 8.24 us: on_device(): jnp.take(returned_grad.reshape(experts * capacity, model_width), pair_slo...]
    slice x5 -> x0, local copies, waits for them, and re-layouts: 16.8 us -> none  [the longest x1 9.2 us: on_device(): route_grad[:, 0] + route_grad[:, 1]]
    dot_general x6 -> x0, matrix products: 12.6 us -> none  [the longest x1 4.71 us: on_device(): jnp.einsum('te,de->td', logit_grad, attn_back[7], preferred_element_type=...]
    convert_element_type x3 -> x1, local copies, waits for them, and re-layouts: 11.7 us -> 0.67 us  [on_device(): gain_second = attn_set[5].astype(jnp.float32).reshape(1, model_width)]
    mul x4 -> x0, local copies, waits for them, and re-layouts: 9.84 us -> none  [the longest x2 9.5 us: on_device(): weighting[:, :, None] * grad_out[:, None, :]]
    scatter x2 -> x0, local copies, waits for them, and re-layouts: 8.66 us -> none  [the longest x1 4.34 us: on_device(): jnp.zeros(experts * capacity + 1, jnp.bool_).at[slot_index].set(True)[:-1]]
    convert_element_type x7 -> x1, other arithmetic: 7.33 us -> 0.08 us  [on_device(): gain_second = attn_set[5].astype(jnp.float32).reshape(1, model_width)]
  transfers between devices with their start and end apart: 1 -> 1, of which waited for: 0 -> 0; matrix products, arithmetic and copies ran while one was open for 8% -> 2% of each run, Pallas kernels for 4% -> 6%
where the time goes in v5:
time: 591 us; the launch traced here: 587 us
  Pallas kernels  508 us (86%)
  local copies, waits for them, and re-layouts  30 us (5%)
  matrix products  26.5 us (4%)
  between operations  14.6 us (2%)
  other arithmetic  8.06 us (1%)
    pallas_call x1, Pallas kernels, expert_all(): pl.pallas_call(functools.partial(expert_kernel, cap, per, order, todo, wc...  232 us
    pallas_call x2, Pallas kernels, attention(): pl.pallas_call(body, out_shape=outs, in_specs=[sm, sm] + [vm] * (len(arra...  92.8 us
    pallas_call x1, Pallas kernels, scatter_all(): pl.pallas_call(functools.partial(scatter_kernel, dims, pieces, n), out_sh...  68.5 us
    pallas_call x1, Pallas kernels, gather_all(): pl.pallas_call(functools.partial(gather_kernel, dims, pieces, na), out_sh...  60.1 us
    pallas_call x1, Pallas kernels, seq_gather(): pl.pallas_call(functools.partial(seq_gather_kernel, n, items, rows), out_...  28.9 us
    pallas_call x1, Pallas kernels, seq_sum(): pl.pallas_call(functools.partial(seq_sum_kernel, n, items), out_shape=[ja...  25.8 us
  transfers between devices with their start and end apart: 1, of which 0 were waited for; matrix products, arithmetic and copies ran while one was open for 2% of the time, Pallas kernels for 6%

profile of v5, /device:TPU:0, one launch (start us, length us, event | category | flops | bytes accessed | tf_op | source)
XLA Modules:
  0.0 587.0 jit_solution(3174255009247974448)
XLA Ops:
  7.2 1.5 fusion.5
  8.7 0.8 copy.52
  9.6 1.4 fusion.16.refs_4_
  10.9 60.1 %shard_map.316 = (bf16[2,2,4,2,32,1024]{5,4,3,2,1,0:T(8,128)(2,1)}, bf16[2,2,4,2,32,1024]{5,4,3,2,1,0:T(8,128)(2,1)}, bf16[2,2,4,2,32,1024]{5,4,3,2,1,0:T(8,128)...) custom-call(bf16[32,1024]{1,0:T(8,128)(2,1)} %refs_0_.1, bf16[32,1024]{1,0:T(8,128)(2,1)} %refs_1_.1, ...), custom_call_target="tpu_custom_call" | custom-call | tf_op jit(solution)/shard_map/pallas_call | solution.py:89
  71.0 0.9 copy.67
  72.1 3.4 convolution_convert_fusion.3.refs_1_.v
  75.5 1.3 convolution_convert_fusion.4.refs_0_.k
  76.9 28.9 %shard_map.317 = (bf16[4,2,128,1024]{3,2,1,0:T(8,128)(2,1)S(1)}, bf16[4,2,128,1024]{3,2,1,0:T(8,128)(2,1)}) custom-call(bf16[512,1024]{1,0:T(8,128)(2,1)S(1)} %convolution_convert_fusion.4.refs_0_.k, bf16[512,1024]{1,0:T(8,128)(2,1)S(1)} %convolution_convert_fusion.3.refs_1_.v), custom_call_target="tpu_custom_call" | custom-call | tf_op jit(solution)/shard_map/pallas_call | solution.py:418
  105.8 1.3 copy-done.2
  107.2 1.1 reshape.224.lcol
  108.3 0.6 reshape.197.lrow
  108.9 0.7 reshape.223.gain
  109.6 0.3 reshape.201
  110.2 0.8 copy.60.scol
  111.0 0.6 pad_add_fusion
  111.6 0.9 copy.61.rcol
  112.5 0.8 pad.22.rt
  113.3 0.6 pad.21.tab
  113.9 4.2 convolution_convert_fusion.5.q
  118.1 33.9 %shard_map.318 = (bf16[512,1024]{1,0:T(8,128)(2,1)}, f32[512,1024]{1,0:T(8,128)}, bf16[8,160,1024]{2,1,0:T(8,128)(2,1)}, bf16[8,160,1024]{2,1,0:T(8,128)(2,1)}, f32[512,128]{1,0:T(8,128)}) custom-call(s32[2]{0:T(128)} %ll.3, s32[2]{0:T(128)} %sl.3, bf16[512,1024]{1,0:T(8,128)(2,1)} %convolution_convert_fusion.5.q, bf16[512,1024]{1,0:T(8,128)(2,1)} %copy-done.1, ...), custom_call_target="tpu_custom_call" | custom-call | tf_op jit(solution)/shard_map/pallas_call | solution.py:379
  152.0 231.8 %shard_map.319 = (bf16[8,160,1024]{2,1,0:T(8,128)(2,1)}, bf16[8,160,1024]{2,1,0:T(8,128)(2,1)}, f32[3,256,2816]{2,1,0:T(8,128)}, bf16[1280,1024]{1,0:T(8,128)(2,1)}, bf16[1280,1024]{1,0:T(8,128)(2,1)}) custom-call(bf16[8,160,1024]{2,1,0:T(8,128)(2,1)} %get-tuple-element.56.xs, bf16[8,160,1024]{2,1,0:T(8,128)(2,1)} %get-tuple-element.57.gs, ...), custom_call_target="tpu_custom_call" | custom-call | tf_op jit(solution)/shard_map/pallas_call | solution.py:623
  383.8 58.9 %shard_map.320 = (bf16[512,1024]{1,0:T(8,128)(2,1)}, bf16[256,1024]{1,0:T(8,128)(2,1)}, bf16[256,1024]{1,0:T(8,128)(2,1)}, bf16[4,2,128,1024]{3,2,1,0:T(8,128)(2...) custom-call(s32[2]{0:T(128)} %ll.3, s32[2]{0:T(128)} %sl.3, ...), custom_call_target="tpu_custom_call" | custom-call | tf_op jit(solution)/shard_map/pallas_call | solution.py:379
  442.7 0.9 slice_subtract_fusion
  443.8 1.6 copy-done.3
  445.3 1.6 copy-done.4
  446.9 25.8 %shard_map.321 = (bf16[2,128,1024]{2,1,0:T(8,128)(2,1)S(1)}, bf16[2,128,1024]{2,1,0:T(8,128)(2,1)S(1)}) custom-call(bf16[4,2,128,1024]{3,2,1,0:T(8,128)(2,1)S(1)} %copy-done.3, bf16[4,2,128,1024]{3,2,1,0:T(8,128)(2,1)S(1)} %copy-done.4), custom_call_target="tpu_custom_call" | custom-call | tf_op jit(solution)/shard_map/pallas_call | solution.py:450
  472.8 2.6 fusion.7
  475.4 2.7 convolution_convert_fusion.1
  478.1 2.6 fusion.34
  480.7 2.7 convolution_convert_fusion.2
  483.6 4.0 convolution_convert_fusion
  487.7 3.0 fusion.3
  491.0 0.3 reshape.218
  491.3 0.5 broadcast.75
  491.8 0.7 reduce.3
  492.7 1.6 copy-done.6
  494.3 68.5 %shard_map.322 = (f32[32,1024]{1,0:T(8,128)S(1)}, f32[32,1024]{1,0:T(8,128)S(1)}, f32[32,1024]{1,0:T(8,128)S(1)}, f32[32,1024]{1,0:T(8,128)S(1)}, f32[8,128]{1,0:T(8,128)S(1)}) custom-call(bf16[2,2,4,2,32,1024]{5,4,3,2,1,0:T(8,128)(2,1)S(1)} %bitcast.51, bf16[2,2,4,2,32,1024]{5,4,3,2,1,0:T(8,128)(2,1)S(1)} %bitcast.52, ...), custom_call_target="tpu_custom_call" | custom-call | tf_op jit(solution)/shard_map/pallas_call | solution.py:162
  562.9 0.6 fusion.33
  563.4 0.6 slice.150
  564.0 0.7 copy.63
  564.7 2.8 fusion.4
  567.6 1.5 fusion.30
  569.2 1.0 fusion.31
  570.2 7.2 %fusion.29 = (f32[1,256,2816]{2,1,0:T(8,128)}, f32[1,256,2816]{2,1,0:T(8,128)}, f32[1,256,2816]{2,1,0:T(8,128)}) fusion(f32[3,256,2816]{2,1,0:T(8,128)} %get-tuple-element.82), kind=kLoop, calls=%fused_computation.51 | loop fusion | bytes 17301504 | tf_op jit(solution)/shard_map/slice | solution.py:756
  577.4 0.7 copy.72
  578.0 0.7 copy.73
  578.7 0.7 copy.74
  579.3 0.7 copy.75
  (76 shorter events, 1.8 us)
Async XLA Ops:
  7.2 144.8 %all-gather.2.cloned.1.call-start = ((), (), s32[]{:S(2)}) async-start(), calls=%async_computation | async-start | bytes 7208960 | tf_op jit(solution)/shard_map/all_gather | solution.py:729
  72.1 3.4 copy-start.7
  72.1 3.4 copy-start.9
  72.1 3.4 copy-start.21
  75.5 1.3 copy-start
  76.8 33.1 %copy-start.1 = (bf16[512,1024]{1,0:T(8,128)(2,1)}, bf16[512,1024]{1,0:T(8,128)(2,1)S(1)}, u32[]{:S(2)}) copy-start(bf16[512,1024]{1,0:T(8,128)(2,1)S(1)} %convolution_convert_fusion.4.refs_0_.k) | copy-start | bytes 3145732
  76.8 30.3 %copy-start.14 = (s32[2,512]{1,0:T(2,128)S(1)}, s32[2,512]{1,0:T(2,128)}, u32[]{:S(2)}) copy-start(s32[2,512]{1,0:T(2,128)} %param.36) | copy-start | bytes 12292
  76.9 33.4 %copy-start.15 = (s32[2,128]{1,0:T(2,128)S(1)}, s32[2,128]{1,0:T(2,128)}, u32[]{:S(2)}) copy-start(s32[2,128]{1,0:T(2,128)} %param.37) | copy-start | bytes 3076
  76.9 34.2 %copy-start.17 = (s32[2,128,2]{1,2,0:T(2,128)S(1)}, s32[2,128,2]{1,2,0:T(2,128)}, u32[]{:S(2)}) copy-start(s32[2,128,2]{1,2,0:T(2,128)} %param.41) | copy-start | bytes 6148
  76.9 34.1 %copy-start.18 = (s32[2,128,2]{1,2,0:T(2,128)S(1)}, s32[2,128,2]{1,2,0:T(2,128)}, u32[]{:S(2)}) copy-start(s32[2,128,2]{1,2,0:T(2,128)} %param.40) | copy-start | bytes 6148
  105.7 1.3 copy-start.2
  443.8 1.6 copy-start.3
  445.3 1.6 copy-start.4
  446.9 25.8 %copy-start.22 = (bf16[2,2,4,2,32,1024]{5,4,3,2,1,0:T(8,128)(2,1)S(1)}, bf16[2,2,4,2,32,1024]{5,4,3,2,1,0:T(8,128)(2,1)}, u32[]{:S(2)}) copy-start(bf16[2,2,4,2,32,1024]{5,4,3,2,1,0:T(8,128)(2,1)} %get-tuple-element.51) | copy-start | bytes 6291460
  446.9 25.8 %copy-start.25 = (bf16[256,1024]{1,0:T(8,128)(2,1)S(1)}, bf16[256,1024]{1,0:T(8,128)(2,1)}, u32[]{:S(2)}) copy-start(bf16[256,1024]{1,0:T(8,128)(2,1)} %get-tuple-element.70) | copy-start | bytes 1572868
  472.8 2.6 copy-start.8
  472.8 2.6 copy-start.10
  475.4 2.7 copy-start.20
  475.4 2.7 copy-start.23
  483.6 4.0 copy-start.11
  483.6 4.0 copy-start.19
  483.6 4.0 copy-start.24
  483.6 4.0 copy-start.26
  483.6 4.0 copy-start.27
  487.7 3.1 copy-start.13
  487.7 4.1 copy-start.16
  487.7 5.0 copy-start.5
  492.7 1.6 copy-start.6
  567.5 1.6 copy-start.12
Sparse Core Ops, SparseCore 0:
  107.2 43.2 all-gather.1

commit v6 on v5

v6 whole, which is shorter than its diff:
```python
import functools

import jax
import jax.numpy as jnp
from jax import lax
from jax.experimental import pallas as pl
from jax.experimental.pallas import tpu as pltpu
from jax.sharding import PartitionSpec as P

MESH = pl.DeviceIdType.MESH

HEADS = 16
HEAD = 64
BUCKETS = 32


epsilon = 1e-06
masked = -1e30


def gather_kernel(dims, pieces, na, *refs):
    X, C, Z, Y = dims
    n = len(pieces)
    lsem, zs, zr, hs, hr, cs, cr = refs[2*na:]
    routes = [p[3] for p in pieces]
    ins = [refs[m].at[pl.ds(r0, nr)] for m, r0, nr, _ in pieces]
    class V:
        def __init__(self, ref, r0, nr): self.ref, self.r0, self.nr = ref, r0, nr
        @property
        def at(self): return self
        def __getitem__(self, k):
            k = k + (slice(None),) * (4 - len(k)) + (pl.ds(self.r0, self.nr),)
            return self.ref.at[k]
    outs = [V(refs[na + m], r0, nr) for m, r0, nr, _ in pieces]
    s = lax.axis_index("seq"); g = lax.axis_index("dp")
    x, c = s // C, lax.rem(s, C)
    z, y = g // Y, lax.rem(g, Y)
    def zdev(k): return (s, lax.rem(z + k, Z) * Y + y)
    ydev = (s, z * Y + (1 - y)); xdev = ((1 - x) * C + c, g); cdev = (x * C + 1 - c, g)
    bar = pltpu.get_barrier_semaphore()
    for d in [zdev(k) for k in range(1, Z)] + [ydev, xdev, cdev]:
        pl.semaphore_signal(bar, inc=1, device_id=d, device_id_type=MESH)
    pl.semaphore_wait(bar, Z + 2)
    def rc(src, dst, ss, rs, dev):
        cp = pltpu.make_async_remote_copy(src_ref=src, dst_ref=dst, send_sem=ss, recv_sem=rs, device_id=dev, device_id_type=MESH)
        cp.start(); return cp
    sends = []
    local = []; zc = []
    for m in range(n):
        lc = pltpu.make_async_copy(ins[m], outs[m].at[x, c, z, y], lsem.at[m]); lc.start(); local.append(lc)
        zc.append([rc(ins[m], outs[m].at[x, c, z, y], zs.at[m, k], zr.at[m, k], zdev(k)) for k in range(1, Z)])
    h = [[None, None] for _ in range(n)]
    cc = [[None]*3 for _ in range(n)]
    for t in range(n + 2):
        for stage in range(3):
            m = t - stage
            if not 0 <= m < n: continue
            o = outs[m]; route = routes[m]
            if stage == 0:
                local[m].wait()
                for q in zc[m]: q.wait_recv()
                mine = o.at[x, c, :, y]
                h[m][0] = rc(mine, mine, hs.at[m,0], hr.at[m,0], xdev if route == 0 else ydev)
                cc[m][0] = rc(mine, mine, cs.at[m,0], cr.at[m,0], cdev)
            elif stage == 1:
                h[m][0].wait_recv()
                if route == 0:
                    both = o.at[:, c, :, y]; got = o.at[1 - x, c, :, y]
                else:
                    both = o.at[x, c]; got = o.at[x, c, :, 1 - y]
                h[m][1] = rc(both, both, hs.at[m,1], hr.at[m,1], ydev if route == 0 else xdev)
                cc[m][1] = rc(got, got, cs.at[m,1], cr.at[m,1], cdev)
            else:
                h[m][1].wait_recv()
                got = o.at[:, c, :, 1 - y] if route == 0 else o.at[1 - x, c]
                cc[m][2] = rc(got, got, cs.at[m,2], cr.at[m,2], cdev)
    for m in range(n):
        for q in zc[m]: q.wait_send()
        for q in h[m]: q.wait_send()
        for q in cc[m]: q.wait()
def gather_all(arrays, pieces, dims, cid):
    X, C, Z, Y = dims; na = len(arrays); n = len(pieces)
    sem = pltpu.SemaphoreType.DMA
    return pl.pallas_call(functools.partial(gather_kernel, dims, pieces, na),
        out_shape=[jax.ShapeDtypeStruct((X, C, Z, Y) + a.shape, a.dtype) for a in arrays],
        in_specs=[pl.BlockSpec(memory_space=pl.ANY)] * na, out_specs=[pl.BlockSpec(memory_space=pl.ANY)] * na,
        scratch_shapes=[sem((n,)), sem((n, Z)), sem((n, Z)), sem((n, 2)), sem((n, 2)), sem((n, 3)), sem((n, 3))],
        compiler_params=pltpu.CompilerParams(collective_id=cid, has_side_effects=True))(*arrays)


def seq_places(C):
    s = lax.axis_index("seq"); g = lax.axis_index("dp")
    x, c = s // C, lax.rem(s, C)
    return s, x, c, ((1 - x) * C + c, g), (x * C + 1 - c, g)
def greet(devs):
    bar = pltpu.get_barrier_semaphore()
    for d in devs:
        pl.semaphore_signal(bar, inc=1, device_id=d, device_id_type=MESH)
    pl.semaphore_wait(bar, len(devs))
def remote(src, dst, ss, rs, dev):
    cp = pltpu.make_async_remote_copy(src_ref=src, dst_ref=dst, send_sem=ss, recv_sem=rs, device_id=dev, device_id_type=MESH)
    cp.start()
    return cp
EDGES = (-90, -63, -45, -31, -22, -15, -11, -7, -6, -5, -4, -3, -2, -1, 0, 1, 2, 3, 4, 5, 6, 7, 8, 12, 16, 23, 32, 46, 64, 91)
FAR = (12, 16, 23, 32, 46, 64, 91)
def fill_buckets(out, q_col, k_row, length, base):
    r = k_row - q_col
    n = jnp.abs(r)
    far = jnp.full(r.shape, 8, jnp.int32)
    for e in FAR:
        far += (n >= e).astype(jnp.int32)
    b = jnp.where(n < 8, n, far) + jnp.where(r > 0, 16, 0)
    j = lax.broadcasted_iota(jnp.int32, r.shape, 1) + base
    out[...] = jnp.where(j < length, b, 32)
def dot(a, b, ca, cb):
    return lax.dot_general(a, b, (((ca,), (cb,)), ((), ())), preferred_element_type=jnp.float32)
def probs_of(qs, kk, tabs, bucket_ref, blocks):
    s = dot(qs, kk, 1, 1)
    t = [jnp.broadcast_to(tab, (128, 128)) for tab in tabs]
    bias = [jnp.concatenate([jnp.take_along_axis(x, bucket_ref[c], axis=1) for x in t], axis=0) for c in range(blocks)]
    s = s + (jnp.concatenate(bias, axis=1) if blocks > 1 else bias[0])
    p = jnp.exp(s - jnp.max(s, axis=1, keepdims=True))
    return p * (1.0 / jnp.sum(p, axis=1, keepdims=True))
def stack_heads(rows, first):
    return jnp.concatenate([jnp.where(first, rows, 0), jnp.where(first, 0, rows)], axis=0)
def column_of(row):
    i = lax.broadcasted_iota(jnp.int32, (128, 128), 0)
    return jnp.sum(jnp.where(i == lax.broadcasted_iota(jnp.int32, (128, 128), 1), row, 0), axis=1, keepdims=True)
def row_of(col):
    i = lax.broadcasted_iota(jnp.int32, (128, 128), 0)
    return jnp.sum(jnp.where(i == lax.broadcasted_iota(jnp.int32, (128, 128), 1), col, 0), axis=0, keepdims=True)
def rows_of(long_ref, short_ref, t):
    ref = long_ref if t == 0 else short_ref
    return ref[...].reshape(ref.shape[0] * ref.shape[1], ref.shape[2])
def rms_scale(mid):
    return lax.rsqrt(jnp.mean(mid * mid, axis=-1, keepdims=True) + epsilon)
def item(b, nl, blocks, cols, k, v, kl, vl):
    rows = pl.ds(b * 128, 128)
    if b < nl:
        return rows, blocks, kl[:, b, :, cols].reshape(blocks * 128, 128), vl[:, b, :, cols].reshape(blocks * 128, 128)
    return rows, 1, k[rows, cols], v[rows, cols]
def mine_of(b, nl, long_ref, short_ref):
    return long_ref.at[b] if b < nl else short_ref.at[b - nl]
def attn_fwd_kernel(nl, ns, blocks, experts, cap, ll, sl, q, k, v, kl, vl, tab, lpos, spos,
                    xl, xsh, gl, gsh, wo, params, lr, sr, mixed, mid, xs, gs, logits, lb, sb, n2, gb):
    me = lax.axis_index("seq")
    for b in range(nl):
        own = column_of(lpos[b:b + 1, pl.ds(pl.multiple_of(me * 128, 128), 128)])
        for c in range(blocks):
            fill_buckets(lb.at[b, c], own, lpos[b:b + 1, c * 128:(c + 1) * 128], ll[b], c * 128)
    for b in range(ns):
        fill_buckets(sb.at[b, 0], column_of(spos[b:b + 1, :]), spos[b:b + 1, :], sl[b], 0)
    first = lax.broadcasted_iota(jnp.int32, (128, 128), 1) < 64
    @pl.loop(0, 8)
    def _(hp):
        cols = pl.ds(pl.multiple_of(hp * 128, 128), 128)
        for b in range(nl + ns):
            rows, n, kk, vv = item(b, nl, blocks, cols, k, v, kl, vl)
            p = probs_of(stack_heads(q[rows, cols], first), kk, (tab[2 * hp], tab[2 * hp + 1]), mine_of(b, nl, lb, sb), n)
            out = dot(p.astype(jnp.bfloat16), vv, 1, 0)
            mixed[rows, cols] = jnp.where(first, out[:128], out[128:]).astype(jnp.bfloat16)
    f32, bf = jnp.float32, jnp.bfloat16
    tokens = q.shape[0]
    gain = params[experts + 1:experts + 2, :].astype(f32)
    for t in range(2):
        rows = pl.ds(t * 256, 256)
        m = rows_of(xl, xsh, t).astype(f32) + jnp.dot(mixed[rows, :], wo[...], preferred_element_type=f32)
        mid[rows, :] = m
        n2[rows, :] = (m * rms_scale(m) * gain).astype(bf)
        gb[rows, :] = rows_of(gl, gsh, t)
    logits[...] = dot(n2[...], params[...], 1, 1)
    logit_t = dot(params[...], n2[...], 1, 1)[:experts]
    routes = [jnp.concatenate([row_of(ref[i, :, j:j + 1]) for ref in (lr, sr) for i in range(ref.shape[0])], axis=1) for j in range(2)]
    e_iota = lax.broadcasted_iota(jnp.int32, (experts, tokens), 0)
    member = ((e_iota == routes[0]) | (e_iota == routes[1])).astype(f32)
    e = jnp.exp(logit_t - jnp.max(logit_t, axis=0, keepdims=True))
    p = e / jnp.sum(e, axis=0, keepdims=True)
    chosen = member * p
    before = (lax.broadcasted_iota(jnp.int32, (tokens, tokens), 0) < lax.broadcasted_iota(jnp.int32, (tokens, tokens), 1)).astype(f32).astype(bf)
    place = jnp.dot(member.astype(bf), before, preferred_element_type=f32)
    kept = (member > 0.5) & (place < cap)
    weight = jnp.where(kept, chosen / jnp.sum(chosen, axis=0, keepdims=True), 0.0)
    slot = jnp.where(kept, place.astype(jnp.int32), -1)
    s_iota = lax.broadcasted_iota(jnp.int32, (cap, tokens), 0)
    for i in range(experts):
        pick = (s_iota == slot[i:i + 1, :]).astype(f32)
        scale = jnp.sum(pick * weight[i:i + 1, :], axis=1, keepdims=True)
        pick = pick.astype(bf)
        xs[i] = jnp.dot(pick, n2[...], preferred_element_type=f32).astype(bf)
        gs[i] = (jnp.dot(pick, gb[...], preferred_element_type=f32) * scale).astype(bf)
def post_kernel(nl, ns, blocks, experts, cap, lpos, spos, eo, ri, mid, mixed, logits, lr, sr, gl, gsh, wo, params, eg,
                lout, sout, midg, wog, small, mg, li, si, eg0, eg1, eg2, bg, n2, lg, fin, bk, sh, ev, sem):
    f32, bf = jnp.float32, jnp.bfloat16
    tokens = mid.shape[0]
    fetch = [pltpu.make_async_copy(eg.at[m], ev.at[m], sem.at[m]) for m in range(3)]
    copies = [pltpu.make_async_copy(ev.at[m], out.at[0], sem.at[m]) for m, out in enumerate((eg0, eg1, eg2))]
    for cp in fetch: cp.start()
    gain = params[experts + 1:experts + 2, :].astype(f32)
    lane = lax.broadcasted_iota(jnp.int32, (tokens, 128), 1)
    routes = jnp.concatenate([ref[i] for ref in (lr, sr) for i in range(ref.shape[0])], axis=0)
    member = ((lane == routes[:, 0:1]) | (lane == routes[:, 1:2])).astype(f32)
    after = (lax.broadcasted_iota(jnp.int32, (tokens, tokens), 1) < lax.broadcasted_iota(jnp.int32, (tokens, tokens), 0)).astype(f32).astype(bf)
    place = jnp.dot(after, member.astype(bf), preferred_element_type=f32)
    kept = (member > 0.5) & (place < cap)
    slot = jnp.where(kept, place.astype(jnp.int32), -1)
    lgt = jnp.where(lane < experts, logits[...], -1e30)
    ex = jnp.exp(lgt - jnp.max(lgt, axis=1, keepdims=True))
    p = ex / jnp.sum(ex, axis=1, keepdims=True)
    chosen = member * p
    both = jnp.sum(chosen, axis=1, keepdims=True)
    gate = chosen / both
    fg = jnp.zeros((1, mid.shape[1]), f32)
    for t in range(2):
        at = slice(t * 256, t * 256 + 256)
        rows = pl.ds(t * 256, 256)
        g = rows_of(gl, gsh, t).astype(f32)
        m = mid[rows, :]
        fin[...] = m
        bk[...] = jnp.zeros_like(m)
        sh[...] = jnp.zeros_like(sh)
        s_iota = lax.broadcasted_iota(jnp.int32, (256, cap), 1)
        slot_t, weight_t, lane_t = slot[at], jnp.where(kept[at], gate[at], 0.0), lane[:256]
        @pl.loop(0, experts)
        def _(i):
            this = lane_t == i
            mine = jnp.sum(jnp.where(this, slot_t, 0), axis=1, keepdims=True)
            weight = jnp.sum(jnp.where(this, weight_t, 0.0), axis=1, keepdims=True)
            pick = (s_iota == mine).astype(f32).astype(bf)
            pair = jnp.dot(pick, eo[i], preferred_element_type=f32)
            fin[...] += weight * pair
            sh[...] = jnp.where(this, jnp.sum(rows_of(gl, gsh, t).astype(f32) * pair, axis=1, keepdims=True), sh[...])
            bk[...] += jnp.dot(pick, ri[i], preferred_element_type=f32)
        (lout, sout)[t][...] = fin[...].astype(bf).reshape(lout.shape)
        share, back = sh[...], bk[...]
        mean = jnp.sum(share * gate[at], axis=1, keepdims=True)
        pg = member[at] * (share - mean) / both[at]
        lgrad = (p[at] * (pg - jnp.sum(p[at] * pg, axis=1, keepdims=True))).astype(bf)
        lg[rows, :] = lgrad
        r2 = rms_scale(m)
        u = m * r2
        n2[rows, :] = (u * gain).astype(bf)
        back += jnp.dot(lgrad, params[...], preferred_element_type=f32)
        fg += jnp.sum(back * u, axis=0, keepdims=True)
        w = back * gain
        out = g + r2 * (w - u * jnp.mean(w * u, axis=-1, keepdims=True))
        midg[rows, :] = out
        bg[rows, :] = out.astype(bf)
        mg[rows, :] = dot(out.astype(bf), wo[...], 1, 1).astype(bf)
    for m in range(3):
        fetch[m].wait()
        copies[m].start()
    small[...] = jnp.zeros_like(small)
    small[1:2, :] = fg
    small[2:2 + experts, :] = dot(lg[...], n2[...], 0, 0)[:experts]
    wog[...] = dot(mixed[...], bg[...], 0, 0).astype(bf).reshape(wog.shape)
    lane = lax.broadcasted_iota(jnp.int32, (128, 128), 1)
    edge = jnp.full((128, 128), 4096, jnp.int32)
    for i, e in enumerate(EDGES):
        edge = jnp.where(lane == i, e, edge)
    edge = jnp.where(lane > len(EDGES), -4096, edge)
    def places(out, q_col, k_row):
        k_first = k_row[:, 0:1]
        t = lax.broadcasted_iota(jnp.int32, (128, 256), 1) + k_first
        below = jnp.sum((column_of(k_row) < t).astype(jnp.int32), axis=0, keepdims=True)
        at = jnp.clip(q_col + edge - k_first, 0, 255)
        lo = jnp.take_along_axis(jnp.broadcast_to(below[:, :128], (128, 128)), at & 127, axis=1)
        hi = jnp.take_along_axis(jnp.broadcast_to(below[:, 128:], (128, 128)), at & 127, axis=1)
        out[...] = jnp.where(at < 128, lo, hi) - 1
    me = lax.axis_index("seq")
    for b in range(nl):
        own = column_of(lpos[b:b + 1, pl.ds(pl.multiple_of(me * 128, 128), 128)])
        for c in range(blocks):
            places(li.at[b, c], own, lpos[b:b + 1, c * 128:(c + 1) * 128])
    for b in range(ns):
        places(si.at[b, 0], column_of(spos[b:b + 1, :]), spos[b:b + 1, :])
    for cp in copies: cp.wait()
def attention(nl, ns, blocks, experts, cap, arrays, tokens, width):
    sm, vm = pl.BlockSpec(memory_space=pltpu.SMEM), pl.BlockSpec(memory_space=pltpu.VMEM)
    S, bf, f32 = jax.ShapeDtypeStruct, jnp.bfloat16, jnp.float32
    slots = S((experts, cap, width), bf)
    outs = [S((tokens, width), bf), S((tokens, width), f32), slots, slots, S((tokens, 128), f32),
            S((nl, blocks, 128, 128), jnp.int32), S((ns, 1, 128, 128), jnp.int32)]
    return pl.pallas_call(functools.partial(attn_fwd_kernel, nl, ns, blocks, experts, cap), out_shape=outs,
        in_specs=[sm, sm] + [vm] * (len(arrays) - 2), out_specs=[vm] * len(outs), scratch_shapes=[pltpu.VMEM((tokens, width), bf)] * 2,
        compiler_params=pltpu.CompilerParams(vmem_limit_bytes=60 * 2**20))(*arrays)
def small_rows(experts):
    return -(-(experts + 4) // 8) * 8
def post(nl, ns, blocks, experts, cap, whole, arrays, tokens, width):
    vm, hbm = pl.BlockSpec(memory_space=pltpu.VMEM), pl.BlockSpec(memory_space=pl.ANY)
    S, bf, f32 = jax.ShapeDtypeStruct, jnp.bfloat16, jnp.float32
    eg = arrays[-1]
    outs = [S((nl, 128, width), bf), S((ns, 128, width), bf), S((tokens, width), f32), S(whole, bf), S((small_rows(experts), width), f32), S((tokens, width), bf),
            S((nl, blocks, 128, 128), jnp.int32), S((ns, 1, 128, 128), jnp.int32)] + [S((1,) + eg.shape[1:], f32)] * 3
    V = pltpu.VMEM
    return pl.pallas_call(functools.partial(post_kernel, nl, ns, blocks, experts, cap), out_shape=outs,
        in_specs=[vm] * (len(arrays) - 1) + [hbm], out_specs=[vm] * (len(outs) - 3) + [hbm] * 3,
        scratch_shapes=[V((tokens, width), bf)] * 2 + [V((tokens, 128), bf)] + [V((256, width), f32)] * 2 + [V((256, 128), f32), V(eg.shape, f32), pltpu.SemaphoreType.DMA((3,))],
        compiler_params=pltpu.CompilerParams(vmem_limit_bytes=60 * 2**20))(*arrays)
def head_kernel(nl, ns, experts, lx, sx, params, wq, wk, wv, q, k, v, kl, vl, n1t, n1, lsem, ss, rs):
    f32, bf = jnp.float32, jnp.bfloat16
    s, x, c, xdev, cdev = seq_places(2)
    far = (1 - x) * 2 + c
    greet([xdev, cdev])
    half = nl * 128
    gain = params[experts:experts + 1, :].astype(f32)
    def norm(t):
        m = rows_of(lx, sx, t).astype(f32)
        n1[pl.ds(t * half, half), :] = (m * rms_scale(m) * gain).astype(bf)
    def project(out, w, r0, nr):
        out[pl.ds(r0, nr), :] = jnp.dot(n1[pl.ds(r0, nr), :], w[...], preferred_element_type=f32).astype(bf)
    norm(0)
    local, a, b, f = [], [], [], []
    for m, (out, w, whole) in enumerate(((k, wk, kl), (v, wv, vl))):
        project(out, w, 0, half)
        for i in range(nl):
            n = m * nl + i
            src = out.at[pl.ds(i * 128, 128)]
            a.append(remote(src, whole.at[s, i], ss.at[n, 0], rs.at[n, 0], xdev))
            b.append(remote(src, whole.at[s, i], ss.at[n, 1], rs.at[n, 1], cdev))
            cp = pltpu.make_async_copy(src, whole.at[s, i], lsem.at[n]); cp.start(); local.append(cp)
    norm(1)
    project(k, wk, half, ns * 128)
    project(v, wv, half, ns * 128)
    project(q, wq, 0, half)
    project(q, wq, half, ns * 128)
    for t in range(2):
        n1t[:, t * half:(t + 1) * half] = n1[pl.ds(t * half, half), :].T
    for m, whole in enumerate((kl, vl)):
        for i in range(nl):
            n = m * nl + i
            a[n].wait_recv()
            f.append(remote(whole.at[far, i], whole.at[far, i], ss.at[n, 2], rs.at[n, 2], cdev))
    for n in range(2 * nl):
        local[n].wait(); a[n].wait_send(); b[n].wait(); f[n].wait()
def head(nl, ns, seq, experts, arrays, cid):
    tokens, width = (nl + ns) * 128, arrays[3].shape[1]
    S, sem, bf = jax.ShapeDtypeStruct, pltpu.SemaphoreType.DMA, jnp.bfloat16
    vm = pl.BlockSpec(memory_space=pltpu.VMEM)
    rows, long = S((tokens, width), bf), S((seq, nl, 128, width), bf)
    return pl.pallas_call(functools.partial(head_kernel, nl, ns, experts), out_shape=[rows] * 3 + [long] * 2 + [S((width, tokens), bf)],
        in_specs=[vm] * 6, out_specs=[vm] * 6,
        scratch_shapes=[pltpu.VMEM((tokens, width), bf), sem((2 * nl,)), sem((2 * nl, 3)), sem((2 * nl, 3))],
        compiler_params=pltpu.CompilerParams(collective_id=cid, has_side_effects=True, vmem_limit_bytes=48 * 2**20))(*arrays)

def back_kernel(dims, nl, ns, experts, pieces, q, k, v, kl, vl, tab, lb, sb, li, si, mg, wog, n1t, lx, sx, params, wq, wk, wv, midg, small_in,
                lgrad, sgrad, og, qg, kg, vg, small, *refs):
    X, C, Z, Y = dims
    blocks = X * C
    f32, bf = jnp.float32, jnp.bfloat16
    np_ = len(pieces)
    bufs = refs[:4 * np_]
    (gw, dq, ka, va, dkl, dvl, kcb, ka1, kb1, seg, sacc, sbuf, cs, cr, hs, hr, zs, zr, kss, krs, sss, srs) = refs[4 * np_:]
    s = lax.axis_index("seq"); g = lax.axis_index("dp")
    x, c = s // C, lax.rem(s, C)
    z, y = g // Y, lax.rem(g, Y)
    def zdev(k): return (s, lax.rem(z + k, Z) * Y + y)
    ydev = (s, z * Y + (1 - y)); xdev = ((1 - x) * C + c, g); cdev = (x * C + 1 - c, g)
    greet([zdev(k) for k in range(1, Z)] + [ydev, xdev, cdev])
    half = nl * 128
    wide = 256
    nb = q.shape[1] // wide
    sources = [wog] + [gw.at[i] for i in range(3)]
    outs = [og, qg, kg, vg]
    first = {}; hh = {}; zz = {}
    def add(dst, a, b):
        dst[...] = (a.astype(f32) + b.astype(f32)).astype(dst.dtype)
    def send_core(i):
        m, c0, nc = pieces[i]
        first[i] = remote(sources[m].at[:, 1 - c, :, :, :, pl.ds(c0, nc)], bufs[4 * i], cs.at[i], cr.at[i], cdev)
    def stage(i, which):
        m, c0, nc = pieces[i]
        b0, b1, b2, b3 = bufs[4 * i:4 * i + 4]
        if which == 0:
            first[i].wait_recv()
            add(b0, sources[m][:, c, :, :, :, c0:c0 + nc], b0[...])
            hh[i, 0] = remote(b0.at[:, :, 1 - y], b1, hs.at[i, 0], hr.at[i, 0], ydev)
        elif which == 1:
            hh[i, 0].wait_recv()
            add(b1, b0[:, :, y], b1[...])
            hh[i, 1] = remote(b1.at[1 - x], b2, hs.at[i, 1], hr.at[i, 1], xdev)
        elif which == 2:
            hh[i, 1].wait_recv()
            add(b2, b1[x], b2[...])
            zz[i] = [remote(b2.at[lax.rem(z + k, Z)], b3.at[k - 1], zs.at[i, k], zr.at[i, k], zdev(k)) for k in range(1, Z)]
        else:
            tot = b2[z].astype(f32)
            for k in range(1, Z):
                zz[i][k - 1].wait_recv()
                tot += b3[k - 1].astype(f32)
            outs[m][:, c0:c0 + nc] = tot
    def piece(m, b):
        return [i for i, p in enumerate(pieces) if p[0] == m and (m == 0 or p[1] == b * wide)]
    def weight_grad(m, rows, b):
        cols = slice(b * wide, (b + 1) * wide)
        quarter = n1t.shape[0] // blocks
        for xx in range(X):
            for cc in range(C):
                part = jnp.dot(n1t[pl.ds((xx * C + cc) * quarter, quarter), :], rows[:, cols], preferred_element_type=f32)
                gw[m - 1, xx, cc, :, :, :, cols] = part.astype(bf).reshape(gw.shape[3:6] + (wide,))
        for i in piece(m, b):
            send_core(i)
    parts, wholes = (dkl, dvl), (ka, va)
    kf, kx = {}, {}
    def kv_core(b):
        cols = pl.ds(b * wide, wide)
        for far in range(2):
            for m in range(2):
                n = b * 2 + m
                at = (1 - x if far == 0 else x) * C + 1 - c
                kf[n, far] = remote(parts[m].at[at, :, :, cols], kcb.at[n, far], kss.at[n, far], krs.at[n, far], cdev)
    def kv_chip(b):
        for m in range(2):
            n = b * 2 + m
            kf[n, 0].wait_recv()
            add(ka1.at[n], parts[m][(1 - x) * C + c, :, :, b * wide:(b + 1) * wide], kcb[n, 0])
            kx[n] = remote(ka1.at[n], kb1.at[n], kss.at[n, 2], krs.at[n, 2], xdev)
    def kv_end(b):
        for m in range(2):
            n = b * 2 + m
            kf[n, 1].wait_recv(); kx[n].wait_recv()
            tot = parts[m][s, :, :, b * wide:(b + 1) * wide].astype(f32) + kcb[n, 1].astype(f32) + kb1[n].astype(f32)
            wholes[m][pl.ds(0, half), b * wide:(b + 1) * wide] = tot.astype(bf).reshape(half, wide)
        weight_grad(2, ka, b)
        weight_grad(3, va, b)
    def stages(which, b, *ms):
        for m in ms:
            for i in piece(m, b):
                stage(i, which)
    seg[...] = jnp.zeros_like(seg)
    lane = lax.broadcasted_iota(jnp.int32, (128, 128), 1)
    head_one = lane < 64
    tri = jnp.where(lax.broadcasted_iota(jnp.int32, (128, 128), 0) <= lane, 1.0, 0.0).astype(bf)
    def attend(b0):
        @pl.loop(0, wide // 128)
        def _(i):
            hp = b0 * (wide // 128) + i
            cols = pl.ds(pl.multiple_of(hp * 128, 128), 128)
            for b in range(nl + ns):
                rows, n, kk, vv = item(b, nl, blocks, cols, k, v, kl, vl)
                idx = mine_of(b, nl, li, si)
                qs = stack_heads(q[rows, cols], head_one); gs = stack_heads(mg[rows, cols], head_one)
                p = probs_of(qs, kk, (tab[2 * hp], tab[2 * hp + 1]), mine_of(b, nl, lb, sb), n)
                dp = dot(gs, vv, 1, 1)
                ds = (p * (dp - jnp.sum(p * dp, axis=1, keepdims=True))).astype(bf)
                dqs = dot(ds, kk, 1, 0)
                dkt = dot(qs, ds, 0, 0)
                dvt = dot(gs, p.astype(bf), 0, 0)
                sums = [0, 0]
                for c_ in range(n):
                    pre = dot(ds[:, c_ * 128:(c_ + 1) * 128], tri, 1, 0)
                    at = idx[c_]
                    for e in range(2):
                        sums[e] += jnp.where(at >= 0, jnp.take_along_axis(pre[e * 128:(e + 1) * 128], jnp.maximum(at, 0), axis=1), 0.0)
                for e in range(2):
                    seg[2 * hp + e] += jnp.sum(sums[e], axis=0, keepdims=True)
                dq[rows, cols] = jnp.where(head_one, dqs[:128], dqs[128:]).astype(bf)
                dkt = dkt.T.astype(bf); dvt = dvt.T.astype(bf)
                if b < nl:
                    dkl[:, b, :, cols] = dkt.reshape(n, 128, 128); dvl[:, b, :, cols] = dvt.reshape(n, 128, 128)
                else:
                    ka[rows, cols] = dkt; va[rows, cols] = dvt
    for i in piece(0, 0):
        send_core(i)
    attend(0)
    kv_core(0); weight_grad(1, dq, 0); stages(0, 0, 0)
    attend(1)
    kv_core(1); kv_chip(0); weight_grad(1, dq, 1); stages(0, 0, 1); stages(1, 0, 0)
    attend(2)
    kv_core(2); kv_chip(1); kv_end(0); weight_grad(1, dq, 2); stages(0, 1, 1); stages(1, 0, 1); stages(2, 0, 0)
    attend(3)
    kv_core(3); kv_chip(2); kv_end(1); weight_grad(1, dq, 3); stages(0, 0, 2, 3); stages(0, 2, 1); stages(1, 1, 1); stages(2, 0, 1)
    kv_chip(3); kv_end(2); stages(0, 1, 2, 3); stages(0, 3, 1); stages(1, 0, 2, 3); stages(1, 2, 1); stages(2, 1, 1); stages(3, 0, 0)
    kv_end(3); stages(0, 2, 2, 3); stages(1, 3, 1); stages(1, 1, 2, 3); stages(2, 2, 1); stages(2, 0, 2, 3); stages(3, 0, 1)
    gain = params[experts:experts + 1, :].astype(f32)
    ag = jnp.zeros((1, q.shape[1]), f32)
    for t in range(2):
        rows = pl.ds(t * half, half)
        ng = dot(dq[rows, :], wq[...], 1, 1) + dot(ka[rows, :], wk[...], 1, 1) + dot(va[rows, :], wv[...], 1, 1)
        m = rows_of(lx, sx, t).astype(f32)
        r1 = rms_scale(m)
        u = m * r1
        ag += jnp.sum(ng * u, axis=0, keepdims=True)
        w = ng * gain
        (lgrad, sgrad)[t][...] = (midg[rows, :] + r1 * (w - u * jnp.mean(w * u, axis=-1, keepdims=True))).reshape(lgrad.shape)
        if t == 0:
            stages(0, 3, 2, 3); stages(1, 2, 2, 3); stages(2, 3, 1); stages(2, 1, 2, 3); stages(3, 1, 1)
    sacc[0] = small_in[...]
    sacc[0, 0:1, :] = ag
    heads = seg.shape[0]
    spot = lax.broadcasted_iota(jnp.int32, (8, 128), 1)
    for h in range(heads):
        upto = jnp.broadcast_to(seg[h], (8, 128))
        within = upto - jnp.where(spot == 0, 0.0, pltpu.roll(upto, 1, 1))
        at = jnp.where(spot < 16, 15 - spot, jnp.minimum(spot - 1, 30))
        by_bucket = jnp.where((spot == 16) | (spot >= 32), 0.0, jnp.take_along_axis(within, at, axis=1))
        r = 2 + experts + h // 8
        sacc[0, r:r + 1, (h % 8) * 128:(h % 8 + 1) * 128] = by_bucket[0:1, :]
    sc = remote(sacc.at[0], sbuf.at[0], sss.at[0], srs.at[0], cdev)
    stages(1, 3, 2, 3); stages(2, 2, 2, 3); stages(3, 2, 1)
    sc.wait_recv()
    sacc[1] = sacc[0] + sbuf[0]
    sx_ = remote(sacc.at[1], sbuf.at[1], sss.at[1], srs.at[1], xdev)
    stages(2, 3, 2, 3); stages(3, 3, 1); stages(3, 0, 2, 3)
    sx_.wait_recv()
    sacc[2] = sacc[1] + sbuf[1]
    sy = remote(sacc.at[2], sbuf.at[2], sss.at[2], srs.at[2], ydev)
    stages(3, 1, 2, 3)
    sy.wait_recv()
    sacc[3] = sacc[2] + sbuf[2]
    sz = [remote(sacc.at[3], sbuf.at[2 + k], sss.at[2 + k], srs.at[2 + k], zdev(k)) for k in range(1, Z)]
    stages(3, 2, 2, 3); stages(3, 3, 2, 3)
    tot = sacc[3]
    for k in range(1, Z):
        sz[k - 1].wait_recv()
        tot += sbuf[2 + k]
    small[...] = tot
    for cp in [sc, sx_, sy] + sz + list(kx.values()) + list(kf.values()) + list(first.values()) + list(hh.values()) + [w for v_ in zz.values() for w in v_]:
        cp.wait_send()
def back(dims, nl, ns, experts, arrays, cid):
    X, C, Z, Y = dims
    q_, small_in = arrays[0], arrays[-1]
    tokens, width = q_.shape
    heads = arrays[5].shape[0]
    nr = width // (X * C * Z * Y)
    wide = 256
    pieces = tuple((0, h * 512, 512) for h in range(width // 512)) + tuple((m, b * wide, wide) for m in range(1, 4) for b in range(width // wide))
    n = len(pieces)
    S, sem, bf, f32 = jax.ShapeDtypeStruct, pltpu.SemaphoreType.DMA, jnp.bfloat16, jnp.float32
    V = pltpu.VMEM
    scr = [V(lead + (nr, nc), bf) for m, c0, nc in pieces for lead in ((X, Z, Y), (X, Z), (Z,), (Z - 1,))]
    kvn = 2 * (width // wide)
    long = V((X * C, nl, 128, width), bf)
    rows = V((tokens, width), bf)
    scr += [V((3, X, C, Z, Y, nr, width), bf), rows, rows, rows, long, long,
            V((kvn, 2, nl, 128, wide), bf), V((kvn, nl, 128, wide), bf), V((kvn, nl, 128, wide), bf), V((heads, 1, 128), f32),
            V((4,) + small_in.shape, f32), V((Z + 2,) + small_in.shape, f32),
            sem((n,)), sem((n,)), sem((n, 2)), sem((n, 2)), sem((n, Z)), sem((n, Z)), sem((kvn, 3)), sem((kvn, 3)), sem((Z + 2,)), sem((Z + 2,))]
    vm = pl.BlockSpec(memory_space=pltpu.VMEM)
    outs = [S((nl, 128, width), f32), S((ns, 128, width), f32)] + [S((nr, width), f32)] * 4 + [S(small_in.shape, f32)]
    return pl.pallas_call(functools.partial(back_kernel, dims, nl, ns, experts, pieces), out_shape=outs,
        in_specs=[vm] * len(arrays), out_specs=[vm] * len(outs), scratch_shapes=scr,
        compiler_params=pltpu.CompilerParams(collective_id=cid, has_side_effects=True, vmem_limit_bytes=63 * 2**20))(*arrays)

def gelu_parts(v):
    c, a = 0.7978845608, 0.044715
    v2 = v * v
    t = jnp.tanh(c * v * (1.0 + a * v2))
    half = 0.5 * (1.0 + t)
    return v * half, half + 0.5 * v * (1.0 - t * t) * (c * (1.0 + 3.0 * a * v2))
RING, LAG = 6, 4
def expert_kernel(cap, per, order, todo, wcut, tile, whole_down, xs, gs, wgi, wui, wdi, eo_out, ri_out, grads, eo_h, ri_h,
                  wall, xr, gr, hall, lall, eo, ri, cb, ab, xb, ob,
                  lsem, xss, xrs, gss, grs, ess, ers, rss, rrs, wss, wrs, wls, css, crs, ass, ars, osem, free):
    dp = lax.axis_size("dp")
    f32, bf = jnp.float32, jnp.bfloat16
    s, x, c, xdev, cdev = seq_places(2)
    g = lax.axis_index("dp")
    def peer(k): return (s, g ^ k)
    greet([xdev, cdev] + [peer(k) for k in range(1, dp)])
    rows_w, ff = wgi.shape; width = xs.shape[2]
    piece = rows_w // wcut
    wx, wc, wl = [], [], []
    shared = ((wgi, 1), (wui, 2)) if whole_down else ((wgi, 1), (wui, 2), (wdi, 0))
    parts = [(src, m, h * piece) for h in range(wcut) for src, m in shared]
    for n, (src, m, r0) in enumerate(parts):
        a = src.at[pl.ds(r0, piece)]
        b = wall.at[m, x, c, pl.ds(r0, piece)]
        wx.append(remote(a, b, wss.at[n, 0], wrs.at[n, 0], xdev))
        wc.append(remote(a, b, wss.at[n, 1], wrs.at[n, 1], cdev))
        cp = pltpu.make_async_copy(a, b, wls.at[n]); cp.start(); wl.append(cp)
    if whole_down:
        cp = pltpu.make_async_copy(wdi, wall.at[0], wls.at[len(parts)]); cp.start(); wl.append(cp)
    sx, sg = {}, {}
    for k in [k for p in order for k in range(p * per, (p + 1) * per)]:
        at = pl.ds(k * cap, cap)
        if k == 0:
            sx[0] = pltpu.make_async_copy(xs.at[g], xr.at[at], lsem.at[0]); sx[0].start()
            sg[0] = pltpu.make_async_copy(gs.at[g], gr.at[at], lsem.at[1]); sg[0].start()
        else:
            sx[k] = remote(xs.at[g ^ k], xr.at[at], xss.at[k], xrs.at[k], peer(k))
            sg[k] = remote(gs.at[g ^ k], gr.at[at], gss.at[k], grs.at[k], peer(k))
    wf = []
    for n, (src, m, r0) in enumerate(parts):
        wx[n].wait_recv()
        b = wall.at[m, 1 - x, c, pl.ds(r0, piece)]
        wf.append(remote(b, b, wss.at[n, 2], wrs.at[n, 2], cdev))
    for cp in wl: cp.wait()
    for n in range(len(parts)):
        wc[n].wait_recv(); wf[n].wait_recv()
    ntile = ff // tile
    re, rr = {}, {}
    wide = 4 * rows_w
    for p in todo:
        ks = list(range(p * per, (p + 1) * per))
        for k in ks:
            if k == 0: sx[0].wait(); sg[0].wait()
            else: sx[k].wait_recv(); sg[k].wait_recv()
        rows = pl.ds(p * per * cap, per * cap)
        @pl.loop(0, ntile)
        def _(t):
            cols = pl.ds(pl.multiple_of(t * tile, 128), tile)
            w = lambda m: wall[m, :, :, :, cols].reshape(wide, tile)
            gp = jnp.dot(xr[rows, :], w(1), preferred_element_type=f32)
            up = jnp.dot(xr[rows, :], w(2), preferred_element_type=f32)
            hg = jnp.dot(gr[rows, :], w(0), preferred_element_type=f32)
            act, der = gelu_parts(gp)
            hall[0, rows, cols] = (act * up).astype(bf)
            hall[1, rows, cols] = (hg * up * der).astype(bf)
            hall[2, rows, cols] = (hg * act).astype(bf)
        @pl.loop(0, 4)
        def _(t):
            part = pl.ds(pl.multiple_of(t * rows_w, 128), rows_w)
            tx, tc = t // 2, lax.rem(t, 2)
            eo[:, part] = dot(hall[0, rows, :], wall[0, tx, tc], 1, 1).astype(bf)
            ri[:, part] = (dot(hall[1, rows, :], wall[1, tx, tc], 1, 1) + dot(hall[2, rows, :], wall[2, tx, tc], 1, 1)).astype(bf)
        keep = [pltpu.make_async_copy(eo, eo_h.at[rows], lsem.at[4]), pltpu.make_async_copy(ri, ri_h.at[rows], lsem.at[5])]
        for cp in keep: cp.start()
        for cp in keep: cp.wait()
        for k in ks:
            at = pl.ds(k * cap, cap)
            if k == 0:
                re[0] = pltpu.make_async_copy(eo_h.at[at], eo_out.at[g], lsem.at[2]); re[0].start()
                rr[0] = pltpu.make_async_copy(ri_h.at[at], ri_out.at[g], lsem.at[3]); rr[0].start()
            else:
                re[k] = remote(eo_h.at[at], eo_out.at[g], ess.at[k], ers.at[k], peer(k))
                rr[k] = remote(ri_h.at[at], ri_out.at[g], rss.at[k], rrs.at[k], peer(k))
    for n in range(len(parts)):
        wx[n].wait_send(); wc[n].wait_send(); wf[n].wait_send()
    total = dp * cap
    @pl.loop(0, total // 256)
    def _(t):
        at = pl.ds(pl.multiple_of(t * 256, 256), 256)
        lall[1, :, at] = xr[at, :].T
        lall[0, :, at] = gr[at, :].T
    nt = 3 * ntile
    def place(n):
        m = n // ntile
        return m, pl.ds(pl.multiple_of((n - m * ntile) * tile, 128), tile)
    def to_core(n):
        m, cols = place(n); r = lax.rem(n, RING)
        return pltpu.make_async_remote_copy(src_ref=wall.at[m, :, 1 - c, :, cols], dst_ref=cb.at[r], send_sem=css.at[r],
            recv_sem=crs.at[r], device_id=cdev, device_id_type=MESH)
    def to_chip(n):
        r = lax.rem(n, RING)
        return pltpu.make_async_remote_copy(src_ref=ab.at[r], dst_ref=xb.at[r], send_sem=ass.at[r],
            recv_sem=ars.at[r], device_id=xdev, device_id_type=MESH)
    def to_out(n):
        m, cols = place(n); r = lax.rem(n, 2)
        return pltpu.make_async_copy(ob.at[r], grads.at[m, :, cols], osem.at[r])
    @pl.loop(0, nt + LAG)
    def _(n):
        @pl.when(n < nt)
        def _():
            m, cols = place(n)
            res = jnp.dot(lall[jnp.minimum(m, 1)], hall[m, :, cols], preferred_element_type=f32)
            wall[m, :, :, :, cols] = res.astype(bf).reshape(2, 2, rows_w, tile)
            @pl.when(n >= RING)
            def _(): pl.semaphore_wait(free.at[0], 1)
            to_core(n).start()
        @pl.when((n >= 1) & (n <= nt))
        def _():
            i = n - 1
            m, cols = place(i); r = lax.rem(i, RING)
            to_core(i).wait_recv()
            @pl.when(i >= RING)
            def _():
                to_chip(i).wait_send()
                pl.semaphore_wait(free.at[1], 1)
            ab[r] = (wall[m, 1 - x, c, :, cols].astype(f32) + cb[r, 1 - x].astype(f32)).astype(bf)
            to_chip(i).start()
        @pl.when(n >= LAG)
        def _():
            j = n - LAG
            m, cols = place(j); r = lax.rem(j, RING)
            to_chip(j).wait_recv()
            to_core(j).wait_send()
            @pl.when(j >= 2)
            def _(): to_out(j).wait()
            ob[lax.rem(j, 2)] = wall[m, x, c, :, cols].astype(f32) + cb[r, x].astype(f32) + xb[r].astype(f32)
            to_out(j).start()
            @pl.when(j < nt - RING)
            def _():
                pl.semaphore_signal(free.at[0], inc=1, device_id=cdev, device_id_type=MESH)
                pl.semaphore_signal(free.at[1], inc=1, device_id=xdev, device_id_type=MESH)
    for j in range(nt - 2, nt): to_out(j).wait()
    for i in range(nt - RING, nt): to_chip(i).wait_send()
    for k in range(dp):
        if k == 0:
            re[0].wait(); rr[0].wait()
        else:
            sx[k].wait_send(); sg[k].wait_send(); re[k].wait(); rr[k].wait()
def expert_all(xs, gs, wg, wu, wd, seq, cid):
    dp, cap, width = xs.shape
    rows_w, ff = wg.shape; total = dp * cap
    whole_down = wd.shape[0] != rows_w
    if whole_down: wd = wd.reshape(seq // 2, 2, rows_w, ff)
    group = 320
    per = group // cap
    ng = dp // per
    order = [p for p in range(ng // 2, ng)] + [p for p in range(ng // 2 - 1, -1, -1)]
    todo = list(range(ng))
    sem = pltpu.SemaphoreType.DMA
    bf = jnp.bfloat16
    any_ = pl.BlockSpec(memory_space=pl.ANY)
    V = pltpu.VMEM
    tile = 256
    wcut = 2
    back = jax.ShapeDtypeStruct((dp, cap, width), bf)
    flat = jax.ShapeDtypeStruct((total, width), bf)
    return pl.pallas_call(functools.partial(expert_kernel, cap, per, order, todo, wcut, tile, whole_down),
        out_shape=[back, back, jax.ShapeDtypeStruct((3, rows_w, ff), jnp.float32), flat, flat],
        in_specs=[any_] * 5, out_specs=[any_] * 5,
        scratch_shapes=[V((3, seq // 2, 2, rows_w, ff), bf), V((total, width), bf), V((total, width), bf), V((3, total, ff), bf),
        V((2, width, total), bf), V((group, width), bf), V((group, width), bf),
        V((RING, seq // 2, rows_w, tile), bf), V((RING, rows_w, tile), bf), V((RING, rows_w, tile), bf), V((2, rows_w, tile), jnp.float32)]
        + [sem((6,))] + [sem((dp,))] * 8 + [sem((3 * wcut, 3))] * 2 + [sem((3 * wcut + 1,))] + [sem((RING,))] * 4 + [sem((2,)), pltpu.SemaphoreType.REGULAR((2,))],
        compiler_params=pltpu.CompilerParams(collective_id=cid, has_side_effects=True, vmem_limit_bytes=63 * 2**20))(xs, gs, wg, wu, wd)[:3]


def on_device(
    long_tokens,
    short_tokens,
    long_grad_out,
    short_grad_out,
    query_weight,
    key_weight,
    value_weight,
    output_weight,
    attn_gain,
    ffn_gain,
    rel_table,
    router_weight,
    gate_weight,
    up_weight,
    down_weight,
    long_positions,
    short_positions,
    long_lengths,
    short_lengths,
    long_routes,
    short_routes,
):
    long_items, quarter, model_width = long_tokens.shape
    short_items, short_len = (short_tokens.shape[0], short_tokens.shape[1])
    long_rows = long_items * quarter
    tokens = long_rows + short_items * short_len
    local_experts = gate_weight.shape[0]
    dp_size = lax.axis_size("dp")
    experts = local_experts * dp_size
    capacity = (5 * tokens + 2 * experts - 1) // (2 * experts)
    seq_size = lax.axis_size("seq")
    dims = (seq_size // 2, 2, dp_size // 2, 2)
    devices = seq_size * dp_size
    table_part, gain_part = rel_table.shape[0], attn_gain.shape[0]
    small = jnp.concatenate([router_weight.T, attn_gain[None], ffn_gain[None]], 0)
    small = jnp.pad(small, ((0, 1), (0, 128 - gain_part)))
    table_row = jnp.pad(rel_table[None], ((experts + 2, 0), (0, 128 - table_part)))
    small = jnp.pad(small + table_row, ((0, -(experts + 3) % 16), (0, 0)))
    rows_part = query_weight.shape[0]
    cuts = 2 if rows_part % 32 == 0 else 1
    cut = rows_part // cuts
    pieces = tuple((m, h * cut, cut, (m + h) % 2) for m in range(4) for h in range(cuts))
    gathered = gather_all(
        (query_weight, key_weight, value_weight, output_weight, small),
        pieces[: 3 * cuts] + ((4, 0, small.shape[0], 0),) + pieces[3 * cuts :],
        dims,
        0,
    )
    query_all, key_all, value_all, output_all = (
        block.reshape(devices * rows_part, model_width) for block in gathered[:4]
    )
    small_all = gathered[4].reshape(devices, small.shape[0], 128)
    params = small_all[:, : experts + 2, :gain_part].transpose(1, 0, 2)
    params = jnp.pad(params.reshape(experts + 2, model_width), ((0, 126 - experts), (0, 0)))
    table = small_all[:, experts + 2, :table_part].reshape(HEADS, 1, BUCKETS).astype(jnp.float32)
    table = jnp.pad(table, ((0, 0), (0, 0), (0, 128 - BUCKETS)), constant_values=masked)
    queries, keys, values, long_keys, long_values, normed_t = head(
        long_items,
        short_items,
        seq_size,
        experts,
        (long_tokens, short_tokens, params, query_all, key_all, value_all),
        1,
    )
    sizes = (long_items, short_items, seq_size, experts, capacity)
    heads_args = (queries, keys, values, long_keys, long_values, table)
    places = (long_positions, short_positions)
    grads = (long_grad_out, short_grad_out, output_all, params)
    routes = (long_routes, short_routes)
    mixed, middle, outgoing, out_slots, logits, long_buckets, short_buckets = attention(
        *sizes,
        (long_lengths, short_lengths)
        + heads_args
        + places
        + (long_tokens, short_tokens)
        + grads
        + routes,
        tokens,
        model_width,
    )
    later_down, unused_keys = lax.optimization_barrier((down_weight[0], long_keys))
    down_full = lax.all_gather(later_down, "seq", axis=0, tiled=True)
    back_rows, back_grads, expert_grads = expert_all(
        outgoing, out_slots, gate_weight[0], up_weight[0], down_full, seq_size, 4
    )
    (
        long_out,
        short_out,
        middle_grad,
        output_local,
        small_local,
        mixed_grad,
        long_places,
        short_places,
        down_grad,
        gate_grad,
        up_grad,
    ) = post(
        *sizes,
        dims + (rows_part, model_width),
        places + (back_rows, back_grads, middle, mixed, logits) + routes + grads + (expert_grads,),
        tokens,
        model_width,
    )
    long_grad_in, short_grad_in, output_grad, query_grad, key_grad, value_grad, small_sum = back(
        dims,
        long_items,
        short_items,
        experts,
        heads_args
        + (long_buckets, short_buckets, long_places, short_places)
        + (mixed_grad, output_local, normed_t, long_tokens, short_tokens, params)
        + (query_all, key_all, value_all, middle_grad, small_local),
        2,
    )
    place = lax.axis_index("seq") * dp_size + lax.axis_index("dp")

    def own(row, column, size, count=1):
        return lax.dynamic_slice(small_sum, (row, column), (count, size))

    entry = place * table_part
    head_at = entry // BUCKETS
    table_grad = own(2 + experts + head_at // 8, head_at % 8 * 128 + entry % BUCKETS, table_part)
    summed = (
        query_grad,
        key_grad,
        value_grad,
        output_grad,
        own(0, place * gain_part, gain_part)[0],
        own(1, place * gain_part, gain_part)[0],
        table_grad[0],
        own(2, place * rows_part, rows_part, experts).T,
    )
    return (
        long_out,
        short_out,
        long_grad_in,
        short_grad_in,
        summed[0],
        summed[1],
        summed[2],
        summed[3],
        summed[4],
        summed[5],
        summed[6],
        summed[7],
        gate_grad,
        up_grad,
        down_grad,
    )


def solution(mesh):
    placed = (
        P("dp", "seq", None),
        P(("seq", "dp"), None, None),
        P("dp", "seq", None),
        P(("seq", "dp"), None, None),
        P(("seq", "dp"), None),
        P(("seq", "dp"), None),
        P(("seq", "dp"), None),
        P(("seq", "dp"), None),
        P(("seq", "dp")),
        P(("seq", "dp")),
        P(("seq", "dp")),
        P(("seq", "dp"), None),
        P("dp", "seq", None),
        P("dp", "seq", None),
        P("dp", "seq", None),
        P("dp", None),
        P(("seq", "dp"), None),
        P("dp"),
        P(("seq", "dp")),
        P("dp", "seq", None),
        P(("seq", "dp"), None, None),
    )
    return jax.shard_map(
        on_device,
        mesh=mesh,
        in_specs=placed,
        out_specs=(
            P("dp", "seq", None),
            P(("seq", "dp"), None, None),
            P("dp", "seq", None),
            P(("seq", "dp"), None, None),
            P(("seq", "dp"), None),
            P(("seq", "dp"), None),
            P(("seq", "dp"), None),
            P(("seq", "dp"), None),
            P(("seq", "dp")),
            P(("seq", "dp")),
            P(("seq", "dp")),
            P(("seq", "dp"), None),
            P("dp", "seq", None),
            P("dp", "seq", None),
            P("dp", "seq", None),
        ),
        check_vma=False,
    )
```

time: 591 us -> 532 us (0.900)
  matrix products: 26.5 us -> 0 us
  Pallas kernels: 508 us -> 487 us
  local copies, waits for them, and re-layouts: 30 us -> 21 us
  other arithmetic: 8.06 us -> 0.73 us
    dot_general x9 -> x0, matrix products: 26.5 us -> none  [the longest x3 8.82 us: on_device(): jnp.dot(normed, matrix, preferred_element_type=jnp.float32)]
    pallas_call x5 -> x4, Pallas kernels: 216 us -> 195 us  [the longest x1 104 us: back(): pl.pallas_call(functools.partial(back_kernel, dims, nl, ns, experts, piec...]
    slice x10 -> x1, local copies, waits for them, and re-layouts: 11.2 us -> 0.86 us  [on_device(): small_all[:, experts + 2, :table_part].reshape(HEADS, 1, BUCKETS)]
    unnamed x64 -> x37, local copies, waits for them, and re-layouts: 11.4 us -> 14.6 us
  transfers between devices with their start and end apart: 1 -> 1, of which waited for: 0 -> 1; matrix products, arithmetic and copies ran while one was open for 2% -> 1% of each run, Pallas kernels for 6% -> 7%
where the time goes in v6:
time: 532 us; the launch traced here: 529 us
  Pallas kernels  487 us (92%)
  local copies, waits for them, and re-layouts  21 us (4%)
  between operations  14.5 us (3%)
  waiting for transfers between devices  5.73 us (1%)
    pallas_call x1, Pallas kernels, expert_all(): pl.pallas_call(functools.partial(expert_kernel, cap, per, order, todo, wc...  232 us
    pallas_call x1, Pallas kernels, back(): pl.pallas_call(functools.partial(back_kernel, dims, nl, ns, experts, piec...  104 us
    pallas_call x1, Pallas kernels, gather_all(): pl.pallas_call(functools.partial(gather_kernel, dims, pieces, na), out_sh...  60.1 us
    pallas_call x1, Pallas kernels, attention(): pl.pallas_call(functools.partial(attn_fwd_kernel, nl, ns, blocks, experts...  34.5 us
    pallas_call x1, Pallas kernels, head(): pl.pallas_call(functools.partial(head_kernel, nl, ns, experts), out_shape...  33.2 us
    pallas_call x1, Pallas kernels, post(): pl.pallas_call(functools.partial(post_kernel, nl, ns, blocks, experts, ca...  23.6 us
    unnamed x37, local copies, waits for them, and re-layouts  14.6 us
  transfers between devices with their start and end apart: 1, of which 1 were waited for; matrix products, arithmetic and copies ran while one was open for 1% of the time, Pallas kernels for 7%

profile of v6, /device:TPU:0, one launch (start us, length us, event | category | flops | bytes accessed | tf_op | source)
XLA Modules:
  0.0 529.1 jit_solution(17617950136836750320)
XLA Ops:
  7.2 0.0 all-gather.2.cloned.1.call-start
  7.2 0.7 fusion.9
  8.0 0.6 pad.22.refs_4_
  8.6 60.1 %shard_map.316 = (bf16[2,2,4,2,32,1024]{5,4,3,2,1,0:T(8,128)(2,1)}, bf16[2,2,4,2,32,1024]{5,4,3,2,1,0:T(8,128)(2,1)}, bf16[2,2,4,2,32,1024]{5,4,3,2,1,0:T(8,128)...) custom-call(bf16[32,1024]{1,0:T(8,128)(2,1)} %refs_0_.1, bf16[32,1024]{1,0:T(8,128)(2,1)} %refs_1_.1, ...), custom_call_target="tpu_custom_call" | custom-call | tf_op jit(solution)/shard_map/pallas_call | solution.py:84
  68.6 0.9 copy.53
  69.6 0.1 reshape.66
  69.7 0.0 copy-start
  69.7 0.0 copy-start.1
  69.8 1.1 copy-done.1
  70.9 0.0 copy-start.2
  70.9 1.0 copy-done.2
  71.9 0.0 copy-start.12
  71.9 0.0 copy-start.13
  71.9 33.2 %shard_map.317 = (bf16[512,1024]{1,0:T(8,128)(2,1)S(1)}, bf16[512,1024]{1,0:T(8,128)(2,1)S(1)}, bf16[512,1024]{1,0:T(8,128)(2,1)S(1)}, bf16[4,2,128,1024]{3,2,1,...) custom-call(bf16[2,128,1024]{2,1,0:T(8,128)(2,1)S(1)} %copy-done.1, ...), custom_call_target="tpu_custom_call" | custom-call | tf_op jit(solution)/shard_map/pallas_call | solution.py:340
  105.1 0.0 copy-done
  105.1 0.0 copy-start.3
  105.1 1.0 copy-done.3
  106.1 1.0 copy-done.4
  107.1 1.0 copy-done.5
  108.1 1.0 copy-done.6
  109.1 0.0 all-gather.2.cloned.1.call-update
  109.1 0.9 slice.9
  110.0 0.1 reshape.72
  110.1 0.0 copy-done.12
  110.1 0.8 copy.45.lr
  110.9 0.0 copy-done.13
  110.9 0.8 copy.46.sr
  111.7 0.6 pad.24.tab
  112.3 34.5 %shard_map.318 = (bf16[512,1024]{1,0:T(8,128)(2,1)}, f32[512,1024]{1,0:T(8,128)}, bf16[8,160,1024]{2,1,0:T(8,128)(2,1)}, bf16[8,160,1024]{2,1,0:T(8,128)(2,1)}, ...) custom-call(s32[2]{0:T(128)} %ll.1, s32[2]{0:T(128)} %sl.1, ...), custom_call_target="tpu_custom_call" | custom-call | tf_op jit(solution)/shard_map/pallas_call | solution.py:283
  146.8 5.7 %all-gather.2.cloned.1.call-done = bf16[1024,2816]{1,0:T(8,128)(2,1)} async-done(((bf16[256,2816]{1,0:T(8,128)(2,1)}), bf16[1024,2816]{1,0:T(8,128)(2,1)}) %all-gather.2.cloned.1.call-update) | async-done | bytes 5767184 | tf_op jit(solution)/shard_map/all_gather | solution.py:802
  152.5 231.9 %shard_map.319 = (bf16[8,160,1024]{2,1,0:T(8,128)(2,1)}, bf16[8,160,1024]{2,1,0:T(8,128)(2,1)}, f32[3,256,2816]{2,1,0:T(8,128)}, bf16[1280,1024]{1,0:T(8,128)(2,1)}, bf16[1280,1024]{1,0:T(8,128)(2,1)}) custom-call(bf16[8,160,1024]{2,1,0:T(8,128)(2,1)} %get-tuple-element.65.xs, bf16[8,160,1024]{2,1,0:T(8,128)(2,1)} %get-tuple-element.66.gs, ...), custom_call_target="tpu_custom_call" | custom-call | tf_op jit(solution)/shard_map/pallas_call | solution.py:710
  384.4 23.6 %shard_map.320 = (bf16[2,128,1024]{2,1,0:T(8,128)(2,1)}, bf16[2,128,1024]{2,1,0:T(8,128)(2,1)}, f32[512,1024]{1,0:T(8,128)}, bf16[2,2,4,2,32,1024]{5,4,3,2,1,0:T...) custom-call(s32[2,512]{1,0:T(2,128)} %lpos.3, ...), custom_call_target="tpu_custom_call" | custom-call | tf_op jit(solution)/shard_map/pallas_call | solution.py:295
  408.0 103.9 %shard_map.321 = (f32[2,128,1024]{2,1,0:T(8,128)}, f32[2,128,1024]{2,1,0:T(8,128)}, f32[32,1024]{1,0:T(8,128)}, f32[32,1024]{1,0:T(8,128)}, f32[32,1024]{1,0:T(8...) custom-call(bf16[512,1024]{1,0:T(8,128)(2,1)} %copy-done.3, bf16[512,1024]{1,0:T(8,128)(2,1)} %copy-done.4, ...), custom_call_target="tpu_custom_call" | custom-call | tf_op jit(solution)/shard_map/pallas_call | solution.py:540
  511.9 0.0 copy-start.7
  511.9 1.5 dynamic-slice_bitcast_fusion
  513.3 1.3 dynamic-slice_bitcast_fusion.2
  514.7 1.3 dynamic-slice_bitcast_fusion.1
  516.0 2.4 copy.60
  518.3 0.0 copy-done.7
  518.3 1.0 copy.61
  519.3 0.0 copy-done.11
  519.3 0.7 copy.62
  520.0 0.0 copy-done.10
  520.0 0.7 copy.63
  520.6 0.0 copy-done.9
  520.6 0.7 copy.64
  521.3 0.0 copy-done.8
  521.3 0.7 copy.65
  (9 shorter events, 0.0 us)
Async XLA Ops:
  7.2 145.3 %all-gather.2.cloned.1.call-start = ((), (), s32[]{:S(2)}) async-start(), calls=%async_computation | async-start | bytes 7208960 | tf_op jit(solution)/shard_map/all_gather | solution.py:802
  69.7 35.4 %copy-start = (bf16[128,1024]{1,0:T(8,128)(2,1)}, bf16[128,1024]{1,0:T(8,128)(2,1)S(1)}, u32[]{:S(2)}) copy-start(bf16[128,1024]{1,0:T(8,128)(2,1)S(1)} %pad.23.params) | copy-start | bytes 786436
  69.7 1.1 copy-start.1
  70.9 1.0 copy-start.2
  71.9 38.2 %copy-start.12 = (s32[2,128,2]{1,2,0:T(2,128)S(1)}, s32[2,128,2]{1,2,0:T(2,128)}, u32[]{:S(2)}) copy-start(s32[2,128,2]{1,2,0:T(2,128)} %param.40) | copy-start | bytes 6148
  71.9 39.0 %copy-start.13 = (s32[2,128,2]{1,2,0:T(2,128)S(1)}, s32[2,128,2]{1,2,0:T(2,128)}, u32[]{:S(2)}) copy-start(s32[2,128,2]{1,2,0:T(2,128)} %param.41) | copy-start | bytes 6148
  105.1 1.0 copy-start.3
  106.1 1.0 copy-start.4
  107.1 1.0 copy-start.5
  108.1 1.0 copy-start.6
  511.9 6.5 %copy-start.7 = (f32[2,128,1024]{2,1,0:T(8,128)S(1)}, f32[2,128,1024]{2,1,0:T(8,128)}, u32[]{:S(2)}) copy-start(f32[2,128,1024]{2,1,0:T(8,128)} %get-tuple-element.115) | copy-start | bytes 3145732
  516.0 3.4 copy-start.11
  516.0 4.0 copy-start.10
  516.0 4.7 copy-start.9
  516.0 5.3 %copy-start.8 = (f32[32,1024]{1,0:T(8,128)S(1)}, f32[32,1024]{1,0:T(8,128)}, u32[]{:S(2)}) copy-start(f32[32,1024]{1,0:T(8,128)} %get-tuple-element.119) | copy-start | bytes 393220
Sparse Core Ops, SparseCore 0:
  109.2 43.2 all-gather.1

commit v7 on v6

--- a/solution.py
+++ b/solution.py
@@ -16,76 +16,6 @@
 
 epsilon = 1e-06
 masked = -1e30
-
-
-def gather_kernel(dims, pieces, na, *refs):
-    X, C, Z, Y = dims
-    n = len(pieces)
-    lsem, zs, zr, hs, hr, cs, cr = refs[2*na:]
-    routes = [p[3] for p in pieces]
-    ins = [refs[m].at[pl.ds(r0, nr)] for m, r0, nr, _ in pieces]
-    class V:
-        def __init__(self, ref, r0, nr): self.ref, self.r0, self.nr = ref, r0, nr
-        @property
-        def at(self): return self
-        def __getitem__(self, k):
-            k = k + (slice(None),) * (4 - len(k)) + (pl.ds(self.r0, self.nr),)
-            return self.ref.at[k]
-    outs = [V(refs[na + m], r0, nr) for m, r0, nr, _ in pieces]
-    s = lax.axis_index("seq"); g = lax.axis_index("dp")
-    x, c = s // C, lax.rem(s, C)
-    z, y = g // Y, lax.rem(g, Y)
-    def zdev(k): return (s, lax.rem(z + k, Z) * Y + y)
-    ydev = (s, z * Y + (1 - y)); xdev = ((1 - x) * C + c, g); cdev = (x * C + 1 - c, g)
-    bar = pltpu.get_barrier_semaphore()
-    for d in [zdev(k) for k in range(1, Z)] + [ydev, xdev, cdev]:
-        pl.semaphore_signal(bar, inc=1, device_id=d, device_id_type=MESH)
-    pl.semaphore_wait(bar, Z + 2)
-    def rc(src, dst, ss, rs, dev):
-        cp = pltpu.make_async_remote_copy(src_ref=src, dst_ref=dst, send_sem=ss, recv_sem=rs, device_id=dev, device_id_type=MESH)
-        cp.start(); return cp
-    sends = []
-    local = []; zc = []
-    for m in range(n):
-        lc = pltpu.make_async_copy(ins[m], outs[m].at[x, c, z, y], lsem.at[m]); lc.start(); local.append(lc)
-        zc.append([rc(ins[m], outs[m].at[x, c, z, y], zs.at[m, k], zr.at[m, k], zdev(k)) for k in range(1, Z)])
-    h = [[None, None] for _ in range(n)]
-    cc = [[None]*3 for _ in range(n)]
-    for t in range(n + 2):
-        for stage in range(3):
-            m = t - stage
-            if not 0 <= m < n: continue
-            o = outs[m]; route = routes[m]
-            if stage == 0:
-                local[m].wait()
-                for q in zc[m]: q.wait_recv()
-                mine = o.at[x, c, :, y]
-                h[m][0] = rc(mine, mine, hs.at[m,0], hr.at[m,0], xdev if route == 0 else ydev)
-                cc[m][0] = rc(mine, mine, cs.at[m,0], cr.at[m,0], cdev)
-            elif stage == 1:
-                h[m][0].wait_recv()
-                if route == 0:
-                    both = o.at[:, c, :, y]; got = o.at[1 - x, c, :, y]
-                else:
-                    both = o.at[x, c]; got = o.at[x, c, :, 1 - y]
-                h[m][1] = rc(both, both, hs.at[m,1], hr.at[m,1], ydev if route == 0 else xdev)
-                cc[m][1] = rc(got, got, cs.at[m,1], cr.at[m,1], cdev)
-            else:
-                h[m][1].wait_recv()
-                got = o.at[:, c, :, 1 - y] if route == 0 else o.at[1 - x, c]
-                cc[m][2] = rc(got, got, cs.at[m,2], cr.at[m,2], cdev)
-    for m in range(n):
-        for q in zc[m]: q.wait_send()
-        for q in h[m]: q.wait_send()
-        for q in cc[m]: q.wait()
-def gather_all(arrays, pieces, dims, cid):
-    X, C, Z, Y = dims; na = len(arrays); n = len(pieces)
-    sem = pltpu.SemaphoreType.DMA
-    return pl.pallas_call(functools.partial(gather_kernel, dims, pieces, na),
-        out_shape=[jax.ShapeDtypeStruct((X, C, Z, Y) + a.shape, a.dtype) for a in arrays],
-        in_specs=[pl.BlockSpec(memory_space=pl.ANY)] * na, out_specs=[pl.BlockSpec(memory_space=pl.ANY)] * na,
-        scratch_shapes=[sem((n,)), sem((n, Z)), sem((n, Z)), sem((n, 2)), sem((n, 2)), sem((n, 3)), sem((n, 3))],
-        compiler_params=pltpu.CompilerParams(collective_id=cid, has_side_effects=True))(*arrays)
 
 
 def seq_places(C):
@@ -138,36 +68,151 @@
     rows = pl.ds(b * 128, 128)
     if b < nl:
         return rows, blocks, kl[:, b, :, cols].reshape(blocks * 128, 128), vl[:, b, :, cols].reshape(blocks * 128, 128)
-    return rows, 1, k[rows, cols], v[rows, cols]
+    short = pl.ds((b - nl) * 128, 128)
+    return rows, 1, k[short, cols], v[short, cols]
 def mine_of(b, nl, long_ref, short_ref):
     return long_ref.at[b] if b < nl else short_ref.at[b - nl]
-def attn_fwd_kernel(nl, ns, blocks, experts, cap, ll, sl, q, k, v, kl, vl, tab, lpos, spos,
-                    xl, xsh, gl, gsh, wo, params, lr, sr, mixed, mid, xs, gs, logits, lb, sb, n2, gb):
-    me = lax.axis_index("seq")
+def front_kernel(dims, nl, ns, experts, cap, pieces, table_part, gain_part, ll, sl, wk_in, wv_in, wq_in, wo_in, small_in, lpos, spos, xl, xsh, gl, gsh, lr, sr,
+                 wk_out, wv_out, wq_out, wo_out, params, tab, q, ks, vs, kl, vl, n1t, mixed, mid, xs, gs, logits, lb, sb,
+                 wall, sm, n1, n2, gb, zs, zr, hs, hr, cs, cr, kss, krs, osem):
+    X, C, Z, Y = dims
+    blocks = X * C
+    f32, bf = jnp.float32, jnp.bfloat16
+    s, x, c, xdev, cdev = seq_places(C)
+    g = lax.axis_index("dp")
+    z, y = g // Y, lax.rem(g, Y)
+    def zdev(k): return (s, lax.rem(z + k, Z) * Y + y)
+    ydev = (s, z * Y + (1 - y))
+    tokens, width = q.shape
+    half = nl * 128
+    wide = 256
+    nb = width // wide
+    greet([zdev(k) for k in range(1, Z)] + [ydev, xdev, cdev])
+    ins = (wk_in, wv_in, wq_in, wo_in)
+    def part(i, *lead):
+        m, r0, nr, route = pieces[i]
+        if m == 4:
+            return sm.at[lead + (slice(None),) * (4 - len(lead))]
+        return wall.at[(m,) + lead + (slice(None),) * (4 - len(lead)) + (pl.ds(r0, nr),)]
+    zc, h, cc = {}, {}, {}
+    for i, (m, r0, nr, route) in enumerate(pieces):
+        src = small_in if m == 4 else ins[m].at[pl.ds(r0, nr)]
+        zc[i] = [remote(src, part(i, x, c, z, y), zs.at[i, k], zr.at[i, k], zdev(k)) for k in range(1, Z)]
+    for m in range(4):
+        wall[m, x, c, z, y] = ins[m][...]
+    sm[x, c, z, y] = small_in[...]
+    def gather_stage(i, stage):
+        route = pieces[i][3]
+        if stage == 0:
+            for k in range(1, Z): zc[i][k - 1].wait_recv()
+            mine = part(i, x, c, slice(None), y)
+            h[i, 0] = remote(mine, mine, hs.at[i, 0], hr.at[i, 0], xdev if route == 0 else ydev)
+            cc[i, 0] = remote(mine, mine, cs.at[i, 0], cr.at[i, 0], cdev)
+        elif stage == 1:
+            h[i, 0].wait_recv()
+            if route == 0:
+                both, got = part(i, slice(None), c, slice(None), y), part(i, 1 - x, c, slice(None), y)
+            else:
+                both, got = part(i, x, c), part(i, x, c, slice(None), 1 - y)
+            h[i, 1] = remote(both, both, hs.at[i, 1], hr.at[i, 1], ydev if route == 0 else xdev)
+            cc[i, 1] = remote(got, got, cs.at[i, 1], cr.at[i, 1], cdev)
+        else:
+            h[i, 1].wait_recv()
+            got = part(i, slice(None), c, slice(None), 1 - y) if route == 0 else part(i, 1 - x, c)
+            cc[i, 2] = remote(got, got, cs.at[i, 2], cr.at[i, 2], cdev)
+    np_ = len(pieces)
+    steps = [(t - st, st) for t in range(np_ + 2) for st in range(3) if 0 <= t - st < np_]
+    done = [0]
+    def gather_until(m):
+        last = max(i for i, p in enumerate(pieces) if p[0] == m)
+        while True:
+            i, st = steps[done[0]]
+            gather_stage(i, st)
+            done[0] += 1
+            if (i, st) == (last, 2): break
+        for i, p in enumerate(pieces):
+            if p[0] == m:
+                for k in range(3): cc[i, k].wait_recv()
+    kept_copies = []
+    def keep(m, out):
+        cp = pltpu.make_async_copy(wall.at[m], out, osem.at[m]); cp.start(); kept_copies.append(cp)
+    def w_of(m):
+        return wall[m].reshape(width, width)
     for b in range(nl):
-        own = column_of(lpos[b:b + 1, pl.ds(pl.multiple_of(me * 128, 128), 128)])
-        for c in range(blocks):
-            fill_buckets(lb.at[b, c], own, lpos[b:b + 1, c * 128:(c + 1) * 128], ll[b], c * 128)
+        own = column_of(lpos[b:b + 1, pl.ds(pl.multiple_of(s * 128, 128), 128)])
+        for k in range(blocks):
+            fill_buckets(lb.at[b, k], own, lpos[b:b + 1, k * 128:(k + 1) * 128], ll[b], k * 128)
     for b in range(ns):
         fill_buckets(sb.at[b, 0], column_of(spos[b:b + 1, :]), spos[b:b + 1, :], sl[b], 0)
+    gather_until(4)
+    flat = sm[...].astype(f32).reshape(X * C * Z * Y, sm.shape[4], 128)
+    per = 128 // gain_part
+    def shifted(rows, n):
+        return rows if n == 0 else pltpu.roll(rows, n, 1)
+    chunks = []
+    for k in range(width // 128):
+        chunks.append(sum(shifted(flat[k * per + i], i * gain_part) for i in range(per)))
+    found = jnp.concatenate(chunks, axis=1)
+    params[...] = jnp.zeros_like(params)
+    params[0:found.shape[0], :] = found.astype(bf)
+    share = 32 // table_part
+    lane8 = lax.broadcasted_iota(jnp.int32, (1, 128), 1)
+    for hd in range(tab.shape[0]):
+        rows = sum(shifted(flat[hd * share + i], i * table_part) for i in range(share))
+        tab[hd] = jnp.where(lane8 < 32, rows[experts + 2:experts + 3, :], masked)
+    gain = params[experts:experts + 1, :].astype(f32)
+    for t in range(2):
+        m = rows_of(xl, xsh, t).astype(f32)
+        n1[pl.ds(t * half, half), :] = (m * rms_scale(m) * gain).astype(bf)
+        gb[pl.ds(t * half, half), :] = rows_of(gl, gsh, t)
+    wholes = (kl, vl)
+    far = (1 - x) * C + c
+    ka, kc, kf = {}, {}, {}
+    def project(m, t):
+        return jnp.dot(n1[pl.ds(t * half, half), :], w_of(m), preferred_element_type=f32).astype(bf)
+    for m in range(2):
+        gather_until(m)
+        wholes[m][s] = project(m, 0).reshape(nl, 128, width)
+        for b in range(nb):
+            n = m * nb + b
+            src = wholes[m].at[s, :, :, pl.ds(b * wide, wide)]
+            ka[n] = remote(src, src, kss.at[n, 0], krs.at[n, 0], xdev)
+            kc[n] = remote(src, src, kss.at[n, 1], krs.at[n, 1], cdev)
+        keep(m, (wk_out, wv_out)[m])
+    ks[...] = project(0, 1)
+    vs[...] = project(1, 1)
+    for t in range(2):
+        n1t[:, t * half:(t + 1) * half] = n1[pl.ds(t * half, half), :].T
+    gather_until(2)
+    for t in range(2):
+        q[pl.ds(t * half, half), :] = project(2, t)
+    keep(2, wq_out)
     first = lax.broadcasted_iota(jnp.int32, (128, 128), 1) < 64
-    @pl.loop(0, 8)
-    def _(hp):
-        cols = pl.ds(pl.multiple_of(hp * 128, 128), 128)
-        for b in range(nl + ns):
-            rows, n, kk, vv = item(b, nl, blocks, cols, k, v, kl, vl)
-            p = probs_of(stack_heads(q[rows, cols], first), kk, (tab[2 * hp], tab[2 * hp + 1]), mine_of(b, nl, lb, sb), n)
-            out = dot(p.astype(jnp.bfloat16), vv, 1, 0)
-            mixed[rows, cols] = jnp.where(first, out[:128], out[128:]).astype(jnp.bfloat16)
-    f32, bf = jnp.float32, jnp.bfloat16
-    tokens = q.shape[0]
+    for b0 in range(nb):
+        for n in (b0, nb + b0):
+            ka[n].wait_recv()
+            got = wholes[n // nb].at[far, :, :, pl.ds(b0 * wide, wide)]
+            kf[n] = remote(got, got, kss.at[n, 2], krs.at[n, 2], cdev)
+        for n in (b0, nb + b0):
+            kc[n].wait_recv(); kf[n].wait_recv()
+        @pl.loop(0, wide // 128)
+        def _(i):
+            hp = b0 * (wide // 128) + i
+            cols = pl.ds(pl.multiple_of(hp * 128, 128), 128)
+            for b in range(nl + ns):
+                rows, n, kk, vv = item(b, nl, blocks, cols, ks, vs, kl, vl)
+                p = probs_of(stack_heads(q[rows, cols], first), kk, (tab[2 * hp], tab[2 * hp + 1]), mine_of(b, nl, lb, sb), n)
+                out = dot(p.astype(bf), vv, 1, 0)
+                mixed[rows, cols] = jnp.where(first, out[:128], out[128:]).astype(bf)
+        if b0 == 0:
+            gather_until(3)
+            keep(3, wo_out)
     gain = params[experts + 1:experts + 2, :].astype(f32)
     for t in range(2):
         rows = pl.ds(t * 256, 256)
-        m = rows_of(xl, xsh, t).astype(f32) + jnp.dot(mixed[rows, :], wo[...], preferred_element_type=f32)
+        m = rows_of(xl, xsh, t).astype(f32) + jnp.dot(mixed[rows, :], w_of(3), preferred_element_type=f32)
         mid[rows, :] = m
         n2[rows, :] = (m * rms_scale(m) * gain).astype(bf)
-        gb[rows, :] = rows_of(gl, gsh, t)
     logits[...] = dot(n2[...], params[...], 1, 1)
     logit_t = dot(params[...], n2[...], 1, 1)[:experts]
     routes = [jnp.concatenate([row_of(ref[i, :, j:j + 1]) for ref in (lr, sr) for i in range(ref.shape[0])], axis=1) for j in range(2)]
@@ -188,6 +233,11 @@
         pick = pick.astype(bf)
         xs[i] = jnp.dot(pick, n2[...], preferred_element_type=f32).astype(bf)
         gs[i] = (jnp.dot(pick, gb[...], preferred_element_type=f32) * scale).astype(bf)
+    for cp in kept_copies: cp.wait()
+    for group in (h, cc, ka, kc, kf):
+        for cp in group.values(): cp.wait_send()
+    for i in zc:
+        for cp in zc[i]: cp.wait_send()
 def post_kernel(nl, ns, blocks, experts, cap, lpos, spos, eo, ri, mid, mixed, logits, lr, sr, gl, gsh, wo, params, eg,
                 lout, sout, midg, wog, small, mg, li, si, eg0, eg1, eg2, bg, n2, lg, fin, bk, sh, ev, sem):
     f32, bf = jnp.float32, jnp.bfloat16
@@ -274,15 +324,22 @@
     for b in range(ns):
         places(si.at[b, 0], column_of(spos[b:b + 1, :]), spos[b:b + 1, :])
     for cp in copies: cp.wait()
-def attention(nl, ns, blocks, experts, cap, arrays, tokens, width):
-    sm, vm = pl.BlockSpec(memory_space=pltpu.SMEM), pl.BlockSpec(memory_space=pltpu.VMEM)
-    S, bf, f32 = jax.ShapeDtypeStruct, jnp.bfloat16, jnp.float32
+def front(dims, nl, ns, experts, cap, pieces, table_part, gain_part, arrays, tokens, width, heads, cid):
+    X, C, Z, Y = dims
+    sm, vm, hbm = pl.BlockSpec(memory_space=pltpu.SMEM), pl.BlockSpec(memory_space=pltpu.VMEM), pl.BlockSpec(memory_space=pl.ANY)
+    S, V, sem, bf, f32 = jax.ShapeDtypeStruct, pltpu.VMEM, pltpu.SemaphoreType.DMA, jnp.bfloat16, jnp.float32
+    rows_part, small_shape = arrays[2].shape[0], arrays[6].shape
+    whole = dims + (rows_part, width)
     slots = S((experts, cap, width), bf)
-    outs = [S((tokens, width), bf), S((tokens, width), f32), slots, slots, S((tokens, 128), f32),
-            S((nl, blocks, 128, 128), jnp.int32), S((ns, 1, 128, 128), jnp.int32)]
-    return pl.pallas_call(functools.partial(attn_fwd_kernel, nl, ns, blocks, experts, cap), out_shape=outs,
-        in_specs=[sm, sm] + [vm] * (len(arrays) - 2), out_specs=[vm] * len(outs), scratch_shapes=[pltpu.VMEM((tokens, width), bf)] * 2,
-        compiler_params=pltpu.CompilerParams(vmem_limit_bytes=60 * 2**20))(*arrays)
+    rows, short, long = S((tokens, width), bf), S((ns * 128, width), bf), S((X * C, nl, 128, width), bf)
+    outs = [S(whole, bf)] * 4 + [S((128, width), bf), S((heads, 1, 128), f32), rows, short, short, long, long, S((width, tokens), bf), rows,
+            S((tokens, width), f32), slots, slots, S((tokens, 128), f32), S((nl, X * C, 128, 128), jnp.int32), S((ns, 1, 128, 128), jnp.int32)]
+    n, kvn = len(pieces), 2 * (width // 256)
+    scr = [V((4,) + whole, bf), V(dims + small_shape, bf)] + [V((tokens, width), bf)] * 3
+    scr += [sem((n, Z)), sem((n, Z)), sem((n, 2)), sem((n, 2)), sem((n, 3)), sem((n, 3)), sem((kvn, 3)), sem((kvn, 3)), sem((4,))]
+    return pl.pallas_call(functools.partial(front_kernel, dims, nl, ns, experts, cap, pieces, table_part, gain_part), out_shape=outs,
+        in_specs=[sm, sm] + [vm] * (len(arrays) - 2), out_specs=[hbm] * 4 + [vm] * (len(outs) - 4), scratch_shapes=scr,
+        compiler_params=pltpu.CompilerParams(collective_id=cid, has_side_effects=True, vmem_limit_bytes=60 * 2**20))(*arrays)
 def small_rows(experts):
     return -(-(experts + 4) // 8) * 8
 def post(nl, ns, blocks, experts, cap, whole, arrays, tokens, width):
@@ -296,52 +353,6 @@
         in_specs=[vm] * (len(arrays) - 1) + [hbm], out_specs=[vm] * (len(outs) - 3) + [hbm] * 3,
         scratch_shapes=[V((tokens, width), bf)] * 2 + [V((tokens, 128), bf)] + [V((256, width), f32)] * 2 + [V((256, 128), f32), V(eg.shape, f32), pltpu.SemaphoreType.DMA((3,))],
         compiler_params=pltpu.CompilerParams(vmem_limit_bytes=60 * 2**20))(*arrays)
-def head_kernel(nl, ns, experts, lx, sx, params, wq, wk, wv, q, k, v, kl, vl, n1t, n1, lsem, ss, rs):
-    f32, bf = jnp.float32, jnp.bfloat16
-    s, x, c, xdev, cdev = seq_places(2)
-    far = (1 - x) * 2 + c
-    greet([xdev, cdev])
-    half = nl * 128
-    gain = params[experts:experts + 1, :].astype(f32)
-    def norm(t):
-        m = rows_of(lx, sx, t).astype(f32)
-        n1[pl.ds(t * half, half), :] = (m * rms_scale(m) * gain).astype(bf)
-    def project(out, w, r0, nr):
-        out[pl.ds(r0, nr), :] = jnp.dot(n1[pl.ds(r0, nr), :], w[...], preferred_element_type=f32).astype(bf)
-    norm(0)
-    local, a, b, f = [], [], [], []
-    for m, (out, w, whole) in enumerate(((k, wk, kl), (v, wv, vl))):
-        project(out, w, 0, half)
-        for i in range(nl):
-            n = m * nl + i
-            src = out.at[pl.ds(i * 128, 128)]
-            a.append(remote(src, whole.at[s, i], ss.at[n, 0], rs.at[n, 0], xdev))
-            b.append(remote(src, whole.at[s, i], ss.at[n, 1], rs.at[n, 1], cdev))
-            cp = pltpu.make_async_copy(src, whole.at[s, i], lsem.at[n]); cp.start(); local.append(cp)
-    norm(1)
-    project(k, wk, half, ns * 128)
-    project(v, wv, half, ns * 128)
-    project(q, wq, 0, half)
-    project(q, wq, half, ns * 128)
-    for t in range(2):
-        n1t[:, t * half:(t + 1) * half] = n1[pl.ds(t * half, half), :].T
-    for m, whole in enumerate((kl, vl)):
-        for i in range(nl):
-            n = m * nl + i
-            a[n].wait_recv()
-            f.append(remote(whole.at[far, i], whole.at[far, i], ss.at[n, 2], rs.at[n, 2], cdev))
-    for n in range(2 * nl):
-        local[n].wait(); a[n].wait_send(); b[n].wait(); f[n].wait()
-def head(nl, ns, seq, experts, arrays, cid):
-    tokens, width = (nl + ns) * 128, arrays[3].shape[1]
-    S, sem, bf = jax.ShapeDtypeStruct, pltpu.SemaphoreType.DMA, jnp.bfloat16
-    vm = pl.BlockSpec(memory_space=pltpu.VMEM)
-    rows, long = S((tokens, width), bf), S((seq, nl, 128, width), bf)
-    return pl.pallas_call(functools.partial(head_kernel, nl, ns, experts), out_shape=[rows] * 3 + [long] * 2 + [S((width, tokens), bf)],
-        in_specs=[vm] * 6, out_specs=[vm] * 6,
-        scratch_shapes=[pltpu.VMEM((tokens, width), bf), sem((2 * nl,)), sem((2 * nl, 3)), sem((2 * nl, 3))],
-        compiler_params=pltpu.CompilerParams(collective_id=cid, has_side_effects=True, vmem_limit_bytes=48 * 2**20))(*arrays)
-
 def back_kernel(dims, nl, ns, experts, pieces, q, k, v, kl, vl, tab, lb, sb, li, si, mg, wog, n1t, lx, sx, params, wq, wk, wv, midg, small_in,
                 lgrad, sgrad, og, qg, kg, vg, small, *refs):
     X, C, Z, Y = dims
@@ -544,11 +555,12 @@
 def gelu_parts(v):
     c, a = 0.7978845608, 0.044715
     v2 = v * v
-    t = jnp.tanh(c * v * (1.0 + a * v2))
-    half = 0.5 * (1.0 + t)
-    return v * half, half + 0.5 * v * (1.0 - t * t) * (c * (1.0 + 3.0 * a * v2))
+    h = 0.5 + 0.5 * jnp.tanh(v * (c + (c * a) * v2))
+    act = v * h
+    return act, h + act * (1.0 - h) * (2.0 * c + (6.0 * c * a) * v2)
 RING, LAG = 6, 4
-def expert_kernel(cap, per, order, todo, wcut, tile, whole_down, xs, gs, wgi, wui, wdi, eo_out, ri_out, grads, eo_h, ri_h,
+SEND_AT, JOIN_AT = 2, 3
+def expert_kernel(cap, per, order, todo, wcut, tile, xs, gs, wgi, wui, wdi, eo_out, ri_out, grads, eo_h, ri_h,
                   wall, xr, gr, hall, lall, eo, ri, cb, ab, xb, ob,
                   lsem, xss, xrs, gss, grs, ess, ers, rss, rrs, wss, wrs, wls, css, crs, ass, ars, osem, free):
     dp = lax.axis_size("dp")
@@ -558,45 +570,37 @@
     def peer(k): return (s, g ^ k)
     greet([xdev, cdev] + [peer(k) for k in range(1, dp)])
     rows_w, ff = wgi.shape; width = xs.shape[2]
-    piece = rows_w // wcut
-    wx, wc, wl = [], [], []
-    shared = ((wgi, 1), (wui, 2)) if whole_down else ((wgi, 1), (wui, 2), (wdi, 0))
-    parts = [(src, m, h * piece) for h in range(wcut) for src, m in shared]
-    for n, (src, m, r0) in enumerate(parts):
-        a = src.at[pl.ds(r0, piece)]
-        b = wall.at[m, x, c, pl.ds(r0, piece)]
+    wx, wc, wl, wf = [], [], [], []
+    shared = ((wgi, 1), (wui, 2), (wdi, 0))
+    parts = [(src, m, f0, nf) for f0, nf in wcut for src, m in shared]
+    for n, (src, m, f0, nf) in enumerate(parts):
+        a = src.at[:, pl.ds(f0, nf)]
+        b = wall.at[m, x, c, :, pl.ds(f0, nf)]
         wx.append(remote(a, b, wss.at[n, 0], wrs.at[n, 0], xdev))
         wc.append(remote(a, b, wss.at[n, 1], wrs.at[n, 1], cdev))
         cp = pltpu.make_async_copy(a, b, wls.at[n]); cp.start(); wl.append(cp)
-    if whole_down:
-        cp = pltpu.make_async_copy(wdi, wall.at[0], wls.at[len(parts)]); cp.start(); wl.append(cp)
     sx, sg = {}, {}
-    for k in [k for p in order for k in range(p * per, (p + 1) * per)]:
-        at = pl.ds(k * cap, cap)
-        if k == 0:
-            sx[0] = pltpu.make_async_copy(xs.at[g], xr.at[at], lsem.at[0]); sx[0].start()
-            sg[0] = pltpu.make_async_copy(gs.at[g], gr.at[at], lsem.at[1]); sg[0].start()
-        else:
-            sx[k] = remote(xs.at[g ^ k], xr.at[at], xss.at[k], xrs.at[k], peer(k))
-            sg[k] = remote(gs.at[g ^ k], gr.at[at], gss.at[k], grs.at[k], peer(k))
-    wf = []
-    for n, (src, m, r0) in enumerate(parts):
-        wx[n].wait_recv()
-        b = wall.at[m, 1 - x, c, pl.ds(r0, piece)]
-        wf.append(remote(b, b, wss.at[n, 2], wrs.at[n, 2], cdev))
-    for cp in wl: cp.wait()
-    for n in range(len(parts)):
-        wc[n].wait_recv(); wf[n].wait_recv()
+    def dispatch(p):
+        for k in range(p * per, (p + 1) * per):
+            at = pl.ds(k * cap, cap)
+            if k == 0:
+                sx[0] = pltpu.make_async_copy(xs.at[g], xr.at[at], lsem.at[0]); sx[0].start()
+                sg[0] = pltpu.make_async_copy(gs.at[g], gr.at[at], lsem.at[1]); sg[0].start()
+            else:
+                sx[k] = remote(xs.at[g ^ k], xr.at[at], xss.at[k], xrs.at[k], peer(k))
+                sg[k] = remote(gs.at[g ^ k], gr.at[at], gss.at[k], grs.at[k], peer(k))
+    for p in order[:-1]: dispatch(p)
     ntile = ff // tile
     re, rr = {}, {}
     wide = 4 * rows_w
-    for p in todo:
-        ks = list(range(p * per, (p + 1) * per))
-        for k in ks:
+    def sources(p): return list(range(p * per, (p + 1) * per))
+    def arrive(p):
+        for k in sources(p):
             if k == 0: sx[0].wait(); sg[0].wait()
             else: sx[k].wait_recv(); sg[k].wait_recv()
+    def inner(p, t0, nt):
         rows = pl.ds(p * per * cap, per * cap)
-        @pl.loop(0, ntile)
+        @pl.loop(t0, t0 + nt)
         def _(t):
             cols = pl.ds(pl.multiple_of(t * tile, 128), tile)
             w = lambda m: wall[m, :, :, :, cols].reshape(wide, tile)
@@ -607,6 +611,8 @@
             hall[0, rows, cols] = (act * up).astype(bf)
             hall[1, rows, cols] = (hg * up * der).astype(bf)
             hall[2, rows, cols] = (hg * act).astype(bf)
+    def outer(p):
+        rows = pl.ds(p * per * cap, per * cap)
         @pl.loop(0, 4)
         def _(t):
             part = pl.ds(pl.multiple_of(t * rows_w, 128), rows_w)
@@ -616,7 +622,7 @@
         keep = [pltpu.make_async_copy(eo, eo_h.at[rows], lsem.at[4]), pltpu.make_async_copy(ri, ri_h.at[rows], lsem.at[5])]
         for cp in keep: cp.start()
         for cp in keep: cp.wait()
-        for k in ks:
+        for k in sources(p):
             at = pl.ds(k * cap, cap)
             if k == 0:
                 re[0] = pltpu.make_async_copy(eo_h.at[at], eo_out.at[g], lsem.at[2]); re[0].start()
@@ -624,6 +630,30 @@
             else:
                 re[k] = remote(eo_h.at[at], eo_out.at[g], ess.at[k], ers.at[k], peer(k))
                 rr[k] = remote(ri_h.at[at], ri_out.at[g], rss.at[k], rrs.at[k], peer(k))
+    early = list(todo[:-2])
+    last = todo[-1]
+    for i, (f0, nf) in enumerate(wcut):
+        mine = range(3 * i, 3 * i + 3)
+        for n in mine:
+            wx[n].wait_recv()
+            src, m, f0, nf = parts[n]
+            b = wall.at[m, 1 - x, c, :, pl.ds(f0, nf)]
+            wf.append(remote(b, b, wss.at[n, 2], wrs.at[n, 2], cdev))
+        if i == SEND_AT: dispatch(last)
+        if i == 0:
+            for p in early: arrive(p)
+        for n in mine:
+            wl[n].wait(); wc[n].wait_recv(); wf[n].wait_recv()
+        for p in early: inner(p, f0 // tile, nf // tile)
+        if i == JOIN_AT:
+            p = todo[-2]
+            arrive(p)
+            inner(p, 0, (f0 + nf) // tile)
+            early.append(p)
+    for p in early[::-1]: outer(p)
+    arrive(last)
+    inner(last, 0, ntile)
+    outer(last)
     for n in range(len(parts)):
         wx[n].wait_send(); wc[n].wait_send(); wf[n].wait_send()
     total = dp * cap
@@ -692,28 +722,27 @@
 def expert_all(xs, gs, wg, wu, wd, seq, cid):
     dp, cap, width = xs.shape
     rows_w, ff = wg.shape; total = dp * cap
-    whole_down = wd.shape[0] != rows_w
-    if whole_down: wd = wd.reshape(seq // 2, 2, rows_w, ff)
     group = 320
     per = group // cap
     ng = dp // per
-    order = [p for p in range(ng // 2, ng)] + [p for p in range(ng // 2 - 1, -1, -1)]
+    order = [ng - 2] + [p for p in range(ng - 3, -1, -1)] + [ng - 1]
     todo = list(range(ng))
     sem = pltpu.SemaphoreType.DMA
     bf = jnp.bfloat16
     any_ = pl.BlockSpec(memory_space=pl.ANY)
     V = pltpu.VMEM
     tile = 256
-    wcut = 2
+    wcut = tuple((f0, min(512, ff - f0)) for f0 in range(0, ff, 512))
+    nw = 3 * len(wcut)
     back = jax.ShapeDtypeStruct((dp, cap, width), bf)
     flat = jax.ShapeDtypeStruct((total, width), bf)
-    return pl.pallas_call(functools.partial(expert_kernel, cap, per, order, todo, wcut, tile, whole_down),
+    return pl.pallas_call(functools.partial(expert_kernel, cap, per, order, todo, wcut, tile),
         out_shape=[back, back, jax.ShapeDtypeStruct((3, rows_w, ff), jnp.float32), flat, flat],
         in_specs=[any_] * 5, out_specs=[any_] * 5,
         scratch_shapes=[V((3, seq // 2, 2, rows_w, ff), bf), V((total, width), bf), V((total, width), bf), V((3, total, ff), bf),
         V((2, width, total), bf), V((group, width), bf), V((group, width), bf),
         V((RING, seq // 2, rows_w, tile), bf), V((RING, rows_w, tile), bf), V((RING, rows_w, tile), bf), V((2, rows_w, tile), jnp.float32)]
-        + [sem((6,))] + [sem((dp,))] * 8 + [sem((3 * wcut, 3))] * 2 + [sem((3 * wcut + 1,))] + [sem((RING,))] * 4 + [sem((2,)), pltpu.SemaphoreType.REGULAR((2,))],
+        + [sem((6,))] + [sem((dp,))] * 8 + [sem((nw, 3))] * 2 + [sem((nw,))] + [sem((RING,))] * 4 + [sem((2,)), pltpu.SemaphoreType.REGULAR((2,))],
         compiler_params=pltpu.CompilerParams(collective_id=cid, has_side_effects=True, vmem_limit_bytes=63 * 2**20))(xs, gs, wg, wu, wd)[:3]
 
 
@@ -760,48 +789,56 @@
     cuts = 2 if rows_part % 32 == 0 else 1
     cut = rows_part // cuts
     pieces = tuple((m, h * cut, cut, (m + h) % 2) for m in range(4) for h in range(cuts))
-    gathered = gather_all(
-        (query_weight, key_weight, value_weight, output_weight, small),
-        pieces[: 3 * cuts] + ((4, 0, small.shape[0], 0),) + pieces[3 * cuts :],
+    pieces = ((4, 0, small.shape[0], 0),) + pieces
+    sizes = (long_items, short_items, seq_size, experts, capacity)
+    places = (long_positions, short_positions)
+    routes = (long_routes, short_routes)
+    (
+        key_all,
+        value_all,
+        query_all,
+        output_all,
+        params,
+        table,
+        queries,
+        keys,
+        values,
+        long_keys,
+        long_values,
+        normed_t,
+        mixed,
+        middle,
+        outgoing,
+        out_slots,
+        logits,
+        long_buckets,
+        short_buckets,
+    ) = front(
         dims,
-        0,
-    )
-    query_all, key_all, value_all, output_all = (
-        block.reshape(devices * rows_part, model_width) for block in gathered[:4]
-    )
-    small_all = gathered[4].reshape(devices, small.shape[0], 128)
-    params = small_all[:, : experts + 2, :gain_part].transpose(1, 0, 2)
-    params = jnp.pad(params.reshape(experts + 2, model_width), ((0, 126 - experts), (0, 0)))
-    table = small_all[:, experts + 2, :table_part].reshape(HEADS, 1, BUCKETS).astype(jnp.float32)
-    table = jnp.pad(table, ((0, 0), (0, 0), (0, 128 - BUCKETS)), constant_values=masked)
-    queries, keys, values, long_keys, long_values, normed_t = head(
         long_items,
         short_items,
-        seq_size,
         experts,
-        (long_tokens, short_tokens, params, query_all, key_all, value_all),
-        1,
-    )
-    sizes = (long_items, short_items, seq_size, experts, capacity)
-    heads_args = (queries, keys, values, long_keys, long_values, table)
-    places = (long_positions, short_positions)
-    grads = (long_grad_out, short_grad_out, output_all, params)
-    routes = (long_routes, short_routes)
-    mixed, middle, outgoing, out_slots, logits, long_buckets, short_buckets = attention(
-        *sizes,
-        (long_lengths, short_lengths)
-        + heads_args
+        capacity,
+        pieces,
+        table_part,
+        gain_part,
+        (long_lengths, short_lengths, key_weight, value_weight, query_weight, output_weight, small)
         + places
-        + (long_tokens, short_tokens)
-        + grads
+        + (long_tokens, short_tokens, long_grad_out, short_grad_out)
         + routes,
         tokens,
         model_width,
+        HEADS,
+        0,
     )
-    later_down, unused_keys = lax.optimization_barrier((down_weight[0], long_keys))
-    down_full = lax.all_gather(later_down, "seq", axis=0, tiled=True)
+    key_all, value_all, query_all, output_all = (
+        block.reshape(devices * rows_part, model_width)
+        for block in (key_all, value_all, query_all, output_all)
+    )
+    heads_args = (queries, keys, values, long_keys, long_values, table)
+    grads = (long_grad_out, short_grad_out, output_all, params)
     back_rows, back_grads, expert_grads = expert_all(
-        outgoing, out_slots, gate_weight[0], up_weight[0], down_full, seq_size, 4
+        outgoing, out_slots, gate_weight[0], up_weight[0], down_weight[0], seq_size, 4
     )
     (
         long_out,

time: 532 us -> 525 us (0.987)
  Pallas kernels: 487 us -> 505 us
  between operations: 14.5 us -> 1.21 us
  local copies, waits for them, and re-layouts: 21 us -> 13.6 us
  waiting for transfers between devices: 5.73 us -> 0 us
    pallas_call x1, Pallas kernels: 104 us -> 123 us  [back(): pl.pallas_call(functools.partial(back_kernel, dims, nl, ns, experts, piec...]
    pallas_call x3 -> x1, Pallas kernels: 128 us -> 119 us  [front(): pl.pallas_call(functools.partial(front_kernel, dims, nl, ns, experts, cap...]
    pallas_call x1, Pallas kernels: 232 us -> 240 us  [expert_all(): pl.pallas_call(functools.partial(expert_kernel, cap, per, order, todo, wc...]
    all_gather x1 -> x0, waiting for transfers between devices: 5.71 us -> none  [on_device(): down_full = lax.all_gather(later_down, 'seq', axis=0, tiled=True)]
    unnamed x37 -> x18, local copies, waits for them, and re-layouts: 14.6 us -> 8.93 us
  transfers between devices with their start and end apart: 1 -> 0, of which waited for: 1 -> 0; matrix products, arithmetic and copies ran while one was open for 1% -> 0% of each run, Pallas kernels for 7% -> 0%
where the time goes in v7:
time: 525 us; the launch traced here: 521 us
  Pallas kernels  505 us (96%)
  local copies, waits for them, and re-layouts  13.6 us (3%)
    pallas_call x1, Pallas kernels, expert_all(): pl.pallas_call(functools.partial(expert_kernel, cap, per, order, todo, wc...  240 us
    pallas_call x1, Pallas kernels, back(): pl.pallas_call(functools.partial(back_kernel, dims, nl, ns, experts, piec...  123 us
    pallas_call x1, Pallas kernels, front(): pl.pallas_call(functools.partial(front_kernel, dims, nl, ns, experts, cap...  119 us
    pallas_call x1, Pallas kernels, post(): pl.pallas_call(functools.partial(post_kernel, nl, ns, blocks, experts, ca...  23.4 us

profile of v7, /device:TPU:0, one launch (start us, length us, event | category | flops | bytes accessed | tf_op | source)
XLA Modules:
  0.0 521.0 jit_solution(14430019014993648279)
XLA Ops:
  0.6 1.5 copy.36.lr
  2.1 1.5 copy.37.sr
  3.6 0.7 fusion.9
  4.3 0.6 pad.14.small_in
  4.9 119.2 %shard_map.316 = (bf16[2,2,4,2,32,1024]{5,4,3,2,1,0:T(8,128)(2,1)}, bf16[2,2,4,2,32,1024]{5,4,3,2,1,0:T(8,128)(2,1)}, bf16[2,2,4,2,32,1024]{5,4,3,2,1,0:T(8,128)...) custom-call(s32[2]{0:T(128)} %ll.1, s32[2]{0:T(128)} %sl.1, ...), custom_call_target="tpu_custom_call" | custom-call | tf_op jit(solution)/shard_map/pallas_call | solution.py:340
  124.1 240.4 %shard_map.317 = (bf16[8,160,1024]{2,1,0:T(8,128)(2,1)}, bf16[8,160,1024]{2,1,0:T(8,128)(2,1)}, f32[3,256,2816]{2,1,0:T(8,128)}, bf16[1280,1024]{1,0:T(8,128)(2,1)}, bf16[1280,1024]{1,0:T(8,128)(2,1)}) custom-call(bf16[8,160,1024]{2,1,0:T(8,128)(2,1)} %get-tuple-element.55.xs, bf16[8,160,1024]{2,1,0:T(8,128)(2,1)} %get-tuple-element.56.gs, ...), custom_call_target="tpu_custom_call" | custom-call | tf_op jit(solution)/shard_map/pallas_call | solution.py:739
  364.5 23.4 %shard_map.318 = (bf16[2,128,1024]{2,1,0:T(8,128)(2,1)}, bf16[2,128,1024]{2,1,0:T(8,128)(2,1)}, f32[512,1024]{1,0:T(8,128)}, bf16[2,2,4,2,32,1024]{5,4,3,2,1,0:T...) custom-call(s32[2,512]{1,0:T(2,128)} %lpos.3, ...), custom_call_target="tpu_custom_call" | custom-call | tf_op jit(solution)/shard_map/pallas_call | solution.py:352
  387.9 122.5 %shard_map.319 = (f32[2,128,1024]{2,1,0:T(8,128)}, f32[2,128,1024]{2,1,0:T(8,128)}, f32[32,1024]{1,0:T(8,128)}, f32[32,1024]{1,0:T(8,128)}, f32[32,1024]{1,0:T(8...) custom-call(bf16[512,1024]{1,0:T(8,128)(2,1)} %get-tuple-element.67.q, bf16[256,1024]{1,0:T(8,128)(2,1)} %get-tuple-element.68.k, ...), custom_call_target="tpu_custom_call" | custom-call | tf_op jit(solution)/shard_map/pallas_call | solution.py:551
  510.4 0.0 copy-start
  510.5 1.4 dynamic-slice_bitcast_fusion.1
  511.9 1.4 dynamic-slice_bitcast_fusion
  513.2 1.3 dynamic-slice_bitcast_fusion.2
  514.6 0.0 copy-start.4
  514.6 0.0 copy-start.3
  514.6 0.0 copy-start.2
  514.6 0.0 copy-start.1
  514.6 2.4 copy.46
  516.9 0.0 copy-done
  516.9 1.0 copy.47
  517.9 0.0 copy-done.4
  517.9 0.7 copy.48
  518.6 0.0 copy-done.3
  518.6 0.7 copy.49
  519.2 0.0 copy-done.2
  519.2 0.7 copy.50
  519.9 0.0 copy-done.1
  519.9 0.7 copy.51
Async XLA Ops:
  510.4 6.5 %copy-start = (f32[2,128,1024]{2,1,0:T(8,128)S(1)}, f32[2,128,1024]{2,1,0:T(8,128)}, u32[]{:S(2)}) copy-start(f32[2,128,1024]{2,1,0:T(8,128)} %get-tuple-element.115) | copy-start | bytes 3145732
  514.6 3.4 copy-start.4
  514.6 4.0 copy-start.3
  514.6 4.7 copy-start.2
  514.6 5.3 %copy-start.1 = (f32[32,1024]{1,0:T(8,128)S(1)}, f32[32,1024]{1,0:T(8,128)}, u32[]{:S(2)}) copy-start(f32[32,1024]{1,0:T(8,128)} %get-tuple-element.119) | copy-start | bytes 393220

commit v8 on v7

--- a/solution.py
+++ b/solution.py
@@ -650,7 +650,7 @@
             arrive(p)
             inner(p, 0, (f0 + nf) // tile)
             early.append(p)
-    for p in early[::-1]: outer(p)
+    for p in early: outer(p)
     arrive(last)
     inner(last, 0, ntile)
     outer(last)
@@ -789,7 +789,7 @@
     cuts = 2 if rows_part % 32 == 0 else 1
     cut = rows_part // cuts
     pieces = tuple((m, h * cut, cut, (m + h) % 2) for m in range(4) for h in range(cuts))
-    pieces = ((4, 0, small.shape[0], 0),) + pieces
+    pieces = ((4, 0, small.shape[0], 0),) + tuple(p[:3] + (0,) for p in pieces)
     sizes = (long_items, short_items, seq_size, experts, capacity)
     places = (long_positions, short_positions)
     routes = (long_routes, short_routes)

time: 525 us -> 496 us (0.945)
  Pallas kernels: 505 us -> 476 us
    pallas_call x1, Pallas kernels: 123 us -> 98 us  [back(): pl.pallas_call(functools.partial(back_kernel, dims, nl, ns, experts, piec...]
where the time goes in v8:
time: 496 us; the launch traced here: 492 us
  Pallas kernels  476 us (96%)
  local copies, waits for them, and re-layouts  13.6 us (3%)
    pallas_call x1, Pallas kernels, expert_all(): pl.pallas_call(functools.partial(expert_kernel, cap, per, order, todo, wc...  240 us
    pallas_call x1, Pallas kernels, front(): pl.pallas_call(functools.partial(front_kernel, dims, nl, ns, experts, cap...  115 us
    pallas_call x1, Pallas kernels, back(): pl.pallas_call(functools.partial(back_kernel, dims, nl, ns, experts, piec...  98 us
    pallas_call x1, Pallas kernels, post(): pl.pallas_call(functools.partial(post_kernel, nl, ns, blocks, experts, ca...  23.4 us

profile of v8, /device:TPU:0, one launch (start us, length us, event | category | flops | bytes accessed | tf_op | source)
XLA Modules:
  0.0 491.8 jit_solution(6535277145812917110)
XLA Ops:
  0.6 1.5 copy.36.lr
  2.1 1.5 copy.37.sr
  3.6 0.7 fusion.9
  4.3 0.6 pad.14.small_in
  4.9 115.3 %shard_map.316 = (bf16[2,2,4,2,32,1024]{5,4,3,2,1,0:T(8,128)(2,1)}, bf16[2,2,4,2,32,1024]{5,4,3,2,1,0:T(8,128)(2,1)}, bf16[2,2,4,2,32,1024]{5,4,3,2,1,0:T(8,128)...) custom-call(s32[2]{0:T(128)} %ll.1, s32[2]{0:T(128)} %sl.1, ...), custom_call_target="tpu_custom_call" | custom-call | tf_op jit(solution)/shard_map/pallas_call | solution.py:340
  120.3 239.6 %shard_map.317 = (bf16[8,160,1024]{2,1,0:T(8,128)(2,1)}, bf16[8,160,1024]{2,1,0:T(8,128)(2,1)}, f32[3,256,2816]{2,1,0:T(8,128)}, bf16[1280,1024]{1,0:T(8,128)(2,1)}, bf16[1280,1024]{1,0:T(8,128)(2,1)}) custom-call(bf16[8,160,1024]{2,1,0:T(8,128)(2,1)} %get-tuple-element.55.xs, bf16[8,160,1024]{2,1,0:T(8,128)(2,1)} %get-tuple-element.56.gs, ...), custom_call_target="tpu_custom_call" | custom-call | tf_op jit(solution)/shard_map/pallas_call | solution.py:739
  359.9 23.4 %shard_map.318 = (bf16[2,128,1024]{2,1,0:T(8,128)(2,1)}, bf16[2,128,1024]{2,1,0:T(8,128)(2,1)}, f32[512,1024]{1,0:T(8,128)}, bf16[2,2,4,2,32,1024]{5,4,3,2,1,0:T...) custom-call(s32[2,512]{1,0:T(2,128)} %lpos.3, ...), custom_call_target="tpu_custom_call" | custom-call | tf_op jit(solution)/shard_map/pallas_call | solution.py:352
  383.3 98.0 %shard_map.319 = (f32[2,128,1024]{2,1,0:T(8,128)}, f32[2,128,1024]{2,1,0:T(8,128)}, f32[32,1024]{1,0:T(8,128)}, f32[32,1024]{1,0:T(8,128)}, f32[32,1024]{1,0:T(8...) custom-call(bf16[512,1024]{1,0:T(8,128)(2,1)} %get-tuple-element.67.q, bf16[256,1024]{1,0:T(8,128)(2,1)} %get-tuple-element.68.k, ...), custom_call_target="tpu_custom_call" | custom-call | tf_op jit(solution)/shard_map/pallas_call | solution.py:551
  481.3 0.0 copy-start
  481.3 1.4 dynamic-slice_bitcast_fusion.1
  482.7 1.4 dynamic-slice_bitcast_fusion
  484.1 1.3 dynamic-slice_bitcast_fusion.2
  485.4 0.0 copy-start.4
  485.4 0.0 copy-start.3
  485.4 0.0 copy-start.2
  485.4 0.0 copy-start.1
  485.4 2.4 copy.46
  487.8 0.0 copy-done
  487.8 1.0 copy.47
  488.8 0.0 copy-done.4
  488.8 0.7 copy.48
  489.4 0.0 copy-done.3
  489.4 0.7 copy.49
  490.1 0.0 copy-done.2
  490.1 0.7 copy.50
  490.7 0.0 copy-done.1
  490.7 0.7 copy.51
Async XLA Ops:
  481.3 6.5 %copy-start = (f32[2,128,1024]{2,1,0:T(8,128)S(1)}, f32[2,128,1024]{2,1,0:T(8,128)}, u32[]{:S(2)}) copy-start(f32[2,128,1024]{2,1,0:T(8,128)} %get-tuple-element.115) | copy-start | bytes 3145732
  485.4 3.4 copy-start.4
  485.4 4.0 copy-start.3
  485.4 4.7 copy-start.2
  485.4 5.3 %copy-start.1 = (f32[32,1024]{1,0:T(8,128)S(1)}, f32[32,1024]{1,0:T(8,128)}, u32[]{:S(2)}) copy-start(f32[32,1024]{1,0:T(8,128)} %get-tuple-element.119) | copy-start | bytes 393220

commit v9 on v8

--- a/solution.py
+++ b/solution.py
@@ -239,7 +239,7 @@
     for i in zc:
         for cp in zc[i]: cp.wait_send()
 def post_kernel(nl, ns, blocks, experts, cap, lpos, spos, eo, ri, mid, mixed, logits, lr, sr, gl, gsh, wo, params, eg,
-                lout, sout, midg, wog, small, mg, li, si, eg0, eg1, eg2, bg, n2, lg, fin, bk, sh, ev, sem):
+                lout, sout, midg, wog, small, mg, li, si, eg0, eg1, eg2, bg, n2, lg, ev, sem):
     f32, bf = jnp.float32, jnp.bfloat16
     tokens = mid.shape[0]
     fetch = [pltpu.make_async_copy(eg.at[m], ev.at[m], sem.at[m]) for m in range(3)]
@@ -265,25 +265,22 @@
         rows = pl.ds(t * 256, 256)
         g = rows_of(gl, gsh, t).astype(f32)
         m = mid[rows, :]
-        fin[...] = m
-        bk[...] = jnp.zeros_like(m)
-        sh[...] = jnp.zeros_like(sh)
-        s_iota = lax.broadcasted_iota(jnp.int32, (256, cap), 1)
-        slot_t, weight_t, lane_t = slot[at], jnp.where(kept[at], gate[at], 0.0), lane[:256]
-        @pl.loop(0, experts)
-        def _(i):
-            this = lane_t == i
-            mine = jnp.sum(jnp.where(this, slot_t, 0), axis=1, keepdims=True)
-            weight = jnp.sum(jnp.where(this, weight_t, 0.0), axis=1, keepdims=True)
-            pick = (s_iota == mine).astype(f32).astype(bf)
-            pair = jnp.dot(pick, eo[i], preferred_element_type=f32)
-            fin[...] += weight * pair
-            sh[...] = jnp.where(this, jnp.sum(rows_of(gl, gsh, t).astype(f32) * pair, axis=1, keepdims=True), sh[...])
-            bk[...] += jnp.dot(pick, ri[i], preferred_element_type=f32)
-        (lout, sout)[t][...] = fin[...].astype(bf).reshape(lout.shape)
-        share, back = sh[...], bk[...]
-        mean = jnp.sum(share * gate[at], axis=1, keepdims=True)
-        pg = member[at] * (share - mean) / both[at]
+        s_iota = lax.broadcasted_iota(jnp.int32, (256, experts * cap), 1)
+        fin, back, mean, shares = m, 0.0, 0.0, []
+        for j in range(2):
+            this = lane[at] == routes[at, j:j + 1]
+            place_j = jnp.sum(jnp.where(this, slot[at], 0), axis=1, keepdims=True)
+            gate_j = jnp.sum(jnp.where(this, gate[at], 0.0), axis=1, keepdims=True)
+            index = jnp.where(place_j >= 0, routes[at, j:j + 1] * cap + place_j, -1)
+            pick = (s_iota == index).astype(f32).astype(bf)
+            pair = jnp.dot(pick, eo[...], preferred_element_type=f32)
+            back += jnp.dot(pick, ri[...], preferred_element_type=f32)
+            fin += jnp.where(place_j >= 0, gate_j, 0.0) * pair
+            share_j = jnp.sum(g * pair, axis=1, keepdims=True)
+            mean += share_j * gate_j
+            shares.append(jnp.where(this, share_j, 0.0))
+        (lout, sout)[t][...] = fin.astype(bf).reshape(lout.shape)
+        pg = member[at] * (shares[0] + shares[1] - mean) / both[at]
         lgrad = (p[at] * (pg - jnp.sum(p[at] * pg, axis=1, keepdims=True))).astype(bf)
         lg[rows, :] = lgrad
         r2 = rms_scale(m)
@@ -351,16 +348,18 @@
     V = pltpu.VMEM
     return pl.pallas_call(functools.partial(post_kernel, nl, ns, blocks, experts, cap), out_shape=outs,
         in_specs=[vm] * (len(arrays) - 1) + [hbm], out_specs=[vm] * (len(outs) - 3) + [hbm] * 3,
-        scratch_shapes=[V((tokens, width), bf)] * 2 + [V((tokens, 128), bf)] + [V((256, width), f32)] * 2 + [V((256, 128), f32), V(eg.shape, f32), pltpu.SemaphoreType.DMA((3,))],
+        scratch_shapes=[V((tokens, width), bf)] * 2 + [V((tokens, 128), bf), V(eg.shape, f32), pltpu.SemaphoreType.DMA((3,))],
         compiler_params=pltpu.CompilerParams(vmem_limit_bytes=60 * 2**20))(*arrays)
-def back_kernel(dims, nl, ns, experts, pieces, q, k, v, kl, vl, tab, lb, sb, li, si, mg, wog, n1t, lx, sx, params, wq, wk, wv, midg, small_in,
+def back_kernel(dims, nl, ns, experts, pieces, q, k, v, kl, vl, tab, lb, sb, li, si, mg, wog, n1t, lx_in, sx_in, params, wq_in, wk_in, wv_in, midg_in, small_in,
                 lgrad, sgrad, og, qg, kg, vg, small, *refs):
     X, C, Z, Y = dims
     blocks = X * C
     f32, bf = jnp.float32, jnp.bfloat16
     np_ = len(pieces)
     bufs = refs[:4 * np_]
-    (gw, dq, ka, va, dkl, dvl, kcb, ka1, kb1, seg, sacc, sbuf, cs, cr, hs, hr, zs, zr, kss, krs, sss, srs) = refs[4 * np_:]
+    (gw, dq, ka, va, dkl, dvl, kcb, ka1, kb1, seg, sacc, sbuf, lx, sx, wq, wk, wv, midg, cs, cr, hs, hr, zs, zr, kss, krs, sss, srs, fs) = refs[4 * np_:]
+    late = [pltpu.make_async_copy(a, b, fs.at[i]) for i, (a, b) in enumerate(((lx_in, lx), (sx_in, sx), (wq_in, wq), (wk_in, wk), (wv_in, wv), (midg_in, midg)))]
+    for cp in late: cp.start()
     s = lax.axis_index("seq"); g = lax.axis_index("dp")
     x, c = s // C, lax.rem(s, C)
     z, y = g // Y, lax.rem(g, Y)
@@ -376,22 +375,24 @@
     def add(dst, a, b):
         dst[...] = (a.astype(f32) + b.astype(f32)).astype(dst.dtype)
     def send_core(i):
-        m, c0, nc = pieces[i]
+        m, c0, nc, route = pieces[i]
         first[i] = remote(sources[m].at[:, 1 - c, :, :, :, pl.ds(c0, nc)], bufs[4 * i], cs.at[i], cr.at[i], cdev)
     def stage(i, which):
-        m, c0, nc = pieces[i]
+        m, c0, nc, route = pieces[i]
         b0, b1, b2, b3 = bufs[4 * i:4 * i + 4]
         if which == 0:
             first[i].wait_recv()
             add(b0, sources[m][:, c, :, :, :, c0:c0 + nc], b0[...])
-            hh[i, 0] = remote(b0.at[:, :, 1 - y], b1, hs.at[i, 0], hr.at[i, 0], ydev)
+            src = b0.at[:, :, 1 - y] if route == 0 else b0.at[1 - x]
+            hh[i, 0] = remote(src, b1, hs.at[i, 0], hr.at[i, 0], ydev if route == 0 else xdev)
         elif which == 1:
             hh[i, 0].wait_recv()
-            add(b1, b0[:, :, y], b1[...])
-            hh[i, 1] = remote(b1.at[1 - x], b2, hs.at[i, 1], hr.at[i, 1], xdev)
+            add(b1, b0[:, :, y] if route == 0 else b0[x], b1[...])
+            src = b1.at[1 - x] if route == 0 else b1.at[:, 1 - y]
+            hh[i, 1] = remote(src, b2, hs.at[i, 1], hr.at[i, 1], xdev if route == 0 else ydev)
         elif which == 2:
             hh[i, 1].wait_recv()
-            add(b2, b1[x], b2[...])
+            add(b2, b1[x] if route == 0 else b1[:, y], b2[...])
             zz[i] = [remote(b2.at[lax.rem(z + k, Z)], b3.at[k - 1], zs.at[i, k], zr.at[i, k], zdev(k)) for k in range(1, Z)]
         else:
             tot = b2[z].astype(f32)
@@ -482,6 +483,7 @@
     kv_core(3); kv_chip(2); kv_end(1); weight_grad(1, dq, 3); stages(0, 0, 2, 3); stages(0, 2, 1); stages(1, 1, 1); stages(2, 0, 1)
     kv_chip(3); kv_end(2); stages(0, 1, 2, 3); stages(0, 3, 1); stages(1, 0, 2, 3); stages(1, 2, 1); stages(2, 1, 1); stages(3, 0, 0)
     kv_end(3); stages(0, 2, 2, 3); stages(1, 3, 1); stages(1, 1, 2, 3); stages(2, 2, 1); stages(2, 0, 2, 3); stages(3, 0, 1)
+    for cp in late: cp.wait()
     gain = params[experts:experts + 1, :].astype(f32)
     ag = jnp.zeros((1, q.shape[1]), f32)
     for t in range(2):
@@ -527,6 +529,7 @@
     small[...] = tot
     for cp in [sc, sx_, sy] + sz + list(kx.values()) + list(kf.values()) + list(first.values()) + list(hh.values()) + [w for v_ in zz.values() for w in v_]:
         cp.wait_send()
+LATE = (13, 14, 16, 17, 18, 19)
 def back(dims, nl, ns, experts, arrays, cid):
     X, C, Z, Y = dims
     q_, small_in = arrays[0], arrays[-1]
@@ -534,22 +537,23 @@
     heads = arrays[5].shape[0]
     nr = width // (X * C * Z * Y)
     wide = 256
-    pieces = tuple((0, h * 512, 512) for h in range(width // 512)) + tuple((m, b * wide, wide) for m in range(1, 4) for b in range(width // wide))
+    pieces = tuple((0, h * 512, 512, 1) for h in range(width // 512)) + tuple(
+        (m, b * wide, wide, 1 if m == 3 and b >= 2 else 0) for m in range(1, 4) for b in range(width // wide))
     n = len(pieces)
     S, sem, bf, f32 = jax.ShapeDtypeStruct, pltpu.SemaphoreType.DMA, jnp.bfloat16, jnp.float32
     V = pltpu.VMEM
-    scr = [V(lead + (nr, nc), bf) for m, c0, nc in pieces for lead in ((X, Z, Y), (X, Z), (Z,), (Z - 1,))]
+    scr = [V(lead + (nr, nc), bf) for m, c0, nc, route in pieces for lead in ((X, Z, Y), (Z, Y) if route else (X, Z), (Z,), (Z - 1,))]
     kvn = 2 * (width // wide)
     long = V((X * C, nl, 128, width), bf)
     rows = V((tokens, width), bf)
     scr += [V((3, X, C, Z, Y, nr, width), bf), rows, rows, rows, long, long,
             V((kvn, 2, nl, 128, wide), bf), V((kvn, nl, 128, wide), bf), V((kvn, nl, 128, wide), bf), V((heads, 1, 128), f32),
-            V((4,) + small_in.shape, f32), V((Z + 2,) + small_in.shape, f32),
-            sem((n,)), sem((n,)), sem((n, 2)), sem((n, 2)), sem((n, Z)), sem((n, Z)), sem((kvn, 3)), sem((kvn, 3)), sem((Z + 2,)), sem((Z + 2,))]
+            V((4,) + small_in.shape, f32), V((Z + 2,) + small_in.shape, f32)] + [V(arrays[i].shape, arrays[i].dtype) for i in LATE] + [
+            sem((n,)), sem((n,)), sem((n, 2)), sem((n, 2)), sem((n, Z)), sem((n, Z)), sem((kvn, 3)), sem((kvn, 3)), sem((Z + 2,)), sem((Z + 2,)), sem((len(LATE),))]
     vm = pl.BlockSpec(memory_space=pltpu.VMEM)
     outs = [S((nl, 128, width), f32), S((ns, 128, width), f32)] + [S((nr, width), f32)] * 4 + [S(small_in.shape, f32)]
     return pl.pallas_call(functools.partial(back_kernel, dims, nl, ns, experts, pieces), out_shape=outs,
-        in_specs=[vm] * len(arrays), out_specs=[vm] * len(outs), scratch_shapes=scr,
+        in_specs=[pl.BlockSpec(memory_space=pl.ANY) if i in LATE else vm for i in range(len(arrays))], out_specs=[vm] * len(outs), scratch_shapes=scr,
         compiler_params=pltpu.CompilerParams(collective_id=cid, has_side_effects=True, vmem_limit_bytes=63 * 2**20))(*arrays)
 
 def gelu_parts(v):
@@ -855,7 +859,9 @@
     ) = post(
         *sizes,
         dims + (rows_part, model_width),
-        places + (back_rows, back_grads, middle, mixed, logits) + routes + grads + (expert_grads,),
+        places
+        + tuple(block.reshape(-1, model_width) for block in (back_rows, back_grads))
+        + (middle, mixed, logits) + routes + grads + (expert_grads,),
         tokens,
         model_width,
     )

time: 496 us -> 489 us (0.986)
  Pallas kernels: 476 us -> 469 us
where the time goes in v9:
time: 489 us; the launch traced here: 485 us
  Pallas kernels  469 us (96%)
  local copies, waits for them, and re-layouts  13.6 us (3%)
    pallas_call x1, Pallas kernels, expert_all(): pl.pallas_call(functools.partial(expert_kernel, cap, per, order, todo, wc...  240 us
    pallas_call x1, Pallas kernels, front(): pl.pallas_call(functools.partial(front_kernel, dims, nl, ns, experts, cap...  115 us
    pallas_call x1, Pallas kernels, back(): pl.pallas_call(functools.partial(back_kernel, dims, nl, ns, experts, piec...  95 us
    pallas_call x1, Pallas kernels, post(): pl.pallas_call(functools.partial(post_kernel, nl, ns, blocks, experts, ca...  19.6 us

profile of v9, /device:TPU:0, one launch (start us, length us, event | category | flops | bytes accessed | tf_op | source)
XLA Modules:
  0.0 484.8 jit_solution(17589448530366562094)
XLA Ops:
  0.6 1.5 copy.36.lr
  2.1 1.5 copy.37.sr
  3.6 0.7 fusion.9
  4.3 0.6 pad.14.small_in
  4.9 115.3 %shard_map.316 = (bf16[2,2,4,2,32,1024]{5,4,3,2,1,0:T(8,128)(2,1)}, bf16[2,2,4,2,32,1024]{5,4,3,2,1,0:T(8,128)(2,1)}, bf16[2,2,4,2,32,1024]{5,4,3,2,1,0:T(8,128)...) custom-call(s32[2]{0:T(128)} %ll.1, s32[2]{0:T(128)} %sl.1, ...), custom_call_target="tpu_custom_call" | custom-call | tf_op jit(solution)/shard_map/pallas_call | solution.py:337
  120.2 239.6 %shard_map.317 = (bf16[8,160,1024]{2,1,0:T(8,128)(2,1)}, bf16[8,160,1024]{2,1,0:T(8,128)(2,1)}, f32[3,256,2816]{2,1,0:T(8,128)}, bf16[1280,1024]{1,0:T(8,128)(2,1)}, bf16[1280,1024]{1,0:T(8,128)(2,1)}) custom-call(bf16[8,160,1024]{2,1,0:T(8,128)(2,1)} %get-tuple-element.55.xs, bf16[8,160,1024]{2,1,0:T(8,128)(2,1)} %get-tuple-element.56.gs, ...), custom_call_target="tpu_custom_call" | custom-call | tf_op jit(solution)/shard_map/pallas_call | solution.py:743
  359.8 19.6 %shard_map.318 = (bf16[2,128,1024]{2,1,0:T(8,128)(2,1)}, bf16[2,128,1024]{2,1,0:T(8,128)(2,1)}, f32[512,1024]{1,0:T(8,128)}, bf16[2,2,4,2,32,1024]{5,4,3,2,1,0:T...) custom-call(s32[2,512]{1,0:T(2,128)} %lpos.3, ...), custom_call_target="tpu_custom_call" | custom-call | tf_op jit(solution)/shard_map/pallas_call | solution.py:349
  379.4 95.0 %shard_map.319 = (f32[2,128,1024]{2,1,0:T(8,128)}, f32[2,128,1024]{2,1,0:T(8,128)}, f32[32,1024]{1,0:T(8,128)}, f32[32,1024]{1,0:T(8,128)}, f32[32,1024]{1,0:T(8...) custom-call(bf16[512,1024]{1,0:T(8,128)(2,1)} %get-tuple-element.67.q, bf16[256,1024]{1,0:T(8,128)(2,1)} %get-tuple-element.68.k, ...), custom_call_target="tpu_custom_call" | custom-call | tf_op jit(solution)/shard_map/pallas_call | solution.py:555
  474.5 0.0 copy-start
  474.5 1.4 dynamic-slice_bitcast_fusion.1
  475.9 1.4 dynamic-slice_bitcast_fusion
  477.3 1.3 dynamic-slice_bitcast_fusion.2
  478.6 0.0 copy-start.4
  478.6 0.0 copy-start.3
  478.6 0.0 copy-start.2
  478.6 0.0 copy-start.1
  478.6 2.4 copy.46
  481.0 0.0 copy-done
  481.0 1.0 copy.47
  481.9 0.0 copy-done.4
  481.9 0.7 copy.48
  482.6 0.0 copy-done.3
  482.6 0.7 copy.49
  483.3 0.0 copy-done.2
  483.3 0.7 copy.50
  483.9 0.0 copy-done.1
  483.9 0.7 copy.51
Async XLA Ops:
  474.5 6.5 %copy-start = (f32[2,128,1024]{2,1,0:T(8,128)S(1)}, f32[2,128,1024]{2,1,0:T(8,128)}, u32[]{:S(2)}) copy-start(f32[2,128,1024]{2,1,0:T(8,128)} %get-tuple-element.115) | copy-start | bytes 3145732
  478.6 3.4 copy-start.4
  478.6 4.0 copy-start.3
  478.6 4.7 copy-start.2
  478.6 5.3 %copy-start.1 = (f32[32,1024]{1,0:T(8,128)S(1)}, f32[32,1024]{1,0:T(8,128)}, u32[]{:S(2)}) copy-start(f32[32,1024]{1,0:T(8,128)} %get-tuple-element.119) | copy-start | bytes 393220

commit v10 on v9

--- a/solution.py
+++ b/solution.py
@@ -56,9 +56,6 @@
 def column_of(row):
     i = lax.broadcasted_iota(jnp.int32, (128, 128), 0)
     return jnp.sum(jnp.where(i == lax.broadcasted_iota(jnp.int32, (128, 128), 1), row, 0), axis=1, keepdims=True)
-def row_of(col):
-    i = lax.broadcasted_iota(jnp.int32, (128, 128), 0)
-    return jnp.sum(jnp.where(i == lax.broadcasted_iota(jnp.int32, (128, 128), 1), col, 0), axis=0, keepdims=True)
 def rows_of(long_ref, short_ref, t):
     ref = long_ref if t == 0 else short_ref
     return ref[...].reshape(ref.shape[0] * ref.shape[1], ref.shape[2])
@@ -215,7 +212,7 @@
         n2[rows, :] = (m * rms_scale(m) * gain).astype(bf)
     logits[...] = dot(n2[...], params[...], 1, 1)
     logit_t = dot(params[...], n2[...], 1, 1)[:experts]
-    routes = [jnp.concatenate([row_of(ref[i, :, j:j + 1]) for ref in (lr, sr) for i in range(ref.shape[0])], axis=1) for j in range(2)]
+    routes = [jnp.concatenate([ref[i, j:j + 1, :] for ref in (lr, sr) for i in range(ref.shape[0])], axis=1) for j in range(2)]
     e_iota = lax.broadcasted_iota(jnp.int32, (experts, tokens), 0)
     member = ((e_iota == routes[0]) | (e_iota == routes[1])).astype(f32)
     e = jnp.exp(logit_t - jnp.max(logit_t, axis=0, keepdims=True))
@@ -247,8 +244,8 @@
     for cp in fetch: cp.start()
     gain = params[experts + 1:experts + 2, :].astype(f32)
     lane = lax.broadcasted_iota(jnp.int32, (tokens, 128), 1)
-    routes = jnp.concatenate([ref[i] for ref in (lr, sr) for i in range(ref.shape[0])], axis=0)
-    member = ((lane == routes[:, 0:1]) | (lane == routes[:, 1:2])).astype(f32)
+    routes = [jnp.concatenate([column_of(ref[i, j:j + 1, :]) for ref in (lr, sr) for i in range(ref.shape[0])], axis=0) for j in range(2)]
+    member = ((lane == routes[0]) | (lane == routes[1])).astype(f32)
     after = (lax.broadcasted_iota(jnp.int32, (tokens, tokens), 1) < lax.broadcasted_iota(jnp.int32, (tokens, tokens), 0)).astype(f32).astype(bf)
     place = jnp.dot(after, member.astype(bf), preferred_element_type=f32)
     kept = (member > 0.5) & (place < cap)
@@ -268,10 +265,10 @@
         s_iota = lax.broadcasted_iota(jnp.int32, (256, experts * cap), 1)
         fin, back, mean, shares = m, 0.0, 0.0, []
         for j in range(2):
-            this = lane[at] == routes[at, j:j + 1]
+            this = lane[at] == routes[j][at]
             place_j = jnp.sum(jnp.where(this, slot[at], 0), axis=1, keepdims=True)
             gate_j = jnp.sum(jnp.where(this, gate[at], 0.0), axis=1, keepdims=True)
-            index = jnp.where(place_j >= 0, routes[at, j:j + 1] * cap + place_j, -1)
+            index = jnp.where(place_j >= 0, routes[j][at] * cap + place_j, -1)
             pick = (s_iota == index).astype(f32).astype(bf)
             pair = jnp.dot(pick, eo[...], preferred_element_type=f32)
             back += jnp.dot(pick, ri[...], preferred_element_type=f32)
@@ -480,8 +477,8 @@
     attend(2)
     kv_core(2); kv_chip(1); kv_end(0); weight_grad(1, dq, 2); stages(0, 1, 1); stages(1, 0, 1); stages(2, 0, 0)
     attend(3)
-    kv_core(3); kv_chip(2); kv_end(1); weight_grad(1, dq, 3); stages(0, 0, 2, 3); stages(0, 2, 1); stages(1, 1, 1); stages(2, 0, 1)
-    kv_chip(3); kv_end(2); stages(0, 1, 2, 3); stages(0, 3, 1); stages(1, 0, 2, 3); stages(1, 2, 1); stages(2, 1, 1); stages(3, 0, 0)
+    kv_core(3); kv_chip(2); kv_end(1); kv_chip(3); weight_grad(1, dq, 3); stages(0, 0, 2, 3); stages(0, 2, 1); stages(1, 1, 1); stages(2, 0, 1)
+    kv_end(2); stages(0, 1, 2, 3); stages(0, 3, 1); stages(1, 0, 2, 3); stages(1, 2, 1); stages(2, 1, 1); stages(3, 0, 0)
     kv_end(3); stages(0, 2, 2, 3); stages(1, 3, 1); stages(1, 1, 2, 3); stages(2, 2, 1); stages(2, 0, 2, 3); stages(3, 0, 1)
     for cp in late: cp.wait()
     gain = params[experts:experts + 1, :].astype(f32)
@@ -796,7 +793,7 @@
     pieces = ((4, 0, small.shape[0], 0),) + tuple(p[:3] + (0,) for p in pieces)
     sizes = (long_items, short_items, seq_size, experts, capacity)
     places = (long_positions, short_positions)
-    routes = (long_routes, short_routes)
+    routes = (long_routes.swapaxes(1, 2), short_routes.swapaxes(1, 2))
     (
         key_all,
         value_all,

time: 489 us -> 491 us (level)
  no operation moved by 1% of the time
where the time goes in v10:
time: 491 us; the launch traced here: 483 us
  Pallas kernels  471 us (96%)
  local copies, waits for them, and re-layouts  10.6 us (2%)
    pallas_call x1, Pallas kernels, expert_all(): pl.pallas_call(functools.partial(expert_kernel, cap, per, order, todo, wc...  240 us
    pallas_call x1, Pallas kernels, front(): pl.pallas_call(functools.partial(front_kernel, dims, nl, ns, experts, cap...  115 us
    pallas_call x1, Pallas kernels, back(): pl.pallas_call(functools.partial(back_kernel, dims, nl, ns, experts, piec...  95.9 us
    pallas_call x1, Pallas kernels, post(): pl.pallas_call(functools.partial(post_kernel, nl, ns, blocks, experts, ca...  19.8 us

profile of v10, /device:TPU:0, one launch (start us, length us, event | category | flops | bytes accessed | tf_op | source)
XLA Modules:
  0.0 483.1 jit_solution(14982633118970237340)
XLA Ops:
  0.6 0.7 fusion.9
  1.4 0.6 pad.14.small_in
  2.0 115.3 %shard_map.316 = (bf16[2,2,4,2,32,1024]{5,4,3,2,1,0:T(8,128)(2,1)}, bf16[2,2,4,2,32,1024]{5,4,3,2,1,0:T(8,128)(2,1)}, bf16[2,2,4,2,32,1024]{5,4,3,2,1,0:T(8,128)...) custom-call(s32[2]{0:T(128)} %ll.1, s32[2]{0:T(128)} %sl.1, ...), custom_call_target="tpu_custom_call" | custom-call | tf_op jit(solution)/shard_map/pallas_call | solution.py:334
  117.3 239.6 %shard_map.317 = (bf16[8,160,1024]{2,1,0:T(8,128)(2,1)}, bf16[8,160,1024]{2,1,0:T(8,128)(2,1)}, f32[3,256,2816]{2,1,0:T(8,128)}, bf16[1280,1024]{1,0:T(8,128)(2,1)}, bf16[1280,1024]{1,0:T(8,128)(2,1)}) custom-call(bf16[8,160,1024]{2,1,0:T(8,128)(2,1)} %get-tuple-element.55.xs, bf16[8,160,1024]{2,1,0:T(8,128)(2,1)} %get-tuple-element.56.gs, ...), custom_call_target="tpu_custom_call" | custom-call | tf_op jit(solution)/shard_map/pallas_call | solution.py:740
  356.9 19.8 %shard_map.318 = (bf16[2,128,1024]{2,1,0:T(8,128)(2,1)}, bf16[2,128,1024]{2,1,0:T(8,128)(2,1)}, f32[512,1024]{1,0:T(8,128)}, bf16[2,2,4,2,32,1024]{5,4,3,2,1,0:T...) custom-call(s32[2,512]{1,0:T(2,128)} %lpos.3, ...), custom_call_target="tpu_custom_call" | custom-call | tf_op jit(solution)/shard_map/pallas_call | solution.py:346
  376.7 95.9 %shard_map.319 = (f32[2,128,1024]{2,1,0:T(8,128)}, f32[2,128,1024]{2,1,0:T(8,128)}, f32[32,1024]{1,0:T(8,128)}, f32[32,1024]{1,0:T(8,128)}, f32[32,1024]{1,0:T(8...) custom-call(bf16[512,1024]{1,0:T(8,128)(2,1)} %get-tuple-element.67.q, bf16[256,1024]{1,0:T(8,128)(2,1)} %get-tuple-element.68.k, ...), custom_call_target="tpu_custom_call" | custom-call | tf_op jit(solution)/shard_map/pallas_call | solution.py:552
  472.6 0.0 copy-start
  472.6 1.4 dynamic-slice_bitcast_fusion.1
  474.0 1.4 dynamic-slice_bitcast_fusion
  475.4 1.3 dynamic-slice_bitcast_fusion.2
  476.7 0.0 copy-start.4
  476.7 0.0 copy-start.3
  476.7 0.0 copy-start.2
  476.7 0.0 copy-start.1
  476.7 2.4 copy.42
  479.1 0.0 copy-done
  479.1 1.0 copy.43
  480.1 0.0 copy-done.4
  480.1 0.7 copy.44
  480.7 0.0 copy-done.3
  480.7 0.7 copy.45
  481.4 0.0 copy-done.2
  481.4 0.7 copy.46
  482.0 0.0 copy-done.1
  482.0 0.7 copy.47
Async XLA Ops:
  472.6 6.5 %copy-start = (f32[2,128,1024]{2,1,0:T(8,128)S(1)}, f32[2,128,1024]{2,1,0:T(8,128)}, u32[]{:S(2)}) copy-start(f32[2,128,1024]{2,1,0:T(8,128)} %get-tuple-element.115) | copy-start | bytes 3145732
  476.7 3.4 copy-start.4
  476.7 4.0 copy-start.3
  476.7 4.7 copy-start.2
  476.7 5.3 %copy-start.1 = (f32[32,1024]{1,0:T(8,128)S(1)}, f32[32,1024]{1,0:T(8,128)}, u32[]{:S(2)}) copy-start(f32[32,1024]{1,0:T(8,128)} %get-tuple-element.119) | copy-start | bytes 393220

commit v11 on v10

--- a/solution.py
+++ b/solution.py
@@ -479,21 +479,22 @@
     attend(3)
     kv_core(3); kv_chip(2); kv_end(1); kv_chip(3); weight_grad(1, dq, 3); stages(0, 0, 2, 3); stages(0, 2, 1); stages(1, 1, 1); stages(2, 0, 1)
     kv_end(2); stages(0, 1, 2, 3); stages(0, 3, 1); stages(1, 0, 2, 3); stages(1, 2, 1); stages(2, 1, 1); stages(3, 0, 0)
-    kv_end(3); stages(0, 2, 2, 3); stages(1, 3, 1); stages(1, 1, 2, 3); stages(2, 2, 1); stages(2, 0, 2, 3); stages(3, 0, 1)
     for cp in late: cp.wait()
     gain = params[experts:experts + 1, :].astype(f32)
-    ag = jnp.zeros((1, q.shape[1]), f32)
-    for t in range(2):
+    def input_grad(t):
         rows = pl.ds(t * half, half)
         ng = dot(dq[rows, :], wq[...], 1, 1) + dot(ka[rows, :], wk[...], 1, 1) + dot(va[rows, :], wv[...], 1, 1)
         m = rows_of(lx, sx, t).astype(f32)
         r1 = rms_scale(m)
         u = m * r1
-        ag += jnp.sum(ng * u, axis=0, keepdims=True)
         w = ng * gain
         (lgrad, sgrad)[t][...] = (midg[rows, :] + r1 * (w - u * jnp.mean(w * u, axis=-1, keepdims=True))).reshape(lgrad.shape)
-        if t == 0:
-            stages(0, 3, 2, 3); stages(1, 2, 2, 3); stages(2, 3, 1); stages(2, 1, 2, 3); stages(3, 1, 1)
+        return jnp.sum(ng * u, axis=0, keepdims=True)
+    ag = input_grad(1)
+    kv_end(3); stages(0, 2, 2, 3); stages(1, 3, 1); stages(1, 1, 2, 3); stages(2, 2, 1); stages(2, 0, 2, 3); stages(3, 0, 1)
+    stages(0, 3, 2, 3)
+    ag += input_grad(0)
+    stages(1, 2, 2, 3); stages(2, 3, 1); stages(2, 1, 2, 3); stages(3, 1, 1)
     sacc[0] = small_in[...]
     sacc[0, 0:1, :] = ag
     heads = seg.shape[0]

time: 491 us -> 491 us (level)
  no operation moved by 1% of the time
where the time goes in v11:
time: 491 us; the launch traced here: 482 us
  Pallas kernels  470 us (96%)
  local copies, waits for them, and re-layouts  10.6 us (2%)
    pallas_call x1, Pallas kernels, expert_all(): pl.pallas_call(functools.partial(expert_kernel, cap, per, order, todo, wc...  240 us
    pallas_call x1, Pallas kernels, front(): pl.pallas_call(functools.partial(front_kernel, dims, nl, ns, experts, cap...  115 us
    pallas_call x1, Pallas kernels, back(): pl.pallas_call(functools.partial(back_kernel, dims, nl, ns, experts, piec...  95.1 us
    pallas_call x1, Pallas kernels, post(): pl.pallas_call(functools.partial(post_kernel, nl, ns, blocks, experts, ca...  19.8 us

profile of v11, /device:TPU:0, one launch (start us, length us, event | category | flops | bytes accessed | tf_op | source)
XLA Modules:
  0.0 482.4 jit_solution(11128325876816282983)
XLA Ops:
  0.6 0.7 fusion.9
  1.4 0.6 pad.14.small_in
  2.0 115.3 %shard_map.316 = (bf16[2,2,4,2,32,1024]{5,4,3,2,1,0:T(8,128)(2,1)}, bf16[2,2,4,2,32,1024]{5,4,3,2,1,0:T(8,128)(2,1)}, bf16[2,2,4,2,32,1024]{5,4,3,2,1,0:T(8,128)...) custom-call(s32[2]{0:T(128)} %ll.1, s32[2]{0:T(128)} %sl.1, ...), custom_call_target="tpu_custom_call" | custom-call | tf_op jit(solution)/shard_map/pallas_call | solution.py:334
  117.3 239.6 %shard_map.317 = (bf16[8,160,1024]{2,1,0:T(8,128)(2,1)}, bf16[8,160,1024]{2,1,0:T(8,128)(2,1)}, f32[3,256,2816]{2,1,0:T(8,128)}, bf16[1280,1024]{1,0:T(8,128)(2,1)}, bf16[1280,1024]{1,0:T(8,128)(2,1)}) custom-call(bf16[8,160,1024]{2,1,0:T(8,128)(2,1)} %get-tuple-element.55.xs, bf16[8,160,1024]{2,1,0:T(8,128)(2,1)} %get-tuple-element.56.gs, ...), custom_call_target="tpu_custom_call" | custom-call | tf_op jit(solution)/shard_map/pallas_call | solution.py:741
  356.9 19.8 %shard_map.318 = (bf16[2,128,1024]{2,1,0:T(8,128)(2,1)}, bf16[2,128,1024]{2,1,0:T(8,128)(2,1)}, f32[512,1024]{1,0:T(8,128)}, bf16[2,2,4,2,32,1024]{5,4,3,2,1,0:T...) custom-call(s32[2,512]{1,0:T(2,128)} %lpos.3, ...), custom_call_target="tpu_custom_call" | custom-call | tf_op jit(solution)/shard_map/pallas_call | solution.py:346
  376.7 95.1 %shard_map.319 = (f32[2,128,1024]{2,1,0:T(8,128)}, f32[2,128,1024]{2,1,0:T(8,128)}, f32[32,1024]{1,0:T(8,128)}, f32[32,1024]{1,0:T(8,128)}, f32[32,1024]{1,0:T(8...) custom-call(bf16[512,1024]{1,0:T(8,128)(2,1)} %get-tuple-element.67.q, bf16[256,1024]{1,0:T(8,128)(2,1)} %get-tuple-element.68.k, ...), custom_call_target="tpu_custom_call" | custom-call | tf_op jit(solution)/shard_map/pallas_call | solution.py:553
  471.8 0.0 copy-start
  471.9 1.4 dynamic-slice_bitcast_fusion.1
  473.2 1.4 dynamic-slice_bitcast_fusion
  474.6 1.3 dynamic-slice_bitcast_fusion.2
  475.9 0.0 copy-start.4
  475.9 0.0 copy-start.3
  475.9 0.0 copy-start.2
  475.9 0.0 copy-start.1
  476.0 2.4 copy.42
  478.3 0.0 copy-done
  478.3 1.0 copy.43
  479.3 0.0 copy-done.4
  479.3 0.7 copy.44
  479.9 0.0 copy-done.3
  480.0 0.7 copy.45
  480.6 0.0 copy-done.2
  480.6 0.7 copy.46
  481.3 0.0 copy-done.1
  481.3 0.7 copy.47
Async XLA Ops:
  471.8 6.5 %copy-start = (f32[2,128,1024]{2,1,0:T(8,128)S(1)}, f32[2,128,1024]{2,1,0:T(8,128)}, u32[]{:S(2)}) copy-start(f32[2,128,1024]{2,1,0:T(8,128)} %get-tuple-element.115) | copy-start | bytes 3145732
  475.9 3.4 copy-start.4
  475.9 4.0 copy-start.3
  475.9 4.7 copy-start.2
  475.9 5.3 %copy-start.1 = (f32[32,1024]{1,0:T(8,128)S(1)}, f32[32,1024]{1,0:T(8,128)}, u32[]{:S(2)}) copy-start(f32[32,1024]{1,0:T(8,128)} %get-tuple-element.119) | copy-start | bytes 393220
